TPU v7x, 256 devices: a whole 4x4x8 slice. The times are simulated.
256 devices in a mesh: seq: 64 (over z, x, core), tp: 4 (over y).
Axes of the slice: x: 4, y: 4, z: 8, core: 2. Of those that a mesh axis runs over, the one named last changes fastest.
Arguments:
- prefix: bfloat16 [16384, 2048], P('seq', 'tp'), may hold values from -48 to 48
- latent_in: bfloat16 [1024, 2048], P('seq', 'tp'), may hold values from -48 to 48
- latent_pos: int32 [1024], replicated, may hold values from 4096 to 16383, as said below
- w_query: bfloat16 [2048, 2048], P(None, 'tp'), may hold values from -0.375 to 0.375
- w_keyval: bfloat16 [2, 2048, 2048], P(None, None, 'tp'), may hold values from -0.125 to 0.125
- w_cross_out: bfloat16 [2048, 2048], P('tp'), may hold values from -0.125 to 0.125
- attn_gain: float32 [2048], replicated, may hold values from 0.1 to 1.9
- w_self_qkv: bfloat16 [3, 2048, 2048], P(None, 'seq', 'tp'), may hold values from -0.91855865 to 0.91855865
- w_self_out: bfloat16 [2048, 2048], P('tp', 'seq'), may hold values from -0.125 to 0.125
- mlp_gain: float32 [2048], replicated, may hold values from 0.1 to 1.9
- w_gate_up: bfloat16 [2, 2048, 4096], P(None, 'seq', 'tp'), may hold values from -0.125 to 0.125
- w_down: bfloat16 [4096, 2048], P('tp', 'seq'), may hold values from -0.09375 to 0.09375
Outputs:
- latent_out: bfloat16 [1024, 2048], P('seq', 'tp')
Inputs may be any that keep to these rules, and one draw needn't show every extreme that they name: `latent_pos`: strictly increasing; the first is 4096 and the last is 16383.
All inputs are finite; a program needn't handle non-finite values.
Results may differ from a plain program's by a relative error of at most 0.02895.
The roundings to bfloat16 on the way count: a program that leaves them out, or rounds other values in their place, can miss the bound.
Values may be sent and summed in bfloat16 or wider, within the bound.
No kernel may reach another device: no remote copies, remote signals or barrier semaphores. Data moves between devices by JAX's collectives and lax.ppermute only.
A program may use at most 64 MiB of HBM per device.

v0:
```python
import jax
import jax.numpy as jnp
from jax import lax
from jax.sharding import PartitionSpec as P

HD = 128


NEG = -1e30


def normalize(x, gain):
    x = x.astype(jnp.float32)
    scale = lax.rsqrt(jnp.mean(x * x, axis=-1, keepdims=True) + 1e-05)
    return (x * scale * gain).astype(jnp.bfloat16)


def split_weights(weights):
    high = lax.optimization_barrier(weights.astype(jnp.bfloat16))
    low = (weights - high.astype(jnp.float32)).astype(jnp.bfloat16)
    return (high, low)


def local(
    prefix,
    latent_in,
    latent_pos,
    w_query,
    w_keyval,
    w_cross_out,
    attn_gain,
    w_self_qkv,
    w_self_out,
    mlp_gain,
    w_gate_up,
    w_down,
):
    seq_count = lax.axis_size("seq")
    seq_index = lax.axis_index("seq")
    local_rows = latent_in.shape[0]
    latents = local_rows * seq_count
    width = w_query.shape[1]
    head_local = width // HD
    pref_rows = prefix.shape[0]
    scale = HD ** (-0.5)
    weight_rows = w_keyval
    keyval = jnp.einsum(
        "pd,cde->cpe",
        lax.all_gather(prefix, "tp", axis=1, tiled=True),
        weight_rows,
        preferred_element_type=jnp.float32,
    ).astype(jnp.bfloat16)
    weight_rows = w_query
    queries = jnp.dot(
        lax.all_gather(latent_in, "tp", axis=1, tiled=True),
        weight_rows,
        preferred_element_type=jnp.float32,
    ).astype(jnp.bfloat16)
    all_queries = lax.all_gather(queries, "seq", axis=0, tiled=True)
    block = min(512, latents)
    key_heads = keyval[0].reshape(pref_rows, head_local, HD)
    value_heads = keyval[1].reshape(pref_rows, head_local, HD)

    def block_scores(query_block):
        return (
            jnp.einsum("bhe,phe->bhp", query_block, key_heads, preferred_element_type=jnp.float32)
            * scale
        )

    scores = lax.map(block_scores, all_queries.reshape(latents // block, block, head_local, HD))
    scores = scores.reshape(latents, head_local, pref_rows)
    key_pos = seq_index * pref_rows + jnp.arange(pref_rows, dtype=jnp.int32)
    visible = (key_pos[None, :] <= latent_pos[:, None])[:, None, :]
    peak_local = jnp.max(jnp.where(visible, scores, NEG), axis=2)
    peak = lax.pmax(peak_local, "seq")
    weights = jnp.where(visible, jnp.exp(scores - peak[:, :, None]), 0.0)
    totals = jnp.sum(weights, axis=2)
    high, low = split_weights(weights)
    summed = jnp.einsum("lhp,phe->lhe", high, value_heads, preferred_element_type=jnp.float32)
    summed = summed + jnp.einsum(
        "lhp,phe->lhe", low, value_heads, preferred_element_type=jnp.float32
    )
    summed, totals = (summed, totals)
    summed, totals = (
        lax.psum_scatter(summed, "seq", scatter_dimension=0, tiled=True),
        lax.psum_scatter(totals, "seq", scatter_dimension=0, tiled=True),
    )
    cross_context = (summed / totals[:, :, None]).reshape(local_rows, width).astype(jnp.bfloat16)
    cross_terms = jnp.dot(cross_context, w_cross_out, preferred_element_type=jnp.float32)
    first = (
        latent_in.astype(jnp.float32)
        + lax.psum_scatter(
            cross_terms.astype(jnp.bfloat16), "tp", scatter_dimension=1, tiled=True
        ).astype(jnp.float32)
    ).astype(jnp.bfloat16)
    normed = normalize(lax.all_gather(first, "tp", axis=1, tiled=True), attn_gain)
    columns = normed
    qkv = jnp.einsum(
        "rd,cde->cre",
        columns,
        lax.all_gather(w_self_qkv, "seq", axis=1, tiled=True),
        preferred_element_type=jnp.float32,
    ).astype(jnp.bfloat16)
    self_q = qkv[0].reshape(local_rows, head_local, HD)
    query_index = seq_index * local_rows + jnp.arange(local_rows, dtype=jnp.int32)
    peak = jnp.full((local_rows, head_local), NEG, jnp.float32)
    key_piece = lax.all_gather(qkv[1], "seq", axis=0, tiled=True)
    value_piece = lax.all_gather(qkv[2], "seq", axis=0, tiled=True)
    count = key_piece.shape[0]
    found = (
        jnp.einsum(
            "rhe,khe->rhk",
            self_q,
            key_piece.reshape(count, head_local, HD),
            preferred_element_type=jnp.float32,
        )
        * scale
    )
    key_index = jnp.arange(count, dtype=jnp.int32)
    allowed = (key_index[None, :] <= query_index[:, None])[:, None, :]
    found = jnp.where(allowed, found, NEG)
    new_peak = jnp.maximum(peak, jnp.max(found, axis=2))
    weights = jnp.where(allowed, jnp.exp(found - new_peak[:, :, None]), 0.0)
    totals = jnp.sum(weights, axis=2)
    value_local = value_piece.reshape(count, head_local, HD)
    high, low = split_weights(weights)
    added = jnp.einsum("rhk,khe->rhe", high, value_local, preferred_element_type=jnp.float32)
    added = added + jnp.einsum("rhk,khe->rhe", low, value_local, preferred_element_type=jnp.float32)
    summed = added
    self_context = (summed / totals[:, :, None]).reshape(local_rows, width).astype(jnp.bfloat16)
    out_terms = jnp.dot(
        self_context,
        lax.all_gather(w_self_out, "seq", axis=1, tiled=True),
        preferred_element_type=jnp.float32,
    )
    second = (
        first.astype(jnp.float32)
        + lax.psum_scatter(
            out_terms.astype(jnp.bfloat16), "tp", scatter_dimension=1, tiled=True
        ).astype(jnp.float32)
    ).astype(jnp.bfloat16)
    normed_mlp = normalize(lax.all_gather(second, "tp", axis=1, tiled=True), mlp_gain)
    columns = normed_mlp
    gate_up = jnp.einsum(
        "rd,cdf->crf",
        columns,
        lax.all_gather(w_gate_up, "seq", axis=1, tiled=True),
        preferred_element_type=jnp.float32,
    )
    hidden = (jax.nn.silu(gate_up[0]) * gate_up[1]).astype(jnp.bfloat16)
    down_terms = jnp.dot(
        hidden,
        lax.all_gather(w_down, "seq", axis=1, tiled=True),
        preferred_element_type=jnp.float32,
    )
    latent_out = (
        second.astype(jnp.float32)
        + lax.psum_scatter(
            down_terms.astype(jnp.bfloat16), "tp", scatter_dimension=1, tiled=True
        ).astype(jnp.float32)
    ).astype(jnp.bfloat16)
    return latent_out


def solution(mesh):
    return jax.shard_map(
        local,
        mesh=mesh,
        in_specs=(
            P("seq", "tp"),
            P("seq", "tp"),
            P(),
            P(None, "tp"),
            P(None, None, "tp"),
            P("tp", None),
            P(),
            P(None, "seq", "tp"),
            P("tp", "seq"),
            P(),
            P(None, "seq", "tp"),
            P("tp", "seq"),
        ),
        out_specs=P("seq", "tp"),
        check_vma=False,
    )
```

profile of v0, /device:TPU:8, one launch (start us, length us, event | category | flops | bytes accessed | tf_op | source)
XLA Modules:
  0.0 1197.1 jit_solution(6615782811588868234)
XLA Ops:
  7.3 12.3 %all_gather.34 = bf16[16,2048]{1,0:T(8,128)(2,1)S(1)} all-gather(bf16[16,512]{1,0:T(8,128)(2,1)} %param.15), channel_id=1, replica_groups=mesh['seq'=64,'tp'=4] {'tp'}, dimensions={1}, use_global_device_ids=true | all-gather | bytes 81920 | tf_op jit(solution)/shard_map/all_gather | solution.py:55
  19.6 2.6 convolution_convert_fusion.5
  23.0 1.6 broadcast_compare_fusion.1
  25.5 12.2 %all-gather.11.cloned.1.call-done = bf16[256,2048]{1,0:T(8,128)(2,1)} async-done(((bf16[256,512]{1,0:T(8,128)(2,1)}), bf16[256,2048]{1,0:T(8,128)(2,1)}) %all-gather.11.cloned.1.call-update) | async-done | bytes 1048592 | tf_op jit(solution)/shard_map/all_gather | solution.py:49
  37.7 3.8 fusion.3
  42.4 75.6 %all-gather.13.cloned.1.call-done = bf16[1024,512]{1,0:T(8,128)(2,1)} async-done(((bf16[16,512]{1,0:T(8,128)(2,1)}), bf16[1024,512]{1,0:T(8,128)(2,1)}) %all-gather.13.cloned.1.call-update) | async-done | bytes 1048592 | tf_op jit(solution)/shard_map/all_gather | solution.py:59
  119.4 3.9 while.11
  119.6 1.8 bitcast_dynamic-update-slice_fusion.3
  121.6 1.8 bitcast_dynamic-update-slice_fusion.3
  123.4 4.6 copy.33
  128.7 248.6 %pmax.7 = f32[1024,4]{0,1:T(4,128)S(1)} all-reduce(f32[1024,4]{0,1:T(4,128)S(1)} %bitcast.104), channel_id=1, replica_groups=mesh['seq'=64,'tp'=4] {'seq'}, use_global_device_ids=true, to_apply=%region_3.4 | all-reduce | flops 4096 | bytes 32768 | tf_op jit(solution)/shard_map/pmax | solution.py:75
  377.3 2.8 fusion.2
  383.1 2.2 add_bitcast_fusion
  385.2 2.9 copy.34
  389.5 3.1 select_reduce_fusion
  392.6 246.3 %all-reduce.1 = f32[1024,4]{0,1:T(4,128)S(1)} all-reduce(f32[1024,4]{0,1:T(4,128)S(1)} %bitcast.103), channel_id=5, replica_groups=mesh['seq'=64,'tp'=4] {'seq'}, use_global_device_ids=true, to_apply=%region_6.7.clone | all-reduce | flops 4096 | bytes 32768
  641.6 18.2 %reduce-scatter.5.cloned.1.call-done = bf16[16,512]{1,0:T(8,128)(2,1)} async-done(((bf16[16,2048]{1,0:T(8,128)(2,1)}), bf16[16,512]{1,0:T(8,128)(2,1)}) %reduce-scatter.5.cloned.1.call-update) | async-done | bytes 16400 | tf_op jit(solution)/shard_map/reduce_scatter | solution.py:92
  660.5 11.9 all_gather.36
  672.5 73.0 %all-gather.15.cloned.1.call-done = bf16[3,2048,512]{2,1,0:T(8,128)(2,1)} async-done(((bf16[3,32,512]{2,1,0:T(8,128)(2,1)}), bf16[3,2048,512]{2,1,0:T(8,128)(2,1)}) %all-gather.15.cloned.1.call-update) | async-done | bytes 6291472 | tf_op jit(solution)/shard_map/all_gather | solution.py:101
  745.6 3.7 fusion.6
  751.6 71.4 %all-gather.25.cloned.1.call-done = bf16[1,1024,512]{2,1,0:T(8,128)(2,1)} async-done(((bf16[1,16,512]{2,1,0:T(8,128)(2,1)}), bf16[1,1024,512]{2,1,0:T(8,128)(2,1)}) %all-gather.25.cloned.1.call-update) | async-done | bytes 1048592 | tf_op jit(solution)/shard_map/all_gather | solution.py:107
  827.0 73.3 %all-gather.23.cloned.1.call-done = bf16[1,1024,512]{2,1,0:T(8,128)(2,1)} async-done(((bf16[1,16,512]{2,1,0:T(8,128)(2,1)}), bf16[1,1024,512]{2,1,0:T(8,128)(2,1)}) %all-gather.23.cloned.1.call-update) | async-done | bytes 1048592 | tf_op jit(solution)/shard_map/all_gather | solution.py:108
  901.9 1.7 fusion.10
  903.5 74.8 %all-gather.17.cloned.1.call-done = bf16[512,2048]{0,1:T(8,128)(2,1)} async-done(((bf16[512,32]{0,1:T(8,128)(2,1)}), bf16[512,2048]{0,1:T(8,128)(2,1)}) %all-gather.17.cloned.1.call-update) | async-done | bytes 2097168 | tf_op jit(solution)/shard_map/all_gather | solution.py:133
  978.4 2.9 convolution_convert_fusion.1
  982.6 17.5 %reduce-scatter.7.cloned.1.call-done = bf16[16,512]{1,0:T(8,128)(2,1)} async-done(((bf16[16,2048]{1,0:T(8,128)(2,1)}), bf16[16,512]{1,0:T(8,128)(2,1)}) %reduce-scatter.7.cloned.1.call-update) | async-done | bytes 16400 | tf_op jit(solution)/shard_map/reduce_scatter | solution.py:138
  1000.9 12.0 %all_gather.41 = bf16[16,2048]{1,0:T(8,128)(2,1)S(1)} all-gather(bf16[16,512]{1,0:T(8,128)(2,1)S(1)} %add_convert_fusion.1), channel_id=1, replica_groups=mesh['seq'=64,'tp'=4] {'tp'}, dimensions={1}, use_global_device_ids=true | all-gather | bytes 81920 | tf_op jit(solution)/shard_map/all_gather | solution.py:142
  1013.1 74.4 %all-gather.19.cloned.1.call-done = bf16[2,2048,1024]{2,1,0:T(8,128)(2,1)} async-done(((bf16[2,32,1024]{2,1,0:T(8,128)(2,1)}), bf16[2,2048,1024]{2,1,0:T(8,128)(2,1)}) %all-gather.19.cloned.1.call-update) | async-done | bytes 8388624 | tf_op jit(solution)/shard_map/all_gather | solution.py:147
  1087.5 4.6 convolution_bitcast_fusion
  1092.1 74.4 %all-gather.21.cloned.1.call-done = bf16[1024,2048]{0,1:T(8,128)(2,1)} async-done(((bf16[1024,32]{0,1:T(8,128)(2,1)}), bf16[1024,2048]{0,1:T(8,128)(2,1)}) %all-gather.21.cloned.1.call-update) | async-done | bytes 4194320 | tf_op jit(solution)/shard_map/all_gather | solution.py:153
  1166.5 4.0 convolution_convert_fusion
  1170.5 18.4 %reduce-scatter.9.cloned.1.call-done = bf16[16,512]{1,0:T(8,128)(2,1)} async-done(((bf16[16,2048]{1,0:T(8,128)(2,1)}), bf16[16,512]{1,0:T(8,128)(2,1)}) %reduce-scatter.9.cloned.1.call-update) | async-done | bytes 16400 | tf_op jit(solution)/shard_map/reduce_scatter | solution.py:158
  (81 shorter events, 24.2 us)
Async XLA Ops:
  6.5 633.4 %copy-start = (bf16[512,2048]{1,0:T(8,128)(2,1)S(1)}, bf16[512,2048]{1,0:T(8,128)(2,1)}, u32[]{:S(2)}) copy-start(bf16[512,2048]{1,0:T(8,128)(2,1)} %param.19) | copy-start | bytes 6291460
  6.5 31.2 %all-gather.11.cloned.1.call-start = ((), (), s32[]{:S(2)}) async-start(), calls=%async_computation.3 | async-start | bytes 1310720 | tf_op jit(solution)/shard_map/all_gather | solution.py:49
  7.3 110.8 %all-gather.13.cloned.1.call-start = ((), (), s32[]{:S(2)}) async-start(), calls=%async_computation.4 | async-start | bytes 1064960 | tf_op jit(solution)/shard_map/all_gather | solution.py:59
  22.2 616.9 %all-reduce.4.cloned.1.call-start = ((), (), s32[]{:S(2)}) async-start(), calls=%async_computation.14 | async-start | bytes 4194304
  123.4 4.6 copy-start.1
  123.4 4.6 copy-start.3
  128.0 249.3 %copy-start.4 = (pred[1024,256]{1,0:T(8,128)(4,1)S(1)}, pred[1024,256]{1,0:T(8,128)(4,1)}, u32[]{:S(2)}) copy-start(pred[1024,256]{1,0:T(8,128)(4,1)} %broadcast_compare_fusion.1) | copy-start | bytes 786436
  377.3 3.5 copy-start.2
  380.8 1.5 copy-start.5
  385.2 3.0 copy-start.10
  388.2 271.6 %copy-start.6 = (bf16[16,512]{1,0:T(8,128)(2,1)S(1)}, bf16[16,512]{1,0:T(8,128)(2,1)}, u32[]{:S(2)}) copy-start(bf16[16,512]{1,0:T(8,128)(2,1)} %param.15) | copy-start | bytes 49156
  388.2 357.4 %copy-start.8 = (f32[2048]{0:T(1024)S(1)}, f32[2048]{0:T(1024)}, u32[]{:S(2)}) copy-start(f32[2048]{0:T(1024)} %param.20) | copy-start | bytes 24580
  388.2 271.6 %reduce-scatter.5.cloned.1.call-start = ((), (), s32[]{:S(2)}) async-start(), calls=%async_computation.5 | async-start | bytes 81920 | tf_op jit(solution)/shard_map/reduce_scatter | solution.py:92
  641.0 104.6 %all-gather.15.cloned.1.call-start = ((), (), s32[]{:S(2)}) async-start(), calls=%async_computation.6 | async-start | bytes 6389760 | tf_op jit(solution)/shard_map/all_gather | solution.py:101
  641.6 181.4 %all-gather.25.cloned.1.call-start = ((), (), s32[]{:S(2)}) async-start(), calls=%async_computation.13 | async-start | bytes 1064960 | tf_op jit(solution)/shard_map/all_gather | solution.py:107
  750.0 150.3 %all-gather.23.cloned.1.call-start = ((), (), s32[]{:S(2)}) async-start(), calls=%async_computation.12 | async-start | bytes 1064960 | tf_op jit(solution)/shard_map/all_gather | solution.py:108
  750.7 227.6 %all-gather.17.cloned.1.call-start = ((), (), s32[]{:S(2)}) async-start(), calls=%async_computation.7 | async-start | bytes 2129920 | tf_op jit(solution)/shard_map/all_gather | solution.py:133
  751.5 248.7 %reduce-scatter.7.cloned.1.call-start = ((), (), s32[]{:S(2)}) async-start(), calls=%async_computation.8 | async-start | bytes 81920 | tf_op jit(solution)/shard_map/reduce_scatter | solution.py:138
  751.6 73.2 %copy-start.7 = (pred[16,1024]{1,0:T(8,128)(4,1)}, pred[16,1024]{1,0:T(8,128)(4,1)S(1)}, u32[]{:S(2)}) copy-start(pred[16,1024]{1,0:T(8,128)(4,1)S(1)} %iota_compare_fusion) | copy-start | bytes 49156
  824.8 0.6 copy-start.9
  981.3 106.2 %all-gather.19.cloned.1.call-start = ((), (), s32[]{:S(2)}) async-start(), calls=%async_computation.9 | async-start | bytes 8519680 | tf_op jit(solution)/shard_map/all_gather | solution.py:147
  981.9 184.6 %all-gather.21.cloned.1.call-start = ((), (), s32[]{:S(2)}) async-start(), calls=%async_computation.10 | async-start | bytes 4259840 | tf_op jit(solution)/shard_map/all_gather | solution.py:153
  982.6 206.4 %reduce-scatter.9.cloned.1.call-start = ((), (), s32[]{:S(2)}) async-start(), calls=%async_computation.11 | async-start | bytes 81920 | tf_op jit(solution)/shard_map/reduce_scatter | solution.py:158
Sparse Core Ops, SparseCore 0:
  9.2 28.4 all-gather.10
  40.5 77.5 all-gather.12
  388.3 187.1 all-reduce.3
  641.1 18.6 reduce-scatter.4
  662.8 82.6 all-gather.14
  750.1 72.8 all-gather.24
  826.2 74.0 all-gather.22
  903.4 74.9 all-gather.16
  981.4 18.7 reduce-scatter.6
  1002.8 84.6 all-gather.18
  1090.3 76.1 all-gather.20
  1170.6 18.2 reduce-scatter.8
where the time goes:
time: 1200 us
  waiting for transfers between devices  587 us (49%)
  blocking collectives  531 us (44%)
  matrix products  31.6 us (3%)
  local copies, waits for them, and re-layouts  16.2 us (1%)
  other arithmetic  16.1 us (1%)
  between operations  14.4 us (1%)
    pmax x1, blocking collectives, local(): peak = lax.pmax(peak_local, 'seq')  249 us
    unnamed x1, blocking collectives  246 us
    all_gather x1, waiting for transfers between devices, local(): all_queries = lax.all_gather(queries, 'seq', axis=0, tiled=True)  75.6 us
    all_gather x1, waiting for transfers between devices, local(): lax.all_gather(w_self_out, 'seq', axis=1, tiled=True)  74.8 us
    all_gather x1, waiting for transfers between devices, local(): lax.all_gather(w_gate_up, 'seq', axis=1, tiled=True)  74.4 us
    all_gather x1, waiting for transfers between devices, local(): lax.all_gather(w_down, 'seq', axis=1, tiled=True)  74.4 us
    all_gather x1, waiting for transfers between devices, local(): value_piece = lax.all_gather(qkv[2], 'seq', axis=0, tiled=True)  73.3 us
    all_gather x1, waiting for transfers between devices, local(): lax.all_gather(w_self_qkv, 'seq', axis=1, tiled=True)  73 us
  transfers between devices with their start and end apart: 12, of which 11 were waited for; matrix products, arithmetic and copies ran while one was open for 2% of the time, Pallas kernels for 0%

commit v1 on v0

v1 whole, which is shorter than its diff:
```python
import jax
import jax.numpy as jnp
from jax import lax
from jax.experimental import pallas as pl
from jax.experimental.pallas import tpu as pltpu
from jax.sharding import Mesh
from jax.sharding import PartitionSpec as P

HD = 128
NEG = -1e30
EPS = 1e-05
SCALE = HD ** (-0.5)
TP = 4
CORES = 2
LANES = 128
ZX = ("z", "x")
SEQ = ("z", "x", "core")
BF16 = jnp.bfloat16
F32 = jnp.float32
NT = (((1,), (1,)), ((), ()))
TN = (((0,), (0,)), ((), ()))


def shifted(x, axis, shift, count):
    return lax.ppermute(x, axis, [(i, (i + shift) % count) for i in range(count)])


def everyone(x):
    return [x] + [shifted(x, "tp", k, TP) for k in range(1, TP)]


def split(weights):
    high = weights.astype(BF16)
    low = (weights - high.astype(F32)).astype(BF16)
    return high, low


def three_terms(x):
    one = x.astype(BF16).astype(F32)
    two = (x - one).astype(BF16).astype(F32)
    three = (x - one - two).astype(BF16).astype(F32)
    return one, two, three


def params(mib=48):
    return pltpu.CompilerParams(vmem_limit_bytes=mib * 1024 * 1024)


def cost(flops, size):
    return pl.CostEstimate(flops=flops, bytes_accessed=size, transcendentals=0)


def gathered_matmul(index, pieces, weight, keep):
    rows, width = pieces[0].shape
    groups, _, cols = weight.shape

    def body(index_ref, *refs):
        piece_refs, weight_ref = refs[:TP], refs[TP]
        out_ref, acc_ref = refs[TP + 1], refs[-1]
        step = pl.program_id(0)
        for k, piece_ref in enumerate(piece_refs):

            @pl.when(step == k)
            def _():
                piece = piece_ref[...]
                for g in range(groups):
                    term = jnp.dot(piece, weight_ref[g], preferred_element_type=F32)
                    acc_ref[g] = term if k == 0 else acc_ref[g] + term
                if keep:
                    refs[TP + 2][...] = piece

        @pl.when(step == TP - 1)
        def _():
            out_ref[...] = acc_ref[...].astype(BF16)

    out_shape = [jax.ShapeDtypeStruct((groups, rows, cols), BF16)]
    out_specs = [pl.BlockSpec((groups, rows, cols), lambda k, i: (0, 0, 0))]
    if keep:
        out_shape.append(jax.ShapeDtypeStruct((rows, TP * width), BF16))
        out_specs.append(pl.BlockSpec((rows, width), lambda k, i: (0, i[k])))
    return pl.pallas_call(
        body,
        grid_spec=pltpu.PrefetchScalarGridSpec(
            num_scalar_prefetch=1,
            grid=(TP,),
            in_specs=[pl.BlockSpec((rows, width), lambda k, i: (0, 0))] * TP
            + [pl.BlockSpec((groups, width, cols), lambda k, i: (0, i[k], 0))],
            out_specs=out_specs,
            scratch_shapes=[pltpu.VMEM((groups, rows, cols), F32)],
        ),
        out_shape=out_shape,
        compiler_params=params(),
        cost_estimate=cost(2 * rows * weight.size, 2 * weight.size),
    )(index, *pieces, weight)


def cross_partial(bases, pos, queries, mine, other):
    count, width = queries.shape
    heads = width // HD
    rows = 128

    def body(base_ref, pos_ref, q_ref, mine_ref, other_ref, out_ref, stat_ref):
        pos = pos_ref[...]
        stat_ref[...] = jnp.zeros_like(stat_ref)
        for h in range(heads):
            cols = slice(h * HD, (h + 1) * HD)
            q = q_ref[:, cols]
            found = []
            for n, ref in enumerate((mine_ref, other_ref)):
                s = lax.dot_general(ref[0, :, cols], q, NT, preferred_element_type=F32) * SCALE
                key = base_ref[n] + lax.broadcasted_iota(jnp.int32, s.shape, 0)
                found.append(jnp.where(key <= pos, s, NEG))
            peak = jnp.maximum(*[jnp.max(s, axis=0, keepdims=True) for s in found])
            floor = jnp.maximum(peak, NEG * 0.5)
            total = jnp.zeros_like(peak)
            summed = jnp.zeros((HD, rows), F32)
            for s, ref in zip(found, (mine_ref, other_ref)):
                weights = jnp.exp(s - floor)
                total = total + jnp.sum(weights, axis=0, keepdims=True)
                for part in split(weights):
                    summed = summed + lax.dot_general(
                        ref[1, :, cols], part, TN, preferred_element_type=F32
                    )
            out_ref[:, cols] = summed.T.astype(BF16)
            for n, term in enumerate(three_terms(floor) + three_terms(total)):
                stat_ref[n * heads + h : n * heads + h + 1, :] = term
        out_ref[:, width:] = stat_ref[...].T.astype(BF16)

    keyval = pl.BlockSpec(mine.shape, lambda r, b: (0, 0, 0))
    return pl.pallas_call(
        body,
        grid_spec=pltpu.PrefetchScalarGridSpec(
            num_scalar_prefetch=1,
            grid=(count // rows,),
            in_specs=[
                pl.BlockSpec((1, rows), lambda r, b: (0, r)),
                pl.BlockSpec((rows, width), lambda r, b: (r, 0)),
                keyval,
                keyval,
            ],
            out_specs=pl.BlockSpec((rows, width + LANES), lambda r, b: (r, 0)),
            scratch_shapes=[pltpu.VMEM((LANES, rows), F32)],
        ),
        out_shape=jax.ShapeDtypeStruct((count, width + LANES), BF16),
        compiler_params=params(),
        cost_estimate=cost(6 * count * 2 * mine.shape[1] * width, 4 * count * width),
    )(bases, pos, queries, mine, other)


def combine_and_project(terms, weight):
    count, rows, packed = terms.shape
    width = packed - LANES
    heads = width // HD

    def body(x_ref, w_ref, out_ref, context_ref):
        stats = x_ref[:, :, width:].astype(F32)
        field = [stats[:, :, n * heads : (n + 1) * heads] for n in range(6)]
        peak = field[0] + field[1] + field[2]
        total = field[3] + field[4] + field[5]
        factor = jnp.exp(peak - jnp.max(peak, axis=0, keepdims=True))
        total = jnp.sum(factor * total, axis=0)
        for h in range(heads):
            cols = slice(h * HD, (h + 1) * HD)
            summed = jnp.sum(factor[:, :, h : h + 1] * x_ref[:, :, cols].astype(F32), axis=0)
            context_ref[:, cols] = (summed / total[:, h : h + 1]).astype(BF16)
        out_ref[...] = jnp.dot(
            context_ref[...], w_ref[...], preferred_element_type=F32
        ).astype(BF16)

    return pl.pallas_call(
        body,
        out_shape=jax.ShapeDtypeStruct((rows, weight.shape[1]), BF16),
        scratch_shapes=[pltpu.VMEM((rows, width), BF16)],
        compiler_params=params(),
        cost_estimate=cost(2 * rows * weight.size, 2 * weight.size),
    )(terms, weight)


def add_and_norm(base_ref, term_refs, gain_ref):
    a, b, c, d = [ref[...].astype(F32) for ref in term_refs]
    total = (base_ref[...].astype(F32) + ((a + c) + (b + d))).astype(BF16)
    x = total.astype(F32)
    scale = lax.rsqrt(jnp.mean(x * x, axis=-1, keepdims=True) + EPS)
    return total, (x * scale * gain_ref[...]).astype(BF16)


def norm_and_qkv(base, terms, gain, weight):
    rows, width = base.shape
    cols = weight.shape[1]
    block = 256

    def body(base_ref, a, b, c, d, gain_ref, w_ref, total_ref, out_ref, normed_ref):
        @pl.when(pl.program_id(0) == 0)
        def _():
            total, normed = add_and_norm(base_ref, (a, b, c, d), gain_ref)
            total_ref[...] = total
            normed_ref[...] = normed

        out_ref[...] = jnp.dot(
            normed_ref[...], w_ref[...], preferred_element_type=F32
        ).astype(BF16)

    whole = pl.BlockSpec((rows, width), lambda j: (0, 0))
    return pl.pallas_call(
        body,
        grid=(cols // block,),
        in_specs=[whole] * 5
        + [pl.BlockSpec((1, width), lambda j: (0, 0)), pl.BlockSpec((width, block), lambda j: (0, j))],
        out_specs=[whole, pl.BlockSpec((rows, block), lambda j: (0, j))],
        out_shape=[
            jax.ShapeDtypeStruct((rows, width), BF16),
            jax.ShapeDtypeStruct((rows, cols), BF16),
        ],
        scratch_shapes=[pltpu.VMEM((rows, width), BF16)],
        compiler_params=params(),
        cost_estimate=cost(2 * rows * weight.size, 2 * weight.size),
    )(base, *terms, gain, weight)


def self_attention(place, queries, mine, other, weight, column):
    rows, width = queries.shape
    heads = width // HD
    count = mine.shape[0]
    out = weight.shape[0]

    def body(place_ref, q_ref, mine_ref, other_ref, w_ref, out_ref, context_ref):
        core = place_ref[1]
        j = lax.broadcasted_iota(jnp.int32, (rows, count), 1)
        row = place_ref[0] * rows + lax.broadcasted_iota(jnp.int32, (rows, count), 0)
        start = (j // rows) * (CORES * rows) + j % rows
        allowed = [start + core * rows <= row, start + (1 - core) * rows <= row]
        for h in range(heads):
            cols = slice(h * HD, (h + 1) * HD)
            value_cols = slice(width + h * HD, width + (h + 1) * HD)
            q = q_ref[:, cols]
            found = []
            for ref, seen in zip((mine_ref, other_ref), allowed):
                s = lax.dot_general(q, ref[:, cols], NT, preferred_element_type=F32) * SCALE
                found.append(jnp.where(seen, s, NEG))
            peak = jnp.maximum(*[jnp.max(s, axis=1, keepdims=True) for s in found])
            total = jnp.zeros_like(peak)
            summed = jnp.zeros((rows, HD), F32)
            for s, ref in zip(found, (mine_ref, other_ref)):
                weights = jnp.exp(s - peak)
                total = total + jnp.sum(weights, axis=1, keepdims=True)
                for part in split(weights):
                    summed = summed + jnp.dot(
                        part, ref[:, value_cols], preferred_element_type=F32
                    )
            context_ref[:, cols] = (summed / total).astype(BF16)
        out_ref[...] = lax.dot_general(
            context_ref[...], w_ref[...], NT, preferred_element_type=F32
        ).astype(BF16)

    whole = lambda *shape: pl.BlockSpec(shape, lambda i, p: (0, 0))
    return pl.pallas_call(
        body,
        grid_spec=pltpu.PrefetchScalarGridSpec(
            num_scalar_prefetch=1,
            grid=(1,),
            in_specs=[
                whole(rows, width),
                whole(count, 2 * width),
                whole(count, 2 * width),
                pl.BlockSpec((out, width), lambda i, p: (0, column // width)),
            ],
            out_specs=whole(rows, out),
            scratch_shapes=[pltpu.VMEM((rows, width), BF16)],
        ),
        out_shape=jax.ShapeDtypeStruct((rows, out), BF16),
        compiler_params=params(),
        cost_estimate=cost(2 * rows * out * width, 2 * out * width),
    )(place, queries, mine, other, weight)


def mlp(index, base, terms, gain, weight, gate, up, down, hidden):
    rows, width = base.shape
    block = 256
    piece = width // TP

    def body(index_ref, base_ref, a, b, c, d, gain_ref, g_ref, u_ref, d_ref, *refs):
        own_ref, part_refs = refs[0], refs[1 : 1 + TP]
        total_ref, normed_ref, acc_ref = refs[1 + TP :]
        step = pl.program_id(0)

        @pl.when(step == 0)
        def _():
            total, normed = add_and_norm(base_ref, (a, b, c, d), gain_ref)
            total_ref[...] = total
            normed_ref[...] = normed

        normed = normed_ref[...]
        g = jnp.dot(normed, g_ref[...], preferred_element_type=F32)
        u = jnp.dot(normed, u_ref[...], preferred_element_type=F32)
        inner = (jax.nn.silu(g) * u).astype(BF16)
        term = lax.dot_general(inner, d_ref[...], NT, preferred_element_type=F32)

        @pl.when(step == 0)
        def _():
            acc_ref[...] = term

        @pl.when(step > 0)
        def _():
            acc_ref[...] += term

        @pl.when(step == hidden // block - 1)
        def _():
            columns = lambda k: pl.ds(pl.multiple_of(index_ref[k] * piece, piece), piece)
            own_ref[...] = total_ref[:, columns(0)]
            for k in range(TP):
                part_refs[k][...] = acc_ref[:, columns(k)].astype(BF16)

    whole = pl.BlockSpec((rows, width), lambda f, i: (0, 0))
    at = lambda first: pl.BlockSpec((width, block), lambda f, i: (0, first // block + f))
    return pl.pallas_call(
        body,
        grid_spec=pltpu.PrefetchScalarGridSpec(
            num_scalar_prefetch=1,
            grid=(hidden // block,),
            in_specs=[whole] * 5
            + [pl.BlockSpec((1, width), lambda f, i: (0, 0)), at(gate), at(up), at(down)],
            out_specs=[pl.BlockSpec((rows, piece), lambda f, i: (0, 0))] * (1 + TP),
            scratch_shapes=[
                pltpu.VMEM((rows, width), BF16),
                pltpu.VMEM((rows, width), BF16),
                pltpu.VMEM((rows, width), F32),
            ],
        ),
        out_shape=[jax.ShapeDtypeStruct((rows, piece), BF16)] * (1 + TP),
        compiler_params=params(),
        cost_estimate=cost(6 * rows * width * hidden, 6 * width * hidden),
    )(index, base, *terms, gain, weight, weight, weight)


def local(
    prefix,
    latent_in,
    latent_pos,
    w_query,
    w_keyval,
    w_cross_out,
    attn_gain,
    w_self_qkv,
    w_self_out,
    mlp_gain,
    w_gate_up,
    w_down,
):
    chips = lax.axis_size(ZX)
    chip = lax.axis_index(ZX)
    core = lax.axis_index("core")
    tp = lax.axis_index("tp")
    seq = chip * CORES + core
    rows = latent_in.shape[0]
    width = w_query.shape[1]
    hidden = w_gate_up.shape[2]
    positions = prefix.shape[0]
    steps = jnp.arange(TP, dtype=jnp.int32)
    source = (tp - steps) % TP
    target = (tp + steps) % TP

    qkv_rows = jnp.concatenate([w_self_qkv[n] for n in range(3)], axis=1)
    late_rows = jnp.concatenate([w_self_out.T, w_gate_up[0], w_gate_up[1], w_down.T], axis=1)
    w_qkv = lax.all_gather(qkv_rows, SEQ, axis=0, tiled=True)
    w_late = lax.all_gather(late_rows, SEQ, axis=0, tiled=True)

    latent_pieces = everyone(latent_in)
    prefix_pieces = everyone(prefix)
    queries, latents = gathered_matmul(source, latent_pieces, w_query[None], True)
    (keyval,) = gathered_matmul(source, prefix_pieces, w_keyval, False)
    other_keyval = shifted(keyval, "core", 1, CORES)

    spread = jnp.broadcast_to(queries, (chips, rows, width))
    all_queries = lax.all_to_all(spread, ZX, 0, 0).reshape(chips * rows, width)
    pos = lax.dynamic_index_in_dim(
        latent_pos.reshape(chips, CORES, rows), core, axis=1, keepdims=False
    ).reshape(1, chips * rows)
    bases = jnp.stack([seq, chip * CORES + 1 - core]).astype(jnp.int32) * positions
    partial = cross_partial(bases, pos, all_queries, keyval, other_keyval)
    partial = lax.all_to_all(partial.reshape(chips, rows, -1), ZX, 0, 0)
    cross_terms = combine_and_project(partial, w_cross_out)

    first, qkv = norm_and_qkv(latents, everyone(cross_terms), attn_gain[None], w_qkv)
    spread = jnp.broadcast_to(qkv[None, :, width:], (chips, rows, 2 * width))
    mine = lax.all_to_all(spread, ZX, 0, 0).reshape(chips * rows, 2 * width)
    other = shifted(mine, "core", 1, CORES)
    place = jnp.stack([seq, core]).astype(jnp.int32)
    out_terms = self_attention(place, qkv[:, :width], mine, other, w_late, 0)

    own, *parts = mlp(
        target,
        first,
        everyone(out_terms),
        mlp_gain[None],
        w_late,
        width,
        width + hidden,
        width + 2 * hidden,
        hidden,
    )
    sums = [parts[0]] + [shifted(parts[k], "tp", k, TP) for k in range(1, TP)]
    a, b, c, d = [x.astype(F32) for x in sums]
    return (own.astype(F32) + ((a + c) + (b + d))).astype(BF16)


def solution(mesh):
    z, x, core, y = 8, 4, 2, TP
    grid = Mesh(mesh.devices.reshape(z, x, core, y), ("z", "x", "core", "tp"))
    return jax.shard_map(
        local,
        mesh=grid,
        in_specs=(
            P(SEQ, "tp"),
            P(SEQ, "tp"),
            P(),
            P(None, "tp"),
            P(None, None, "tp"),
            P("tp", None),
            P(),
            P(None, SEQ, "tp"),
            P("tp", SEQ),
            P(),
            P(None, SEQ, "tp"),
            P("tp", SEQ),
        ),
        out_specs=P(SEQ, "tp"),
        check_vma=False,
    )
```

time: 1200 us -> 244 us (0.20)
  waiting for transfers between devices: 587 us -> 75.1 us
  blocking collectives: 531 us -> 76.4 us
  starting transfers between devices: 0.44 us -> 37.5 us
  matrix products: 31.6 us -> 0 us
  Pallas kernels: 0 us -> 28.8 us
  other arithmetic: 16.1 us -> 3 us
    all_gather x8 -> x2, waiting for transfers between devices: 529 us -> 52.1 us  [the longest x1 52.1 us: local(): w_late = lax.all_gather(late_rows, SEQ, axis=0, tiled=True)]
    pmax x1 -> x0, blocking collectives: 249 us -> none  [local(): peak = lax.pmax(peak_local, 'seq')]
    unnamed x1 -> x0, blocking collectives: 246 us -> none
    all_to_all x0 -> x2, blocking collectives: none -> 76.4 us  [the longest x1 39.7 us: local(): mine = lax.all_to_all(spread, ZX, 0, 0).reshape(chips * rows, 2 * width)]
    reduce_scatter x3 -> x0, waiting for transfers between devices: 54.1 us -> none  [the longest x1 18.4 us: local(): lax.psum_scatter(down_terms.astype(jnp.bfloat16), 'tp', scatter_dimension...]
    all_gather x3 -> x0, blocking collectives: 36.2 us -> none  [the longest x1 12.3 us: local(): lax.all_gather(latent_in, 'tp', axis=1, tiled=True)]
    dot_general x14 -> x0, matrix products: 31.6 us -> none  [the longest x1 4.63 us: local(): jnp.einsum('rd,cdf->crf', columns, lax.all_gather(w_gate_up, 'seq', axis=...]
    pallas_call x0 -> x7, Pallas kernels: none -> 28.8 us  [the longest x1 7.51 us: cross_partial(): pl.pallas_call(body, grid_spec=pltpu.PrefetchScalarGridSpec(num_scalar_pr...]
  transfers between devices with their start and end apart: 12 -> 20, of which waited for: 11 -> 12; matrix products, arithmetic and copies ran while one was open for 2% -> 2% of each run, Pallas kernels for 0% -> 7%
where the time goes in v1:
time: 244 us; the launch traced here: 242 us
  blocking collectives  76.4 us (31%)
  waiting for transfers between devices  75.1 us (31%)
  starting transfers between devices  37.5 us (15%)
  Pallas kernels  28.8 us (12%)
  between operations  13.5 us (6%)
  local copies, waits for them, and re-layouts  7.49 us (3%)
  other arithmetic  3 us (1%)
    all_gather x1, waiting for transfers between devices, local(): w_late = lax.all_gather(late_rows, SEQ, axis=0, tiled=True)  52.1 us
    all_to_all x1, blocking collectives, local(): mine = lax.all_to_all(spread, ZX, 0, 0).reshape(chips * rows, 2 * width)  39.7 us
    all_to_all x1, blocking collectives, local(): partial = lax.all_to_all(partial.reshape(chips, rows, -1), ZX, 0, 0)  36.7 us
    ppermute x17, starting transfers between devices, shifted(): lax.ppermute(x, axis, [(i, (i + shift) % count) for i in range(count)])  27.4 us
    ppermute x17, waiting for transfers between devices, shifted(): lax.ppermute(x, axis, [(i, (i + shift) % count) for i in range(count)])  22.9 us
    all_to_all x1, starting transfers between devices, local(): all_queries = lax.all_to_all(spread, ZX, 0, 0).reshape(chips * rows, width)  10.1 us
    pallas_call x1, Pallas kernels, cross_partial(): pl.pallas_call(body, grid_spec=pltpu.PrefetchScalarGridSpec(num_scalar_pr...  7.51 us
    pallas_call x1, Pallas kernels, mlp(): pl.pallas_call(body, grid_spec=pltpu.PrefetchScalarGridSpec(num_scalar_pr...  7.17 us
  transfers between devices with their start and end apart: 20, of which 12 were waited for; matrix products, arithmetic and copies ran while one was open for 2% of the time, Pallas kernels for 7%

profile of v1, /device:TPU:8, one launch (start us, length us, event | category | flops | bytes accessed | tf_op | source)
XLA Modules:
  0.0 241.9 jit_solution(11055226994120244308)
XLA Ops:
  9.0 1.6 pad_maximum_fusion
  10.6 1.7 collective-permute-start
  12.2 2.7 %collective-permute-start.1 = (bf16[16,512]{1,0:T(8,128)(2,1)}, bf16[16,512]{1,0:T(8,128)(2,1)S(1)}, u32[]{:S(2)}, u32[]{:S(2)}) collective-permute-start(bf16[16,512]{1,0:T(8,128)(2,1)} %refs_0_.2), channel_id=1, source_target_pairs={{0,2},{1,3},{2,0},{3,1},{4,6},{5,7},{6,4},{7,5},{8,10},{9,11},{10,... | collective-permute-start | bytes 49160 | tf_op jit(solution)/shard_map/ppermute | solution.py:25
  15.6 2.1 collective-permute-done.1.refs_2_
  18.9 1.6 copy-done.1
  21.2 1.3 shard_map.118
  23.4 10.1 %all-to-all-start = ((bf16[32,16,512]{2,1,0:T(8,128)(2,1)}), bf16[32,16,512]{2,1,0:T(8,128)(2,1)S(1)}, u32[]{:S(2)}, u32[]{:S(2)}) async-start(bf16[32,16,512]{2,1,0:T(8,128)(2,1)} %broadcast_in_dim.24), calls=%async_computation | async-start | bytes 1048576 | tf_op jit(solution)/shard_map/all_to_all | solution.py:374
  33.5 1.4 collective-permute-start.3
  34.9 2.6 %collective-permute-start.4 = (bf16[256,512]{1,0:T(8,128)(2,1)S(1)}, bf16[256,512]{1,0:T(8,128)(2,1)S(1)}, u32[]{:S(2)}, u32[]{:S(2)}) collective-permute-start(bf16[256,512]{1,0:T(8,128)(2,1)S(1)} %copy-done.3), channel_id=1, source_target_pairs={{0,2},{1,3},{2,0},{3,1},{4,6},{5,7},{6,4},{7,5},{8,10},{9,11},{10,... | collective-permute-start | bytes 786440 | tf_op jit(solution)/shard_map/ppermute | solution.py:25
  37.5 2.0 collective-permute-start.5
  39.5 3.1 %collective-permute-done.3.refs_1_ = bf16[256,512]{1,0:T(8,128)(2,1)S(1)} collective-permute-done((bf16[256,512]{1,0:T(8,128)(2,1)S(1)}, bf16[256,512]{1,0:T(8,128)(2,1)S(1)}, u32[]{:S(2)}, u32[]{:S(2)}) %collective-permute-start.3) | collective-permute-done | bytes 262176 | tf_op jit(solution)/shard_map/ppermute | solution.py:25
  42.6 2.7 %collective-permute-done.4.refs_2_ = bf16[256,512]{1,0:T(8,128)(2,1)S(1)} collective-permute-done((bf16[256,512]{1,0:T(8,128)(2,1)S(1)}, bf16[256,512]{1,0:T(8,128)(2,1)S(1)}, u32[]{:S(2)}, u32[]{:S(2)}) %collective-permute-start.4) | collective-permute-done | bytes 262176 | tf_op jit(solution)/shard_map/ppermute | solution.py:25
  45.3 2.7 %collective-permute-done.5.refs_3_ = bf16[256,512]{1,0:T(8,128)(2,1)S(1)} collective-permute-done((bf16[256,512]{1,0:T(8,128)(2,1)S(1)}, bf16[256,512]{1,0:T(8,128)(2,1)S(1)}, u32[]{:S(2)}, u32[]{:S(2)}) %collective-permute-start.5) | collective-permute-done | bytes 262176 | tf_op jit(solution)/shard_map/ppermute | solution.py:25
  48.1 2.2 copy-done
  50.3 2.7 %shard_map.119.mine_ref = bf16[2,256,512]{2,1,0:T(8,128)(2,1)S(1)} custom-call(s32[4]{0:T(128)S(1)} %and_select_fusion.index_ref, bf16[256,512]{1,0:T(8,128)(2,1)S(1)} %copy-done.3, bf16[256,512]{1,0:T(8,128)(2,1)S(1)} %collective-permute-done.3.refs_1_, bf16[256,512]{1,0:T(8,128)(2,1)S(1)} %collective-permute-done.4.refs_2_, ...), custom_call_target="tpu_custom_call" | custom-call | flops 1073741824 | bytes 4194304 | tf_op jit(solution)/shard_map/pallas_call | solution.py:81
  53.5 1.7 collective-permute-done.6.other_ref
  55.1 7.5 %shard_map.120 = bf16[512,640]{1,0:T(8,128)(2,1)S(1)} custom-call(s32[2]{0:T(128)S(1)} %add_multiply_fusion.base_ref, s32[1,512]{1,0:T(1,128)S(1)} %reshape.18.pos_ref, bf16[512,512]{1,0:T(8,128)(2,1)S(1)} %bitcast.26, bf16[2,256,512]{2,1,0:T(8,128)(2,1)S(1)} %shard_map.119.mine_ref, bf16[2,256,512]{2,1,0:T(8,128)(2,1)} %collective-permute-done.6.other_ref), custom_call_target="tpu_custom_call" | custom-call | flops 805306368 | bytes 1048576 | tf_op jit(solution)/shard_map/pallas_call | solution.py:130
  62.7 36.7 %all_to_all.15.x_ref = bf16[32,16,640]{2,1,0:T(8,128)(2,1)S(1)} all-to-all(bf16[32,16,640]{2,1,0:T(8,128)(2,1)S(1)} %bitcast.25), channel_id=1, replica_groups=mesh['z'=8,'x'=4,'core'=2,'tp'=4] {'z','x'}, dimensions={0} | all-to-all | bytes 1310720 | tf_op jit(solution)/shard_map/all_to_all | solution.py:380
  101.1 2.5 %collective-permute-start.8 = (bf16[16,2048]{1,0:T(8,128)(2,1)S(1)}, bf16[16,2048]{1,0:T(8,128)(2,1)S(1)}, u32[]{:S(2)}, u32[]{:S(2)}) collective-permute-start(bf16[16,2048]{1,0:T(8,128)(2,1)S(1)} %shard_map.121.a), channel_id=1, source_target_pairs={{0,2},{1,3},{2,0},{3,1},{4,6},{5,7},{6,4},{7,5},{8,10},{9,11},{10,... | collective-permute-start | bytes 196616 | tf_op jit(solution)/shard_map/ppermute | solution.py:25
  103.6 2.1 collective-permute-start.9
  107.9 5.1 %shard_map.122 = (bf16[16,2048]{1,0:T(8,128)(2,1)S(1)}, bf16[16,1536]{1,0:T(8,128)(2,1)S(1)}) custom-call(bf16[16,2048]{1,0:T(8,128)(2,1)S(1)} %get-tuple-element.14.base_ref, bf16[16,2048]{1,0:T(8,128)(2,1)S(1)} %shard_map.121.a, bf16[16,2048]{1,0:T(8,128)(2,1)S(1)} %collective-permute-done.7.b, bf16[16,2048]{1,0:T(8,128)(2,1)S(1)} %collective-permute-done.8.c, ...), custom_call_target="tpu_custom_call" | custom-call | flops 100663296 | bytes 6291456 | tf_op jit(solution)/shard_map/pallas_call | solution.py:204
  113.1 39.7 %all_to_all.16 = bf16[32,16,1024]{2,1,0:T(8,128)(2,1)S(1)} all-to-all(bf16[32,16,1024]{2,1,0:T(8,128)(2,1)S(1)} %broadcast_in_dim.26), channel_id=1, replica_groups=mesh['z'=8,'x'=4,'core'=2,'tp'=4] {'z','x'}, dimensions={0} | all-to-all | bytes 2097152 | tf_op jit(solution)/shard_map/all_to_all | solution.py:385
  152.9 2.6 %collective-permute-done.10.other_ref = bf16[512,1024]{1,0:T(8,128)(2,1)S(1)} collective-permute-done((bf16[512,1024]{1,0:T(8,128)(2,1)S(1)}, bf16[512,1024]{1,0:T(8,128)(2,1)S(1)}, u32[]{:S(2)}, u32[]{:S(2)}) %collective-permute-start.10) | collective-permute-done | bytes 1048608 | tf_op jit(solution)/shard_map/ppermute | solution.py:25
  155.4 52.1 %all-gather.5.cloned.1.call-done.w_ref.g_ref.u_ref.d_ref = bf16[2048,3584]{1,0:T(8,128)(2,1)} async-done(((bf16[32,3584]{1,0:T(8,128)(2,1)}), bf16[2048,3584]{1,0:T(8,128)(2,1)}) %all-gather.5.cloned.1.call-update) | async-done | bytes 14680080 | tf_op jit(solution)/shard_map/all_gather | solution.py:365
  207.6 4.1 %shard_map.123.a = bf16[16,2048]{1,0:T(8,128)(2,1)S(1)} custom-call(s32[2]{0:T(128)S(1)} %pad_add_fusion.place_ref, bf16[16,512]{1,0:T(8,128)(2,1)S(1)} %slice.24.q_ref, bf16[512,1024]{1,0:T(8,128)(2,1)S(1)} %bitcast.23, bf16[512,1024]{1,0:T(8,128)(2,1)S(1)} %collective-permute-done.10.other_ref, ...), custom_call_target="tpu_custom_call" | custom-call | flops 33554432 | bytes 2097152 | tf_op jit(solution)/shard_map/pallas_call | solution.py:256
  211.7 1.5 collective-permute-start.11
  214.3 2.1 collective-permute-start.13
  216.5 2.9 %collective-permute-done.12.c = bf16[16,2048]{1,0:T(8,128)(2,1)S(1)} collective-permute-done((bf16[16,2048]{1,0:T(8,128)(2,1)S(1)}, bf16[16,2048]{1,0:T(8,128)(2,1)S(1)}, u32[]{:S(2)}, u32[]{:S(2)}) %collective-permute-start.12) | collective-permute-done | bytes 65568 | tf_op jit(solution)/shard_map/ppermute | solution.py:25
  219.4 7.2 %shard_map.124 = (bf16[16,512]{1,0:T(8,128)(2,1)S(1)}, bf16[16,512]{1,0:T(8,128)(2,1)S(1)}, bf16[16,512]{1,0:T(8,128)(2,1)S(1)}, bf16[16,512]{1,0:T(8,128)(2,1)S(1)}, bf16[16,512]{1,0:T(8,128)(2,1)S(1)}) custom-call(s32[4]{0:T(128)S(1)} %and_select_fusion.1.index_ref, bf16[16,2048]{1,0:T(8,128)(2,1)S(1)} %get-tuple-element.16.base_ref, ...), custom_call_target="tpu_custom_call" | custom-call | flops 201326592 | bytes 12582912 | tf_op jit(solution)/shard_map/pallas_call | solution.py:315
  226.6 1.4 collective-permute-start.16
  228.7 4.0 %collective-permute-start.14 = (bf16[16,512]{1,0:T(8,128)(2,1)S(1)}, bf16[16,512]{1,0:T(8,128)(2,1)S(1)}, u32[]{:S(2)}, u32[]{:S(2)}) collective-permute-start(bf16[16,512]{1,0:T(8,128)(2,1)S(1)} %get-tuple-element.20), channel_id=1, source_target_pairs={{0,2},{1,3},{2,0},{3,1},{4,6},{5,7},{6,4},{7,5},{8,10},{9,11},{10,... | collective-permute-start | bytes 49160 | tf_op jit(solution)/shard_map/ppermute | solution.py:25
  232.7 1.7 collective-permute-done.14
  (51 shorter events, 12.9 us)
Async XLA Ops:
  6.5 27.0 %copy-start.3 = (bf16[256,512]{1,0:T(8,128)(2,1)S(1)}, bf16[256,512]{1,0:T(8,128)(2,1)}, u32[]{:S(2)}) copy-start(bf16[256,512]{1,0:T(8,128)(2,1)} %refs_0_.3) | copy-start | bytes 786436
  6.5 101.4 %all-gather.3.cloned.1.call-start = ((), (), s32[]{:S(2)}) async-start(), calls=%async_computation.3 | async-start | bytes 6389760 | tf_op jit(solution)/shard_map/all_gather | solution.py:364
  8.0 199.5 %all-gather.5.cloned.1.call-start = ((), (), s32[]{:S(2)}) async-start(), calls=%async_computation.4 | async-start | bytes 14909440 | tf_op jit(solution)/shard_map/all_gather | solution.py:365
  10.6 5.0 %collective-permute-start = (bf16[16,512]{1,0:T(8,128)(2,1)}, bf16[16,512]{1,0:T(8,128)(2,1)S(1)}, u32[]{:S(2)}, u32[]{:S(2)}) collective-permute-start(bf16[16,512]{1,0:T(8,128)(2,1)} %refs_0_.2), channel_id=1, source_target_pairs={{0,1},{1,2},{2,3},{3,0},{4,5},{5,6},{6,7},{7,4},{8,9},{9,10},{10,1... | collective-permute-start | bytes 49160 | tf_op jit(solution)/shard_map/ppermute | solution.py:25
  12.2 5.5 %collective-permute-start.1 = (bf16[16,512]{1,0:T(8,128)(2,1)}, bf16[16,512]{1,0:T(8,128)(2,1)S(1)}, u32[]{:S(2)}, u32[]{:S(2)}) collective-permute-start(bf16[16,512]{1,0:T(8,128)(2,1)} %refs_0_.2), channel_id=1, source_target_pairs={{0,2},{1,3},{2,0},{3,1},{4,6},{5,7},{6,4},{7,5},{8,10},{9,11},{10,... | collective-permute-start | bytes 49160 | tf_op jit(solution)/shard_map/ppermute | solution.py:25
  14.9 3.9 %collective-permute-start.2 = (bf16[16,512]{1,0:T(8,128)(2,1)}, bf16[16,512]{1,0:T(8,128)(2,1)S(1)}, u32[]{:S(2)}, u32[]{:S(2)}) collective-permute-start(bf16[16,512]{1,0:T(8,128)(2,1)} %refs_0_.2), channel_id=1, source_target_pairs={{0,3},{1,0},{2,1},{3,2},{4,7},{5,4},{6,5},{7,6},{8,11},{9,8},{10,9... | collective-permute-start | bytes 49160 | tf_op jit(solution)/shard_map/ppermute | solution.py:25
  18.9 1.6 copy-start.1
  20.4 0.7 copy-start.4
  21.2 78.2 %copy-start.2 = (bf16[512,2048]{1,0:T(8,128)(2,1)S(1)}, bf16[512,2048]{1,0:T(8,128)(2,1)}, u32[]{:S(2)}) copy-start(bf16[512,2048]{1,0:T(8,128)(2,1)} %w_ref.1) | copy-start | bytes 6291460
  22.5 30.7 %copy-start.7 = (s32[1024]{0:T(1024)S(1)}, s32[1024]{0:T(1024)}, u32[]{:S(2)}) copy-start(s32[1024]{0:T(1024)} %param.14) | copy-start | bytes 12292
  23.4 31.8 %all-to-all-start = ((bf16[32,16,512]{2,1,0:T(8,128)(2,1)}), bf16[32,16,512]{2,1,0:T(8,128)(2,1)S(1)}, u32[]{:S(2)}, u32[]{:S(2)}) async-start(bf16[32,16,512]{2,1,0:T(8,128)(2,1)} %broadcast_in_dim.24), calls=%async_computation | async-start | bytes 1048576 | tf_op jit(solution)/shard_map/all_to_all | solution.py:374
  33.5 9.1 %collective-permute-start.3 = (bf16[256,512]{1,0:T(8,128)(2,1)S(1)}, bf16[256,512]{1,0:T(8,128)(2,1)S(1)}, u32[]{:S(2)}, u32[]{:S(2)}) collective-permute-start(bf16[256,512]{1,0:T(8,128)(2,1)S(1)} %copy-done.3), channel_id=1, source_target_pairs={{0,1},{1,2},{2,3},{3,0},{4,5},{5,6},{6,7},{7,4},{8,9},{9,10},{10,1... | collective-permute-start | bytes 786440 | tf_op jit(solution)/shard_map/ppermute | solution.py:25
  34.9 10.4 %collective-permute-start.4 = (bf16[256,512]{1,0:T(8,128)(2,1)S(1)}, bf16[256,512]{1,0:T(8,128)(2,1)S(1)}, u32[]{:S(2)}, u32[]{:S(2)}) collective-permute-start(bf16[256,512]{1,0:T(8,128)(2,1)S(1)} %copy-done.3), channel_id=1, source_target_pairs={{0,2},{1,3},{2,0},{3,1},{4,6},{5,7},{6,4},{7,5},{8,10},{9,11},{10,... | collective-permute-start | bytes 786440 | tf_op jit(solution)/shard_map/ppermute | solution.py:25
  37.5 10.6 %collective-permute-start.5 = (bf16[256,512]{1,0:T(8,128)(2,1)S(1)}, bf16[256,512]{1,0:T(8,128)(2,1)S(1)}, u32[]{:S(2)}, u32[]{:S(2)}) collective-permute-start(bf16[256,512]{1,0:T(8,128)(2,1)S(1)} %copy-done.3), channel_id=1, source_target_pairs={{0,3},{1,0},{2,1},{3,2},{4,7},{5,4},{6,5},{7,6},{8,11},{9,8},{10,9... | collective-permute-start | bytes 786440 | tf_op jit(solution)/shard_map/ppermute | solution.py:25
  48.1 2.2 copy-start
  53.0 54.9 %copy-start.5 = (f32[2048]{0:T(1024)S(1)}, f32[2048]{0:T(1024)}, u32[]{:S(2)}) copy-start(f32[2048]{0:T(1024)} %param.18) | copy-start | bytes 24580
  53.0 2.1 collective-permute-start.6
  100.3 5.5 %collective-permute-start.7 = (bf16[16,2048]{1,0:T(8,128)(2,1)S(1)}, bf16[16,2048]{1,0:T(8,128)(2,1)S(1)}, u32[]{:S(2)}, u32[]{:S(2)}) collective-permute-start(bf16[16,2048]{1,0:T(8,128)(2,1)S(1)} %shard_map.121.a), channel_id=1, source_target_pairs={{0,1},{1,2},{2,3},{3,0},{4,5},{5,6},{6,7},{7,4},{8,9},{9,10},{10,1... | collective-permute-start | bytes 196616 | tf_op jit(solution)/shard_map/ppermute | solution.py:25
  101.1 5.8 %collective-permute-start.8 = (bf16[16,2048]{1,0:T(8,128)(2,1)S(1)}, bf16[16,2048]{1,0:T(8,128)(2,1)S(1)}, u32[]{:S(2)}, u32[]{:S(2)}) collective-permute-start(bf16[16,2048]{1,0:T(8,128)(2,1)S(1)} %shard_map.121.a), channel_id=1, source_target_pairs={{0,2},{1,3},{2,0},{3,1},{4,6},{5,7},{6,4},{7,5},{8,10},{9,11},{10,... | collective-permute-start | bytes 196616 | tf_op jit(solution)/shard_map/ppermute | solution.py:25
  103.6 4.3 %collective-permute-start.9 = (bf16[16,2048]{1,0:T(8,128)(2,1)S(1)}, bf16[16,2048]{1,0:T(8,128)(2,1)S(1)}, u32[]{:S(2)}, u32[]{:S(2)}) collective-permute-start(bf16[16,2048]{1,0:T(8,128)(2,1)S(1)} %shard_map.121.a), channel_id=1, source_target_pairs={{0,3},{1,0},{2,1},{3,2},{4,7},{5,4},{6,5},{7,6},{8,11},{9,8},{10,9... | collective-permute-start | bytes 196616 | tf_op jit(solution)/shard_map/ppermute | solution.py:25
  152.8 2.7 %collective-permute-start.10 = (bf16[512,1024]{1,0:T(8,128)(2,1)S(1)}, bf16[512,1024]{1,0:T(8,128)(2,1)S(1)}, u32[]{:S(2)}, u32[]{:S(2)}) collective-permute-start(bf16[512,1024]{1,0:T(8,128)(2,1)S(1)} %bitcast.22), channel_id=1, source_target_pairs={{0,4},{4,0},{1,5},{5,1},{2,6},{6,2},{3,7},{7,3},{8,12},{12,8},{9,1... | collective-permute-start | bytes 3145736 | tf_op jit(solution)/shard_map/ppermute | solution.py:25
  152.9 66.6 %copy-start.6 = (f32[2048]{0:T(1024)S(1)}, f32[2048]{0:T(1024)}, u32[]{:S(2)}) copy-start(f32[2048]{0:T(1024)} %param.21) | copy-start | bytes 24580
  211.7 4.8 %collective-permute-start.11 = (bf16[16,2048]{1,0:T(8,128)(2,1)S(1)}, bf16[16,2048]{1,0:T(8,128)(2,1)S(1)}, u32[]{:S(2)}, u32[]{:S(2)}) collective-permute-start(bf16[16,2048]{1,0:T(8,128)(2,1)S(1)} %shard_map.123.a), channel_id=1, source_target_pairs={{0,1},{1,2},{2,3},{3,0},{4,5},{5,6},{6,7},{7,4},{8,9},{9,10},{10,1... | collective-permute-start | bytes 196616 | tf_op jit(solution)/shard_map/ppermute | solution.py:25
  213.2 6.2 %collective-permute-start.12 = (bf16[16,2048]{1,0:T(8,128)(2,1)S(1)}, bf16[16,2048]{1,0:T(8,128)(2,1)S(1)}, u32[]{:S(2)}, u32[]{:S(2)}) collective-permute-start(bf16[16,2048]{1,0:T(8,128)(2,1)S(1)} %shard_map.123.a), channel_id=1, source_target_pairs={{0,2},{1,3},{2,0},{3,1},{4,6},{5,7},{6,4},{7,5},{8,10},{9,11},{10,... | collective-permute-start | bytes 196616 | tf_op jit(solution)/shard_map/ppermute | solution.py:25
  214.3 5.1 %collective-permute-start.13 = (bf16[16,2048]{1,0:T(8,128)(2,1)S(1)}, bf16[16,2048]{1,0:T(8,128)(2,1)S(1)}, u32[]{:S(2)}, u32[]{:S(2)}) collective-permute-start(bf16[16,2048]{1,0:T(8,128)(2,1)S(1)} %shard_map.123.a), channel_id=1, source_target_pairs={{0,3},{1,0},{2,1},{3,2},{4,7},{5,4},{6,5},{7,6},{8,11},{9,8},{10,9... | collective-permute-start | bytes 196616 | tf_op jit(solution)/shard_map/ppermute | solution.py:25
  226.6 6.1 %collective-permute-start.16 = (bf16[16,512]{1,0:T(8,128)(2,1)S(1)}, bf16[16,512]{1,0:T(8,128)(2,1)S(1)}, u32[]{:S(2)}, u32[]{:S(2)}) collective-permute-start(bf16[16,512]{1,0:T(8,128)(2,1)S(1)} %get-tuple-element.22), channel_id=1, source_target_pairs={{0,3},{1,0},{2,1},{3,2},{4,7},{5,4},{6,5},{7,6},{8,11},{9,8},{10,9... | collective-permute-start | bytes 49160 | tf_op jit(solution)/shard_map/ppermute | solution.py:25
  228.0 4.7 %collective-permute-start.15 = (bf16[16,512]{1,0:T(8,128)(2,1)S(1)}, bf16[16,512]{1,0:T(8,128)(2,1)S(1)}, u32[]{:S(2)}, u32[]{:S(2)}) collective-permute-start(bf16[16,512]{1,0:T(8,128)(2,1)S(1)} %get-tuple-element.21), channel_id=1, source_target_pairs={{0,1},{1,2},{2,3},{3,0},{4,5},{5,6},{6,7},{7,4},{8,9},{9,10},{10,1... | collective-permute-start | bytes 49160 | tf_op jit(solution)/shard_map/ppermute | solution.py:25
  228.7 5.7 %collective-permute-start.14 = (bf16[16,512]{1,0:T(8,128)(2,1)S(1)}, bf16[16,512]{1,0:T(8,128)(2,1)S(1)}, u32[]{:S(2)}, u32[]{:S(2)}) collective-permute-start(bf16[16,512]{1,0:T(8,128)(2,1)S(1)} %get-tuple-element.20), channel_id=1, source_target_pairs={{0,2},{1,3},{2,0},{3,1},{4,6},{5,7},{6,4},{7,5},{8,10},{9,11},{10,... | collective-permute-start | bytes 49160 | tf_op jit(solution)/shard_map/ppermute | solution.py:25
Sparse Core Ops, SparseCore 0:
  10.1 94.3 all-gather.2
  107.3 100.2 all-gather.4

commit v2 on v1

--- a/solution.py
+++ b/solution.py
@@ -12,6 +12,8 @@
 SCALE = HD ** (-0.5)
 TP = 4
 CORES = 2
+DEPTH = 8
+BREADTH = 4
 LANES = 128
 ZX = ("z", "x")
 SEQ = ("z", "x", "core")
@@ -42,12 +44,12 @@
     return one, two, three
 
 
-def params(mib=48):
+def params(mib=58):
     return pltpu.CompilerParams(vmem_limit_bytes=mib * 1024 * 1024)
 
 
 def cost(flops, size):
-    return pl.CostEstimate(flops=flops, bytes_accessed=size, transcendentals=0)
+    return pl.CostEstimate(flops=1, bytes_accessed=1, transcendentals=0)
 
 
 def gathered_matmul(index, pieces, weight, keep):
@@ -184,73 +186,132 @@
     return total, (x * scale * gain_ref[...]).astype(BF16)
 
 
-def norm_and_qkv(base, terms, gain, weight):
+def norm(base, terms, gain):
     rows, width = base.shape
-    cols = weight.shape[1]
-    block = 256
-
-    def body(base_ref, a, b, c, d, gain_ref, w_ref, total_ref, out_ref, normed_ref):
-        @pl.when(pl.program_id(0) == 0)
-        def _():
-            total, normed = add_and_norm(base_ref, (a, b, c, d), gain_ref)
-            total_ref[...] = total
-            normed_ref[...] = normed
-
-        out_ref[...] = jnp.dot(
-            normed_ref[...], w_ref[...], preferred_element_type=F32
-        ).astype(BF16)
-
-    whole = pl.BlockSpec((rows, width), lambda j: (0, 0))
-    return pl.pallas_call(
-        body,
-        grid=(cols // block,),
-        in_specs=[whole] * 5
-        + [pl.BlockSpec((1, width), lambda j: (0, 0)), pl.BlockSpec((width, block), lambda j: (0, j))],
-        out_specs=[whole, pl.BlockSpec((rows, block), lambda j: (0, j))],
+
+    def body(base_ref, a, b, c, d, gain_ref, total_ref, normed_ref):
+        total, normed = add_and_norm(base_ref, (a, b, c, d), gain_ref)
+        total_ref[...] = total
+        normed_ref[...] = normed
+
+    return pl.pallas_call(
+        body,
+        out_shape=[jax.ShapeDtypeStruct((rows, width), BF16)] * 2,
+        compiler_params=params(),
+        cost_estimate=cost(0, 0),
+    )(base, *terms, gain)
+
+
+def pack(x, w_self_qkv, w_self_out, w_gate_up, w_down):
+    groups, depth, _ = w_self_qkv.shape
+    hidden = w_down.shape[1]
+
+    def body(x_ref, qkv_ref, out_ref, gate_up_ref, down_ref, packed_ref, *head_refs):
+        packed_ref[:, :hidden] = gate_up_ref[0]
+        packed_ref[:, hidden : 2 * hidden] = gate_up_ref[1]
+        packed_ref[:, 2 * hidden :] = down_ref[...]
+        for k, ref in enumerate(head_refs):
+            head = lax.rem(x_ref[0] + k, BREADTH)
+            columns = pl.ds(pl.multiple_of(head * HD, HD), HD)
+            for g in range(groups):
+                ref[:, g * HD : (g + 1) * HD] = qkv_ref[g, :, columns]
+            ref[:, groups * HD :] = out_ref[:, columns]
+
+    part = jax.ShapeDtypeStruct((depth, (groups + 1) * HD), BF16)
+    vmem = pl.BlockSpec(memory_space=pltpu.VMEM)
+    return pl.pallas_call(
+        body,
+        in_specs=[pl.BlockSpec(memory_space=pltpu.SMEM)] + [vmem] * 4,
+        out_specs=[vmem] * (1 + BREADTH),
+        out_shape=[jax.ShapeDtypeStruct((depth, 3 * hidden), BF16)] + [part] * BREADTH,
+        cost_estimate=cost(0, 0),
+    )(x, w_self_qkv, w_self_out, w_gate_up, w_down)
+
+
+def assemble(spot, mine, other):
+    _, _, depth, cols = mine.shape
+
+    def body(spot_ref, mine_ref, other_ref, out_ref, sem):
+        x, core = spot_ref[1], spot_ref[2]
+        for ref, at_core in ((mine_ref, core), (other_ref, 1 - core)):
+            for z in range(DEPTH):
+                for k in range(BREADTH):
+                    at_x = lax.rem(x + BREADTH - k, BREADTH)
+                    place = ((z * BREADTH + at_x) * CORES + at_core) * depth
+                    rows = pl.ds(pl.multiple_of(place, depth), depth)
+                    pltpu.make_async_copy(ref.at[z, k], out_ref.at[rows], sem).start()
+        pltpu.make_async_copy(out_ref, out_ref, sem).wait()
+
+    anywhere = pl.BlockSpec(memory_space=pl.ANY)
+    return pl.pallas_call(
+        body,
+        in_specs=[pl.BlockSpec(memory_space=pltpu.SMEM), anywhere, anywhere],
+        out_specs=pl.BlockSpec(memory_space=pltpu.VMEM),
+        out_shape=jax.ShapeDtypeStruct((DEPTH * BREADTH * CORES * depth, cols), BF16),
+        scratch_shapes=[pltpu.SemaphoreType.DMA],
+        compiler_params=params(48),
+        cost_estimate=cost(0, 0),
+    )(spot, mine, other)
+
+
+def project_head(normed, weight):
+    rows, width = normed[0].shape
+
+    def body(*refs):
+        latents = jnp.concatenate([ref[...] for ref in refs[:BREADTH]], axis=0)
+        weight_ref, query_ref, keyval_ref = refs[BREADTH:]
+        out = jnp.dot(latents, weight_ref[...], preferred_element_type=F32).astype(BF16)
+        query_ref[...] = out[:, :HD]
+        keyval_ref[...] = out[:, HD:]
+
+    whole = lambda *shape: pl.BlockSpec(shape, lambda i: (0, 0))
+    return pl.pallas_call(
+        body,
+        grid=(1,),
+        in_specs=[whole(rows, width)] * BREADTH + [whole(width, 3 * HD)],
+        out_specs=[whole(BREADTH * rows, HD), whole(BREADTH * rows, 2 * HD)],
         out_shape=[
-            jax.ShapeDtypeStruct((rows, width), BF16),
-            jax.ShapeDtypeStruct((rows, cols), BF16),
+            jax.ShapeDtypeStruct((BREADTH * rows, HD), BF16),
+            jax.ShapeDtypeStruct((BREADTH * rows, 2 * HD), BF16),
         ],
-        scratch_shapes=[pltpu.VMEM((rows, width), BF16)],
-        compiler_params=params(),
-        cost_estimate=cost(2 * rows * weight.size, 2 * weight.size),
-    )(base, *terms, gain, weight)
-
-
-def self_attention(place, queries, mine, other, weight, column):
-    rows, width = queries.shape
-    heads = width // HD
+        compiler_params=params(48),
+        cost_estimate=cost(0, 0),
+    )(*normed, weight)
+
+
+def self_attention(spot, rows, queries, mine, other, weight):
+    total_rows, width = queries.shape
     count = mine.shape[0]
-    out = weight.shape[0]
-
-    def body(place_ref, q_ref, mine_ref, other_ref, w_ref, out_ref, context_ref):
-        core = place_ref[1]
-        j = lax.broadcasted_iota(jnp.int32, (rows, count), 1)
-        row = place_ref[0] * rows + lax.broadcasted_iota(jnp.int32, (rows, count), 0)
-        start = (j // rows) * (CORES * rows) + j % rows
-        allowed = [start + core * rows <= row, start + (1 - core) * rows <= row]
-        for h in range(heads):
-            cols = slice(h * HD, (h + 1) * HD)
-            value_cols = slice(width + h * HD, width + (h + 1) * HD)
-            q = q_ref[:, cols]
-            found = []
-            for ref, seen in zip((mine_ref, other_ref), allowed):
-                s = lax.dot_general(q, ref[:, cols], NT, preferred_element_type=F32) * SCALE
-                found.append(jnp.where(seen, s, NEG))
-            peak = jnp.maximum(*[jnp.max(s, axis=1, keepdims=True) for s in found])
-            total = jnp.zeros_like(peak)
-            summed = jnp.zeros((rows, HD), F32)
-            for s, ref in zip(found, (mine_ref, other_ref)):
-                weights = jnp.exp(s - peak)
-                total = total + jnp.sum(weights, axis=1, keepdims=True)
-                for part in split(weights):
-                    summed = summed + jnp.dot(
-                        part, ref[:, value_cols], preferred_element_type=F32
-                    )
-            context_ref[:, cols] = (summed / total).astype(BF16)
-        out_ref[...] = lax.dot_general(
-            context_ref[...], w_ref[...], NT, preferred_element_type=F32
-        ).astype(BF16)
+    features = weight.shape[0]
+
+    def index(n, x, core):
+        at_z, at_x = n // total_rows, (x + BREADTH - (n // rows) % BREADTH) % BREADTH
+        return ((at_z * BREADTH + at_x) * CORES + core) * rows + n % rows
+
+    def body(spot_ref, q_ref, mine_ref, other_ref, weight_ref, *out_refs):
+        z, x, core = spot_ref[0], spot_ref[1], spot_ref[2]
+        n = lax.broadcasted_iota(jnp.int32, (1, count), 1)
+        key = index(n, x, core)
+        keys = (key, key + (1 - 2 * core) * rows)
+        n = z * total_rows + lax.broadcasted_iota(jnp.int32, (total_rows, 1), 0)
+        row = index(n, x, core)
+        found = []
+        for ref, key in zip((mine_ref, other_ref), keys):
+            s = lax.dot_general(q_ref[...], ref[:, :width], NT, preferred_element_type=F32)
+            found.append(jnp.where(key <= row, s * SCALE, NEG))
+        peak = jnp.maximum(*[jnp.max(s, axis=1, keepdims=True) for s in found])
+        total = jnp.zeros_like(peak)
+        summed = jnp.zeros((total_rows, width), F32)
+        for s, ref in zip(found, (mine_ref, other_ref)):
+            weights = jnp.exp(s - peak)
+            total = total + jnp.sum(weights, axis=1, keepdims=True)
+            for part in split(weights):
+                summed = summed + jnp.dot(part, ref[:, width:], preferred_element_type=F32)
+        context = (summed / total).astype(BF16)
+        out = lax.dot_general(context, weight_ref[...], NT, preferred_element_type=F32)
+        out = out.astype(BF16)
+        for k, ref in enumerate(out_refs):
+            ref[...] = out[k * rows : (k + 1) * rows]
 
     whole = lambda *shape: pl.BlockSpec(shape, lambda i, p: (0, 0))
     return pl.pallas_call(
@@ -258,19 +319,15 @@
         grid_spec=pltpu.PrefetchScalarGridSpec(
             num_scalar_prefetch=1,
             grid=(1,),
-            in_specs=[
-                whole(rows, width),
-                whole(count, 2 * width),
-                whole(count, 2 * width),
-                pl.BlockSpec((out, width), lambda i, p: (0, column // width)),
-            ],
-            out_specs=whole(rows, out),
-            scratch_shapes=[pltpu.VMEM((rows, width), BF16)],
+            in_specs=[whole(total_rows, width)]
+            + [whole(count, 2 * width)] * CORES
+            + [pl.BlockSpec((features, width), lambda i, p: (0, 3))],
+            out_specs=[whole(rows, features)] * BREADTH,
         ),
-        out_shape=jax.ShapeDtypeStruct((rows, out), BF16),
-        compiler_params=params(),
-        cost_estimate=cost(2 * rows * out * width, 2 * out * width),
-    )(place, queries, mine, other, weight)
+        out_shape=[jax.ShapeDtypeStruct((rows, features), BF16)] * BREADTH,
+        compiler_params=params(48),
+        cost_estimate=cost(0, 0),
+    )(spot, queries, mine, other, weight)
 
 
 def mlp(index, base, terms, gain, weight, gate, up, down, hidden):
@@ -359,33 +416,43 @@
     source = (tp - steps) % TP
     target = (tp + steps) % TP
 
-    qkv_rows = jnp.concatenate([w_self_qkv[n] for n in range(3)], axis=1)
-    late_rows = jnp.concatenate([w_self_out.T, w_gate_up[0], w_gate_up[1], w_down.T], axis=1)
-    w_qkv = lax.all_gather(qkv_rows, SEQ, axis=0, tiled=True)
-    w_late = lax.all_gather(late_rows, SEQ, axis=0, tiled=True)
+    x = lax.axis_index("x")
+    late, *heads = pack(x.astype(jnp.int32)[None], w_self_qkv, w_self_out.T, w_gate_up, w_down.T)
+    quad = jnp.stack(
+        [heads[0]] + [shifted(heads[k], "x", k, BREADTH) for k in range(1, BREADTH)]
+    )
+    quad, late = lax.optimization_barrier((quad, late))
+    quads = lax.all_gather(quad, "z", axis=0)
+    w_late = lax.all_gather(late, SEQ, axis=0, tiled=True)
 
     latent_pieces = everyone(latent_in)
     prefix_pieces = everyone(prefix)
     queries, latents = gathered_matmul(source, latent_pieces, w_query[None], True)
+    queries, prefix_pieces = lax.optimization_barrier((queries, prefix_pieces))
+    spread = jnp.broadcast_to(queries, (chips, rows, width))
+    all_queries = lax.all_to_all(spread, ZX, 0, 0).reshape(chips * rows, width)
     (keyval,) = gathered_matmul(source, prefix_pieces, w_keyval, False)
     other_keyval = shifted(keyval, "core", 1, CORES)
-
-    spread = jnp.broadcast_to(queries, (chips, rows, width))
-    all_queries = lax.all_to_all(spread, ZX, 0, 0).reshape(chips * rows, width)
     pos = lax.dynamic_index_in_dim(
         latent_pos.reshape(chips, CORES, rows), core, axis=1, keepdims=False
     ).reshape(1, chips * rows)
     bases = jnp.stack([seq, chip * CORES + 1 - core]).astype(jnp.int32) * positions
     partial = cross_partial(bases, pos, all_queries, keyval, other_keyval)
     partial = lax.all_to_all(partial.reshape(chips, rows, -1), ZX, 0, 0)
+    spot = jnp.stack([lax.axis_index("z"), x, core]).astype(jnp.int32)
+    w_head = assemble(spot, quads, shifted(quads, "core", 1, CORES))
+    partial, w_head = lax.optimization_barrier((partial, w_head))
     cross_terms = combine_and_project(partial, w_cross_out)
 
-    first, qkv = norm_and_qkv(latents, everyone(cross_terms), attn_gain[None], w_qkv)
-    spread = jnp.broadcast_to(qkv[None, :, width:], (chips, rows, 2 * width))
-    mine = lax.all_to_all(spread, ZX, 0, 0).reshape(chips * rows, 2 * width)
+    first, normed = norm(latents, everyone(cross_terms), attn_gain[None])
+    group = [normed] + [shifted(normed, "x", k, BREADTH) for k in range(1, BREADTH)]
+    queries, keyval = project_head(group, w_head)
+    spread = jnp.broadcast_to(keyval, (DEPTH, *keyval.shape))
+    mine = lax.all_to_all(spread, "z", 0, 0).reshape(-1, keyval.shape[1])
     other = shifted(mine, "core", 1, CORES)
-    place = jnp.stack([seq, core]).astype(jnp.int32)
-    out_terms = self_attention(place, qkv[:, :width], mine, other, w_late, 0)
+    terms = self_attention(spot, rows, queries, mine, other, w_head)
+    terms = [terms[0]] + [shifted(terms[k], "x", BREADTH - k, BREADTH) for k in range(1, BREADTH)]
+    out_terms = sum(term.astype(F32) for term in terms).astype(BF16)
 
     own, *parts = mlp(
         target,
@@ -393,9 +460,9 @@
         everyone(out_terms),
         mlp_gain[None],
         w_late,
-        width,
-        width + hidden,
-        width + 2 * hidden,
+        0,
+        hidden,
+        2 * hidden,
         hidden,
     )
     sums = [parts[0]] + [shifted(parts[k], "tp", k, TP) for k in range(1, TP)]
@@ -404,7 +471,7 @@
 
 
 def solution(mesh):
-    z, x, core, y = 8, 4, 2, TP
+    z, x, core, y = DEPTH, BREADTH, CORES, TP
     grid = Mesh(mesh.devices.reshape(z, x, core, y), ("z", "x", "core", "tp"))
     return jax.shard_map(
         local,

time: 244 us -> 195 us (0.80)
  blocking collectives: 76.4 us -> 16.3 us
  waiting for transfers between devices: 75.1 us -> 58.1 us
  starting transfers between devices: 37.5 us -> 52.8 us
  Pallas kernels: 28.8 us -> 39.1 us
    all_to_all x2 -> x1, blocking collectives: 76.4 us -> 16.3 us  [local(): mine = lax.all_to_all(spread, 'z', 0, 0).reshape(-1, keyval.shape[1])]
    all_gather x2, waiting for transfers between devices: 52.1 us -> 0.02 us  [the longest x1 0.02 us: local(): quads = lax.all_gather(quad, 'z', axis=0)]
    all_to_all x0 -> x1, waiting for transfers between devices: none -> 15.4 us  [local(): partial = lax.all_to_all(partial.reshape(chips, rows, -1), ZX, 0, 0)]
    ppermute x17 -> x27, waiting for transfers between devices: 22.9 us -> 33.7 us  [shifted(): lax.ppermute(x, axis, [(i, (i + shift) % count) for i in range(count)])]
    ppermute x17 -> x27, starting transfers between devices: 27.4 us -> 37.2 us  [shifted(): lax.ppermute(x, axis, [(i, (i + shift) % count) for i in range(count)])]
    all_to_all x1, waiting for transfers between devices: 0.01 us -> 8.26 us  [local(): all_queries = lax.all_to_all(spread, ZX, 0, 0).reshape(chips * rows, width)]
    pallas_call x2, Pallas kernels: 4.04 us -> 10.2 us  [gathered_matmul(): pl.pallas_call(body, grid_spec=pltpu.PrefetchScalarGridSpec(num_scalar_pr...]
    all_to_all x0 -> x1, starting transfers between devices: none -> 4.96 us  [local(): partial = lax.all_to_all(partial.reshape(chips, rows, -1), ZX, 0, 0)]
  transfers between devices with their start and end apart: 20 -> 31, of which waited for: 12 -> 23; matrix products, arithmetic and copies ran while one was open for 2% -> 2% of each run, Pallas kernels for 7% -> 15%
where the time goes in v2:
time: 195 us; the launch traced here: 193 us
  waiting for transfers between devices  58.1 us (30%)
  starting transfers between devices  52.8 us (27%)
  Pallas kernels  39.1 us (20%)
  blocking collectives  16.3 us (8%)
  between operations  13.6 us (7%)
  local copies, waits for them, and re-layouts  8.02 us (4%)
  other arithmetic  4.64 us (2%)
    ppermute x27, starting transfers between devices, shifted(): lax.ppermute(x, axis, [(i, (i + shift) % count) for i in range(count)])  37.2 us
    ppermute x27, waiting for transfers between devices, shifted(): lax.ppermute(x, axis, [(i, (i + shift) % count) for i in range(count)])  33.7 us
    all_to_all x1, blocking collectives, local(): mine = lax.all_to_all(spread, 'z', 0, 0).reshape(-1, keyval.shape[1])  16.3 us
    all_to_all x1, waiting for transfers between devices, local(): partial = lax.all_to_all(partial.reshape(chips, rows, -1), ZX, 0, 0)  15.4 us
    all_to_all x1, starting transfers between devices, local(): all_queries = lax.all_to_all(spread, ZX, 0, 0).reshape(chips * rows, width)  10.6 us
    pallas_call x2, Pallas kernels, gathered_matmul(): pl.pallas_call(body, grid_spec=pltpu.PrefetchScalarGridSpec(num_scalar_pr...  10.2 us
    pallas_call x1, Pallas kernels, cross_partial(): pl.pallas_call(body, grid_spec=pltpu.PrefetchScalarGridSpec(num_scalar_pr...  8.55 us
    pallas_call x1, Pallas kernels, mlp(): pl.pallas_call(body, grid_spec=pltpu.PrefetchScalarGridSpec(num_scalar_pr...  8.31 us
  transfers between devices with their start and end apart: 31, of which 23 were waited for; matrix products, arithmetic and copies ran while one was open for 2% of the time, Pallas kernels for 15%

profile of v2, /device:TPU:8, one launch (start us, length us, event | category | flops | bytes accessed | tf_op | source)
XLA Modules:
  0.0 192.6 jit_solution(1889113492694164786)
XLA Ops:
  6.5 1.8 shard_map.121
  9.8 2.7 %collective-permute-start.8 = (bf16[32,512]{1,0:T(8,128)(2,1)}, bf16[32,512]{1,0:T(8,128)(2,1)S(1)}, u32[]{:S(2)}, u32[]{:S(2)}) collective-permute-start(bf16[32,512]{1,0:T(8,128)(2,1)} %get-tuple-element.43), channel_id=1, source_target_pairs={{0,16},{8,24},{16,0},{24,8},{1,17},{9,25},{17,1},{25,9},{2,18},{10... | collective-permute-start | bytes 98312 | tf_op jit(solution)/shard_map/ppermute | solution.py:27
  18.9 1.7 collective-permute-start.3
  21.5 2.4 %collective-permute-start.5 = (bf16[256,512]{1,0:T(8,128)(2,1)}, bf16[256,512]{1,0:T(8,128)(2,1)S(1)}, u32[]{:S(2)}, u32[]{:S(2)}) collective-permute-start(bf16[256,512]{1,0:T(8,128)(2,1)} %refs_0_.2), channel_id=1, source_target_pairs={{0,3},{1,0},{2,1},{3,2},{4,7},{5,4},{6,5},{7,6},{8,11},{9,8},{10,9... | collective-permute-start | bytes 786440 | tf_op jit(solution)/shard_map/ppermute | solution.py:27
  23.9 3.4 %collective-permute-start.1 = (bf16[16,512]{1,0:T(8,128)(2,1)}, bf16[16,512]{1,0:T(8,128)(2,1)S(1)}, u32[]{:S(2)}, u32[]{:S(2)}) collective-permute-start(bf16[16,512]{1,0:T(8,128)(2,1)} %refs_0_.1), channel_id=1, source_target_pairs={{0,2},{1,3},{2,0},{3,1},{4,6},{5,7},{6,4},{7,5},{8,10},{9,11},{10,... | collective-permute-start | bytes 49160 | tf_op jit(solution)/shard_map/ppermute | solution.py:27
  27.3 4.6 %collective-permute-done.refs_1_ = bf16[16,512]{1,0:T(8,128)(2,1)S(1)} collective-permute-done((bf16[16,512]{1,0:T(8,128)(2,1)}, bf16[16,512]{1,0:T(8,128)(2,1)S(1)}, u32[]{:S(2)}, u32[]{:S(2)}) %collective-permute-start) | collective-permute-done | bytes 16416 | tf_op jit(solution)/shard_map/ppermute | solution.py:27
  32.5 2.2 %collective-permute-done.1.refs_2_ = bf16[16,512]{1,0:T(8,128)(2,1)S(1)} collective-permute-done((bf16[16,512]{1,0:T(8,128)(2,1)}, bf16[16,512]{1,0:T(8,128)(2,1)S(1)}, u32[]{:S(2)}, u32[]{:S(2)}) %collective-permute-start.1) | collective-permute-done | bytes 16416 | tf_op jit(solution)/shard_map/ppermute | solution.py:27
  36.5 4.4 %shard_map.118 = (bf16[1,16,512]{2,1,0:T(8,128)(2,1)}, bf16[16,2048]{1,0:T(8,128)(2,1)}) custom-call(s32[4]{0:T(128)} %and_select_fusion.index_ref, bf16[16,512]{1,0:T(8,128)(2,1)} %refs_0_.1, bf16[16,512]{1,0:T(8,128)(2,1)} %copy-done.15, bf16[16,512]{1,0:T(8,128)(2,1)} %copy-done.16, bf16[16,512]{1,0:T(8,128)(2,1)} %copy-done.17, ...), custom_call_target="tpu_custom_call" | custom-call | flops 1 | bytes 1 | tf_op jit(solution)/shard_map/pallas_call | solution.py:83
  40.9 1.6 broadcast_in_dim.22
  42.5 10.6 %all-to-all-start = ((bf16[32,16,512]{2,1,0:T(8,128)(2,1)}), bf16[32,16,512]{2,1,0:T(8,128)(2,1)S(1)}, u32[]{:S(2)}, u32[]{:S(2)}) async-start(bf16[32,16,512]{2,1,0:T(8,128)(2,1)} %broadcast_in_dim.22), calls=%async_computation | async-start | bytes 1048576 | tf_op jit(solution)/shard_map/all_to_all | solution.py:433
  53.2 5.8 %shard_map.119.mine_ref = bf16[2,256,512]{2,1,0:T(8,128)(2,1)} custom-call(s32[4]{0:T(128)} %and_select_fusion.index_ref, bf16[256,512]{1,0:T(8,128)(2,1)} %refs_0_.2, bf16[256,512]{1,0:T(8,128)(2,1)} %copy-done.6, bf16[256,512]{1,0:T(8,128)(2,1)} %copy-done.7, bf16[256,512]{1,0:T(8,128)(2,1)} %copy-done.8, bf16[2,2048,512]{2,1,0:T(8,128)(2,1)} %refs_4_.1), custom_call_target="tpu_custom_call" | custom-call | flops 1 | bytes 1 | tf_op jit(solution)/shard_map/pallas_call | solution.py:83
  61.2 8.3 %all-to-all-done = bf16[32,16,512]{2,1,0:T(8,128)(2,1)S(1)} async-done(((bf16[32,16,512]{2,1,0:T(8,128)(2,1)}), bf16[32,16,512]{2,1,0:T(8,128)(2,1)S(1)}, u32[]{:S(2)}, u32[]{:S(2)}) %all-to-all-start) | async-done | bytes 524320 | tf_op jit(solution)/shard_map/all_to_all | solution.py:433
  70.3 8.5 %shard_map.120 = bf16[512,640]{1,0:T(8,128)(2,1)} custom-call(s32[2]{0:T(128)} %add_multiply_fusion.base_ref, s32[1,512]{1,0:T(1,128)} %reshape.17.pos_ref, bf16[512,512]{1,0:T(8,128)(2,1)} %bitcast.25, bf16[2,256,512]{2,1,0:T(8,128)(2,1)} %shard_map.119.mine_ref, bf16[2,256,512]{2,1,0:T(8,128)(2,1)} %copy-done.4), custom_call_target="tpu_custom_call" | custom-call | flops 1 | bytes 1 | tf_op jit(solution)/shard_map/pallas_call | solution.py:132
  78.8 5.0 %all-to-all-start.1 = ((bf16[32,16,640]{2,1,0:T(8,128)(2,1)}), bf16[32,16,640]{2,1,0:T(8,128)(2,1)S(1)}, u32[]{:S(2)}, u32[]{:S(2)}) async-start(bf16[32,16,640]{2,1,0:T(8,128)(2,1)} %bitcast.23), calls=%async_computation.1 | async-start | bytes 1310720 | tf_op jit(solution)/shard_map/all_to_all | solution.py:441
  84.2 2.8 %collective-permute-done.10.other_ref = bf16[8,4,32,512]{3,2,1,0:T(8,128)(2,1)S(1)} collective-permute-done((bf16[8,4,32,512]{3,2,1,0:T(8,128)(2,1)}, bf16[8,4,32,512]{3,2,1,0:T(8,128)(2,1)S(1)}, u32[]{:S(2)}, u32[]{:S(2)}) %collective-permute-start.10) | collective-permute-done | bytes 1048608 | tf_op jit(solution)/shard_map/ppermute | solution.py:27
  88.2 3.4 %shard_map.122.refs_4_.weight_ref = bf16[2048,512]{1,0:T(8,128)(2,1)S(1)} custom-call(s32[3]{0:T(128)S(1)} %pad_add_fusion.spot_ref, bf16[8,4,32,512]{3,2,1,0:T(8,128)(2,1)S(1)} %bitcast.20, bf16[8,4,32,512]{3,2,1,0:T(8,128)(2,1)S(1)} %collective-permute-done.10.other_ref), custom_call_target="tpu_custom_call" | custom-call | flops 1 | bytes 1 | tf_op jit(solution)/shard_map/pallas_call | solution.py:246
  91.6 15.4 %all-to-all-done.1.x_ref = bf16[32,16,640]{2,1,0:T(8,128)(2,1)S(1)} async-done(((bf16[32,16,640]{2,1,0:T(8,128)(2,1)}), bf16[32,16,640]{2,1,0:T(8,128)(2,1)S(1)}, u32[]{:S(2)}, u32[]{:S(2)}) %all-to-all-start.1) | async-done | bytes 655392 | tf_op jit(solution)/shard_map/all_to_all | solution.py:441
  107.8 3.4 %shard_map.123.a = bf16[16,2048]{1,0:T(8,128)(2,1)} custom-call(bf16[32,16,640]{2,1,0:T(8,128)(2,1)} %copy-done.2, bf16[512,2048]{1,0:T(8,128)(2,1)} %w_ref.1), custom_call_target="tpu_custom_call" | custom-call | flops 1 | bytes 1 | tf_op jit(solution)/shard_map/pallas_call | solution.py:172
  113.7 2.6 %collective-permute-start.13 = (bf16[16,2048]{1,0:T(8,128)(2,1)}, bf16[16,2048]{1,0:T(8,128)(2,1)S(1)}, u32[]{:S(2)}, u32[]{:S(2)}) collective-permute-start(bf16[16,2048]{1,0:T(8,128)(2,1)} %shard_map.123.a), channel_id=1, source_target_pairs={{0,3},{1,0},{2,1},{3,2},{4,7},{5,4},{6,5},{7,6},{8,11},{9,8},{10,9... | collective-permute-start | bytes 196616 | tf_op jit(solution)/shard_map/ppermute | solution.py:27
  116.4 2.0 %collective-permute-done.12.c = bf16[16,2048]{1,0:T(8,128)(2,1)S(1)} collective-permute-done((bf16[16,2048]{1,0:T(8,128)(2,1)}, bf16[16,2048]{1,0:T(8,128)(2,1)S(1)}, u32[]{:S(2)}, u32[]{:S(2)}) %collective-permute-start.12) | collective-permute-done | bytes 65568 | tf_op jit(solution)/shard_map/ppermute | solution.py:27
  119.5 1.7 shard_map.124
  121.9 2.7 %collective-permute-start.15 = (bf16[16,2048]{1,0:T(8,128)(2,1)}, bf16[16,2048]{1,0:T(8,128)(2,1)S(1)}, u32[]{:S(2)}, u32[]{:S(2)}) collective-permute-start(bf16[16,2048]{1,0:T(8,128)(2,1)} %get-tuple-element.49.refs_0_), channel_id=1, source_target_pairs={{0,16},{8,24},{16,0},{24,8},{1,17},{9,25},{17,1},{25,9},{2,18},{10... | collective-permute-start | bytes 196616 | tf_op jit(solution)/shard_map/ppermute | solution.py:27
  126.1 2.2 %collective-permute-done.14.refs_1_ = bf16[16,2048]{1,0:T(8,128)(2,1)S(1)} collective-permute-done((bf16[16,2048]{1,0:T(8,128)(2,1)}, bf16[16,2048]{1,0:T(8,128)(2,1)S(1)}, u32[]{:S(2)}, u32[]{:S(2)}) %collective-permute-start.14) | collective-permute-done | bytes 65568 | tf_op jit(solution)/shard_map/ppermute | solution.py:27
  128.3 2.2 %collective-permute-done.15.refs_2_ = bf16[16,2048]{1,0:T(8,128)(2,1)S(1)} collective-permute-done((bf16[16,2048]{1,0:T(8,128)(2,1)}, bf16[16,2048]{1,0:T(8,128)(2,1)S(1)}, u32[]{:S(2)}, u32[]{:S(2)}) %collective-permute-start.15) | collective-permute-done | bytes 65568 | tf_op jit(solution)/shard_map/ppermute | solution.py:27
  132.6 16.3 %all_to_all.15 = bf16[8,64,256]{2,1,0:T(8,128)(2,1)S(1)} all-to-all(bf16[8,64,256]{2,1,0:T(8,128)(2,1)S(1)} %broadcast_in_dim.24), channel_id=1, replica_groups=mesh['z'=8,'x'=4,'core'=2,'tp'=4] {'z'}, dimensions={0} | all-to-all | bytes 524288 | tf_op jit(solution)/shard_map/all_to_all | solution.py:451
  151.8 1.9 collective-permute-start.18
  155.0 1.8 collective-permute-done.18
  156.8 2.9 %collective-permute-done.19 = bf16[16,2048]{1,0:T(8,128)(2,1)S(1)} collective-permute-done((bf16[16,2048]{1,0:T(8,128)(2,1)S(1)}, bf16[16,2048]{1,0:T(8,128)(2,1)S(1)}, u32[]{:S(2)}, u32[]{:S(2)}) %collective-permute-start.19) | collective-permute-done | bytes 65568 | tf_op jit(solution)/shard_map/ppermute | solution.py:27
  162.0 2.7 %collective-permute-start.22 = (bf16[16,2048]{1,0:T(8,128)(2,1)S(1)}, bf16[16,2048]{1,0:T(8,128)(2,1)S(1)}, u32[]{:S(2)}, u32[]{:S(2)}) collective-permute-start(bf16[16,2048]{1,0:T(8,128)(2,1)S(1)} %add_convert_fusion.a), channel_id=1, source_target_pairs={{0,2},{1,3},{2,0},{3,1},{4,6},{5,7},{6,4},{7,5},{8,10},{9,11},{10,... | collective-permute-start | bytes 196616 | tf_op jit(solution)/shard_map/ppermute | solution.py:27
  169.5 8.3 %shard_map.127 = (bf16[16,512]{1,0:T(8,128)(2,1)}, bf16[16,512]{1,0:T(8,128)(2,1)}, bf16[16,512]{1,0:T(8,128)(2,1)}, bf16[16,512]{1,0:T(8,128)(2,1)}, bf16[16,512]{1,0:T(8,128)(2,1)}) custom-call(s32[4]{0:T(128)} %and_select_fusion.1.index_ref, bf16[16,2048]{1,0:T(8,128)(2,1)} %get-tuple-element.48.base_ref, bf16[16,2048]{1,0:T(8,128)(2,1)} %copy-done.5, ...), custom_call_target="tpu_custom_call" | custom-call | flops 1 | bytes 1 | tf_op jit(solution)/shard_map/pallas_call | solution.py:372
  177.8 2.3 %collective-permute-start.24 = (bf16[16,512]{1,0:T(8,128)(2,1)}, bf16[16,512]{1,0:T(8,128)(2,1)S(1)}, u32[]{:S(2)}, u32[]{:S(2)}) collective-permute-start(bf16[16,512]{1,0:T(8,128)(2,1)} %get-tuple-element.60), channel_id=1, source_target_pairs={{0,2},{1,3},{2,0},{3,1},{4,6},{5,7},{6,4},{7,5},{8,10},{9,11},{10,... | collective-permute-start | bytes 49160 | tf_op jit(solution)/shard_map/ppermute | solution.py:27
  180.5 1.7 collective-permute-start.26
  (93 shorter events, 39.6 us)
Async XLA Ops:
  6.5 77.3 %all-gather.6.cloned.1.call-start = ((), (), s32[]{:S(2)}) async-start(), calls=%async_computation.4 | async-start | bytes 1179648 | tf_op jit(solution)/shard_map/all_gather | solution.py:425
  8.3 5.7 %collective-permute-start.7 = (bf16[32,512]{1,0:T(8,128)(2,1)}, bf16[32,512]{1,0:T(8,128)(2,1)S(1)}, u32[]{:S(2)}, u32[]{:S(2)}) collective-permute-start(bf16[32,512]{1,0:T(8,128)(2,1)} %get-tuple-element.42), channel_id=1, source_target_pairs={{0,8},{8,16},{16,24},{24,0},{1,9},{9,17},{17,25},{25,1},{2,10},{10... | collective-permute-start | bytes 98312 | tf_op jit(solution)/shard_map/ppermute | solution.py:27
  9.8 5.6 %collective-permute-start.8 = (bf16[32,512]{1,0:T(8,128)(2,1)}, bf16[32,512]{1,0:T(8,128)(2,1)S(1)}, u32[]{:S(2)}, u32[]{:S(2)}) collective-permute-start(bf16[32,512]{1,0:T(8,128)(2,1)} %get-tuple-element.43), channel_id=1, source_target_pairs={{0,16},{8,24},{16,0},{24,8},{1,17},{9,25},{17,1},{25,9},{2,18},{10... | collective-permute-start | bytes 98312 | tf_op jit(solution)/shard_map/ppermute | solution.py:27
  12.5 4.1 %collective-permute-start.9 = (bf16[32,512]{1,0:T(8,128)(2,1)}, bf16[32,512]{1,0:T(8,128)(2,1)S(1)}, u32[]{:S(2)}, u32[]{:S(2)}) collective-permute-start(bf16[32,512]{1,0:T(8,128)(2,1)} %get-tuple-element.44), channel_id=1, source_target_pairs={{0,24},{8,0},{16,8},{24,16},{1,25},{9,1},{17,9},{25,17},{2,26},{10... | collective-permute-start | bytes 98312 | tf_op jit(solution)/shard_map/ppermute | solution.py:27
  18.1 150.8 %all-gather.4.cloned.1.call-start = ((), (), s32[]{:S(2)}) async-start(), calls=%async_computation.3 | async-start | bytes 12779520 | tf_op jit(solution)/shard_map/all_gather | solution.py:426
  18.9 22.0 %collective-permute-start.3 = (bf16[256,512]{1,0:T(8,128)(2,1)}, bf16[256,512]{1,0:T(8,128)(2,1)S(1)}, u32[]{:S(2)}, u32[]{:S(2)}) collective-permute-start(bf16[256,512]{1,0:T(8,128)(2,1)} %refs_0_.2), channel_id=1, source_target_pairs={{0,1},{1,2},{2,3},{3,0},{4,5},{5,6},{6,7},{7,4},{8,9},{9,10},{10,1... | collective-permute-start | bytes 786440 | tf_op jit(solution)/shard_map/ppermute | solution.py:27
  20.5 20.4 %collective-permute-start.4 = (bf16[256,512]{1,0:T(8,128)(2,1)}, bf16[256,512]{1,0:T(8,128)(2,1)S(1)}, u32[]{:S(2)}, u32[]{:S(2)}) collective-permute-start(bf16[256,512]{1,0:T(8,128)(2,1)} %refs_0_.2), channel_id=1, source_target_pairs={{0,2},{1,3},{2,0},{3,1},{4,6},{5,7},{6,4},{7,5},{8,10},{9,11},{10,... | collective-permute-start | bytes 786440 | tf_op jit(solution)/shard_map/ppermute | solution.py:27
  21.5 19.5 %collective-permute-start.5 = (bf16[256,512]{1,0:T(8,128)(2,1)}, bf16[256,512]{1,0:T(8,128)(2,1)S(1)}, u32[]{:S(2)}, u32[]{:S(2)}) collective-permute-start(bf16[256,512]{1,0:T(8,128)(2,1)} %refs_0_.2), channel_id=1, source_target_pairs={{0,3},{1,0},{2,1},{3,2},{4,7},{5,4},{6,5},{7,6},{8,11},{9,8},{10,9... | collective-permute-start | bytes 786440 | tf_op jit(solution)/shard_map/ppermute | solution.py:27
  23.9 8.1 %collective-permute-start = (bf16[16,512]{1,0:T(8,128)(2,1)}, bf16[16,512]{1,0:T(8,128)(2,1)S(1)}, u32[]{:S(2)}, u32[]{:S(2)}) collective-permute-start(bf16[16,512]{1,0:T(8,128)(2,1)} %refs_0_.1), channel_id=1, source_target_pairs={{0,1},{1,2},{2,3},{3,0},{4,5},{5,6},{6,7},{7,4},{8,9},{9,10},{10,1... | collective-permute-start | bytes 49160 | tf_op jit(solution)/shard_map/ppermute | solution.py:27
  23.9 10.9 %collective-permute-start.1 = (bf16[16,512]{1,0:T(8,128)(2,1)}, bf16[16,512]{1,0:T(8,128)(2,1)S(1)}, u32[]{:S(2)}, u32[]{:S(2)}) collective-permute-start(bf16[16,512]{1,0:T(8,128)(2,1)} %refs_0_.1), channel_id=1, source_target_pairs={{0,2},{1,3},{2,0},{3,1},{4,6},{5,7},{6,4},{7,5},{8,10},{9,11},{10,... | collective-permute-start | bytes 49160 | tf_op jit(solution)/shard_map/ppermute | solution.py:27
  31.9 3.9 %collective-permute-start.2 = (bf16[16,512]{1,0:T(8,128)(2,1)}, bf16[16,512]{1,0:T(8,128)(2,1)S(1)}, u32[]{:S(2)}, u32[]{:S(2)}) collective-permute-start(bf16[16,512]{1,0:T(8,128)(2,1)} %refs_0_.1), channel_id=1, source_target_pairs={{0,3},{1,0},{2,1},{3,2},{4,7},{5,4},{6,5},{7,6},{8,11},{9,8},{10,9... | collective-permute-start | bytes 49160 | tf_op jit(solution)/shard_map/ppermute | solution.py:27
  40.9 12.3 %copy-start.6 = (bf16[256,512]{1,0:T(8,128)(2,1)}, bf16[256,512]{1,0:T(8,128)(2,1)S(1)}, u32[]{:S(2)}) copy-start(bf16[256,512]{1,0:T(8,128)(2,1)S(1)} %collective-permute-done.3.refs_1_) | copy-start | bytes 786436
  42.5 26.9 %all-to-all-start = ((bf16[32,16,512]{2,1,0:T(8,128)(2,1)}), bf16[32,16,512]{2,1,0:T(8,128)(2,1)S(1)}, u32[]{:S(2)}, u32[]{:S(2)}) async-start(bf16[32,16,512]{2,1,0:T(8,128)(2,1)} %broadcast_in_dim.22), calls=%async_computation | async-start | bytes 1048576 | tf_op jit(solution)/shard_map/all_to_all | solution.py:433
  59.1 2.1 %collective-permute-start.6 = (bf16[2,256,512]{2,1,0:T(8,128)(2,1)}, bf16[2,256,512]{2,1,0:T(8,128)(2,1)S(1)}, u32[]{:S(2)}, u32[]{:S(2)}) collective-permute-start(bf16[2,256,512]{2,1,0:T(8,128)(2,1)} %shard_map.119.mine_ref), channel_id=1, source_target_pairs={{0,4},{4,0},{1,5},{5,1},{2,6},{6,2},{3,7},{7,3},{8,12},{12,8},{9,1... | collective-permute-start | bytes 1572872 | tf_op jit(solution)/shard_map/ppermute | solution.py:27
  78.8 28.2 %all-to-all-start.1 = ((bf16[32,16,640]{2,1,0:T(8,128)(2,1)}), bf16[32,16,640]{2,1,0:T(8,128)(2,1)S(1)}, u32[]{:S(2)}, u32[]{:S(2)}) async-start(bf16[32,16,640]{2,1,0:T(8,128)(2,1)} %bitcast.23), calls=%async_computation.1 | async-start | bytes 1310720 | tf_op jit(solution)/shard_map/all_to_all | solution.py:441
  83.8 3.1 %collective-permute-start.10 = (bf16[8,4,32,512]{3,2,1,0:T(8,128)(2,1)}, bf16[8,4,32,512]{3,2,1,0:T(8,128)(2,1)S(1)}, u32[]{:S(2)}, u32[]{:S(2)}) collective-permute-start(bf16[8,4,32,512]{3,2,1,0:T(8,128)(2,1)} %bitcast.19), channel_id=1, source_target_pairs={{0,4},{4,0},{1,5},{5,1},{2,6},{6,2},{3,7},{7,3},{8,12},{12,8},{9,1... | collective-permute-start | bytes 3145736 | tf_op jit(solution)/shard_map/ppermute | solution.py:27
  111.2 5.2 %collective-permute-start.11 = (bf16[16,2048]{1,0:T(8,128)(2,1)}, bf16[16,2048]{1,0:T(8,128)(2,1)S(1)}, u32[]{:S(2)}, u32[]{:S(2)}) collective-permute-start(bf16[16,2048]{1,0:T(8,128)(2,1)} %shard_map.123.a), channel_id=1, source_target_pairs={{0,1},{1,2},{2,3},{3,0},{4,5},{5,6},{6,7},{7,4},{8,9},{9,10},{10,1... | collective-permute-start | bytes 196616 | tf_op jit(solution)/shard_map/ppermute | solution.py:27
  112.3 6.1 %collective-permute-start.12 = (bf16[16,2048]{1,0:T(8,128)(2,1)}, bf16[16,2048]{1,0:T(8,128)(2,1)S(1)}, u32[]{:S(2)}, u32[]{:S(2)}) collective-permute-start(bf16[16,2048]{1,0:T(8,128)(2,1)} %shard_map.123.a), channel_id=1, source_target_pairs={{0,2},{1,3},{2,0},{3,1},{4,6},{5,7},{6,4},{7,5},{8,10},{9,11},{10,... | collective-permute-start | bytes 196616 | tf_op jit(solution)/shard_map/ppermute | solution.py:27
  113.7 5.2 %collective-permute-start.13 = (bf16[16,2048]{1,0:T(8,128)(2,1)}, bf16[16,2048]{1,0:T(8,128)(2,1)S(1)}, u32[]{:S(2)}, u32[]{:S(2)}) collective-permute-start(bf16[16,2048]{1,0:T(8,128)(2,1)} %shard_map.123.a), channel_id=1, source_target_pairs={{0,3},{1,0},{2,1},{3,2},{4,7},{5,4},{6,5},{7,6},{8,11},{9,8},{10,9... | collective-permute-start | bytes 196616 | tf_op jit(solution)/shard_map/ppermute | solution.py:27
  121.3 7.1 %collective-permute-start.14 = (bf16[16,2048]{1,0:T(8,128)(2,1)}, bf16[16,2048]{1,0:T(8,128)(2,1)S(1)}, u32[]{:S(2)}, u32[]{:S(2)}) collective-permute-start(bf16[16,2048]{1,0:T(8,128)(2,1)} %get-tuple-element.49.refs_0_), channel_id=1, source_target_pairs={{0,8},{8,16},{16,24},{24,0},{1,9},{9,17},{17,25},{25,1},{2,10},{10... | collective-permute-start | bytes 196616 | tf_op jit(solution)/shard_map/ppermute | solution.py:27
  121.9 8.6 %collective-permute-start.15 = (bf16[16,2048]{1,0:T(8,128)(2,1)}, bf16[16,2048]{1,0:T(8,128)(2,1)S(1)}, u32[]{:S(2)}, u32[]{:S(2)}) collective-permute-start(bf16[16,2048]{1,0:T(8,128)(2,1)} %get-tuple-element.49.refs_0_), channel_id=1, source_target_pairs={{0,16},{8,24},{16,0},{24,8},{1,17},{9,25},{17,1},{25,9},{2,18},{10... | collective-permute-start | bytes 196616 | tf_op jit(solution)/shard_map/ppermute | solution.py:27
  124.6 6.7 %collective-permute-start.16 = (bf16[16,2048]{1,0:T(8,128)(2,1)}, bf16[16,2048]{1,0:T(8,128)(2,1)S(1)}, u32[]{:S(2)}, u32[]{:S(2)}) collective-permute-start(bf16[16,2048]{1,0:T(8,128)(2,1)} %get-tuple-element.49.refs_0_), channel_id=1, source_target_pairs={{0,24},{8,0},{16,8},{24,16},{1,25},{9,1},{17,9},{25,17},{2,26},{10... | collective-permute-start | bytes 196616 | tf_op jit(solution)/shard_map/ppermute | solution.py:27
  148.9 1.5 collective-permute-start.17
  151.8 5.0 %collective-permute-start.18 = (bf16[16,2048]{1,0:T(8,128)(2,1)S(1)}, bf16[16,2048]{1,0:T(8,128)(2,1)S(1)}, u32[]{:S(2)}, u32[]{:S(2)}) collective-permute-start(bf16[16,2048]{1,0:T(8,128)(2,1)S(1)} %get-tuple-element.54), channel_id=1, source_target_pairs={{0,24},{8,0},{16,8},{24,16},{1,25},{9,1},{17,9},{25,17},{2,26},{10... | collective-permute-start | bytes 196616 | tf_op jit(solution)/shard_map/ppermute | solution.py:27
  153.6 6.1 %collective-permute-start.19 = (bf16[16,2048]{1,0:T(8,128)(2,1)S(1)}, bf16[16,2048]{1,0:T(8,128)(2,1)S(1)}, u32[]{:S(2)}, u32[]{:S(2)}) collective-permute-start(bf16[16,2048]{1,0:T(8,128)(2,1)S(1)} %get-tuple-element.55), channel_id=1, source_target_pairs={{0,16},{8,24},{16,0},{24,8},{1,17},{9,25},{17,1},{25,9},{2,18},{10... | collective-permute-start | bytes 196616 | tf_op jit(solution)/shard_map/ppermute | solution.py:27
  154.2 6.2 %collective-permute-start.20 = (bf16[16,2048]{1,0:T(8,128)(2,1)S(1)}, bf16[16,2048]{1,0:T(8,128)(2,1)S(1)}, u32[]{:S(2)}, u32[]{:S(2)}) collective-permute-start(bf16[16,2048]{1,0:T(8,128)(2,1)S(1)} %get-tuple-element.56), channel_id=1, source_target_pairs={{0,8},{8,16},{16,24},{24,0},{1,9},{9,17},{17,25},{25,1},{2,10},{10... | collective-permute-start | bytes 196616 | tf_op jit(solution)/shard_map/ppermute | solution.py:27
  160.5 5.8 %collective-permute-start.21 = (bf16[16,2048]{1,0:T(8,128)(2,1)S(1)}, bf16[16,2048]{1,0:T(8,128)(2,1)S(1)}, u32[]{:S(2)}, u32[]{:S(2)}) collective-permute-start(bf16[16,2048]{1,0:T(8,128)(2,1)S(1)} %add_convert_fusion.a), channel_id=1, source_target_pairs={{0,1},{1,2},{2,3},{3,0},{4,5},{5,6},{6,7},{7,4},{8,9},{9,10},{10,1... | collective-permute-start | bytes 196616 | tf_op jit(solution)/shard_map/ppermute | solution.py:27
  162.0 5.8 %collective-permute-start.22 = (bf16[16,2048]{1,0:T(8,128)(2,1)S(1)}, bf16[16,2048]{1,0:T(8,128)(2,1)S(1)}, u32[]{:S(2)}, u32[]{:S(2)}) collective-permute-start(bf16[16,2048]{1,0:T(8,128)(2,1)S(1)} %add_convert_fusion.a), channel_id=1, source_target_pairs={{0,2},{1,3},{2,0},{3,1},{4,6},{5,7},{6,4},{7,5},{8,10},{9,11},{10,... | collective-permute-start | bytes 196616 | tf_op jit(solution)/shard_map/ppermute | solution.py:27
  164.6 4.3 %collective-permute-start.23 = (bf16[16,2048]{1,0:T(8,128)(2,1)S(1)}, bf16[16,2048]{1,0:T(8,128)(2,1)S(1)}, u32[]{:S(2)}, u32[]{:S(2)}) collective-permute-start(bf16[16,2048]{1,0:T(8,128)(2,1)S(1)} %add_convert_fusion.a), channel_id=1, source_target_pairs={{0,3},{1,0},{2,1},{3,2},{4,7},{5,4},{6,5},{7,6},{8,11},{9,8},{10,9... | collective-permute-start | bytes 196616 | tf_op jit(solution)/shard_map/ppermute | solution.py:27
  177.8 5.5 %collective-permute-start.24 = (bf16[16,512]{1,0:T(8,128)(2,1)}, bf16[16,512]{1,0:T(8,128)(2,1)S(1)}, u32[]{:S(2)}, u32[]{:S(2)}) collective-permute-start(bf16[16,512]{1,0:T(8,128)(2,1)} %get-tuple-element.60), channel_id=1, source_target_pairs={{0,2},{1,3},{2,0},{3,1},{4,6},{5,7},{6,4},{7,5},{8,10},{9,11},{10,... | collective-permute-start | bytes 49160 | tf_op jit(solution)/shard_map/ppermute | solution.py:27
  180.1 3.9 %collective-permute-start.25 = (bf16[16,512]{1,0:T(8,128)(2,1)}, bf16[16,512]{1,0:T(8,128)(2,1)S(1)}, u32[]{:S(2)}, u32[]{:S(2)}) collective-permute-start(bf16[16,512]{1,0:T(8,128)(2,1)} %get-tuple-element.61), channel_id=1, source_target_pairs={{0,1},{1,2},{2,3},{3,0},{4,5},{5,6},{6,7},{7,4},{8,9},{9,10},{10,1... | collective-permute-start | bytes 49160 | tf_op jit(solution)/shard_map/ppermute | solution.py:27
  180.5 3.9 %collective-permute-start.26 = (bf16[16,512]{1,0:T(8,128)(2,1)}, bf16[16,512]{1,0:T(8,128)(2,1)S(1)}, u32[]{:S(2)}, u32[]{:S(2)}) collective-permute-start(bf16[16,512]{1,0:T(8,128)(2,1)} %get-tuple-element.62), channel_id=1, source_target_pairs={{0,3},{1,0},{2,1},{3,2},{4,7},{5,4},{6,5},{7,6},{8,11},{9,8},{10,9... | collective-permute-start | bytes 49160 | tf_op jit(solution)/shard_map/ppermute | solution.py:27
  (18 other events, 64.8 us)
Sparse Core Ops, SparseCore 0:
  18.2 42.6 all-gather.5
  63.7 99.9 all-gather.3

commit v3 on v2

--- a/solution.py
+++ b/solution.py
@@ -44,7 +44,7 @@
     return one, two, three
 
 
-def params(mib=58):
+def params(mib=48):
     return pltpu.CompilerParams(vmem_limit_bytes=mib * 1024 * 1024)
 
 
@@ -91,7 +91,7 @@
             scratch_shapes=[pltpu.VMEM((groups, rows, cols), F32)],
         ),
         out_shape=out_shape,
-        compiler_params=params(),
+        compiler_params=params(48 if keep else 58),
         cost_estimate=cost(2 * rows * weight.size, 2 * weight.size),
     )(index, *pieces, weight)
 
@@ -204,54 +204,59 @@
 
 def pack(x, w_self_qkv, w_self_out, w_gate_up, w_down):
     groups, depth, _ = w_self_qkv.shape
-    hidden = w_down.shape[1]
-
-    def body(x_ref, qkv_ref, out_ref, gate_up_ref, down_ref, packed_ref, *head_refs):
-        packed_ref[:, :hidden] = gate_up_ref[0]
-        packed_ref[:, hidden : 2 * hidden] = gate_up_ref[1]
-        packed_ref[:, 2 * hidden :] = down_ref[...]
-        for k, ref in enumerate(head_refs):
-            head = lax.rem(x_ref[0] + k, BREADTH)
-            columns = pl.ds(pl.multiple_of(head * HD, HD), HD)
-            for g in range(groups):
-                ref[:, g * HD : (g + 1) * HD] = qkv_ref[g, :, columns]
-            ref[:, groups * HD :] = out_ref[:, columns]
-
-    part = jax.ShapeDtypeStruct((depth, (groups + 1) * HD), BF16)
+    share = w_down.shape[1] // BREADTH
+
+    def body(x_ref, qkv_ref, out_ref, gate_up_ref, down_ref, *refs):
+        for k, ref in enumerate(refs):
+            chip = lax.rem(x_ref[0] + k, BREADTH)
+            head = pl.ds(pl.multiple_of(chip * HD, HD), HD)
+            units = pl.ds(pl.multiple_of(chip * share, share), share)
+            parts = [qkv_ref[g, :, head] for g in range(groups)] + [out_ref[:, head]]
+            parts += [gate_up_ref[g, :, units] for g in range(2)] + [down_ref[:, units]]
+            ref[...] = jnp.concatenate(parts, axis=1)
+
     vmem = pl.BlockSpec(memory_space=pltpu.VMEM)
     return pl.pallas_call(
         body,
         in_specs=[pl.BlockSpec(memory_space=pltpu.SMEM)] + [vmem] * 4,
-        out_specs=[vmem] * (1 + BREADTH),
-        out_shape=[jax.ShapeDtypeStruct((depth, 3 * hidden), BF16)] + [part] * BREADTH,
+        out_specs=[vmem] * BREADTH,
+        out_shape=[jax.ShapeDtypeStruct((depth, 4 * HD + 3 * share), BF16)] * BREADTH,
         cost_estimate=cost(0, 0),
     )(x, w_self_qkv, w_self_out, w_gate_up, w_down)
 
 
-def assemble(spot, mine, other):
-    _, _, depth, cols = mine.shape
-
-    def body(spot_ref, mine_ref, other_ref, out_ref, sem):
-        x, core = spot_ref[1], spot_ref[2]
-        for ref, at_core in ((mine_ref, core), (other_ref, 1 - core)):
-            for z in range(DEPTH):
+def assemble(spot, rows, splits):
+    depth = rows.shape[3]
+
+    def body(spot_ref, rows_ref, *refs):
+        sems = refs[len(splits)]
+        for z in range(DEPTH):
+            for core in range(CORES):
                 for k in range(BREADTH):
-                    at_x = lax.rem(x + BREADTH - k, BREADTH)
-                    place = ((z * BREADTH + at_x) * CORES + at_core) * depth
-                    rows = pl.ds(pl.multiple_of(place, depth), depth)
-                    pltpu.make_async_copy(ref.at[z, k], out_ref.at[rows], sem).start()
-        pltpu.make_async_copy(out_ref, out_ref, sem).wait()
-
-    anywhere = pl.BlockSpec(memory_space=pl.ANY)
-    return pl.pallas_call(
-        body,
-        in_specs=[pl.BlockSpec(memory_space=pltpu.SMEM), anywhere, anywhere],
-        out_specs=pl.BlockSpec(memory_space=pltpu.VMEM),
-        out_shape=jax.ShapeDtypeStruct((DEPTH * BREADTH * CORES * depth, cols), BF16),
-        scratch_shapes=[pltpu.SemaphoreType.DMA],
-        compiler_params=params(48),
-        cost_estimate=cost(0, 0),
-    )(spot, mine, other)
+                    at_x = lax.rem(spot_ref[1] + BREADTH - k, BREADTH)
+                    place = ((z * BREADTH + at_x) * CORES + core) * depth
+                    at = pl.ds(pl.multiple_of(place, depth), depth)
+                    first = 0
+                    for n, width in enumerate(splits):
+                        pltpu.make_async_copy(
+                            rows_ref.at[z, core, k, :, pl.ds(first, width)],
+                            refs[n].at[at],
+                            sems.at[n],
+                        ).start()
+                        first += width
+        for n in range(len(splits)):
+            pltpu.make_async_copy(refs[n], refs[n], sems.at[n]).wait()
+
+    count = DEPTH * BREADTH * CORES * depth
+    return pl.pallas_call(
+        body,
+        in_specs=[pl.BlockSpec(memory_space=pltpu.SMEM), pl.BlockSpec(memory_space=pl.ANY)],
+        out_specs=[pl.BlockSpec(memory_space=pltpu.VMEM)] * len(splits),
+        out_shape=[jax.ShapeDtypeStruct((count, width), BF16) for width in splits],
+        scratch_shapes=[pltpu.SemaphoreType.DMA((len(splits),))],
+        compiler_params=params(58),
+        cost_estimate=cost(0, 0),
+    )(spot, rows)
 
 
 def project_head(normed, weight):
@@ -321,7 +326,7 @@
             grid=(1,),
             in_specs=[whole(total_rows, width)]
             + [whole(count, 2 * width)] * CORES
-            + [pl.BlockSpec((features, width), lambda i, p: (0, 3))],
+            + [whole(features, width)],
             out_specs=[whole(rows, features)] * BREADTH,
         ),
         out_shape=[jax.ShapeDtypeStruct((rows, features), BF16)] * BREADTH,
@@ -330,63 +335,62 @@
     )(spot, queries, mine, other, weight)
 
 
-def mlp(index, base, terms, gain, weight, gate, up, down, hidden):
+def norm_own(index, base, terms, gain):
     rows, width = base.shape
-    block = 256
     piece = width // TP
 
-    def body(index_ref, base_ref, a, b, c, d, gain_ref, g_ref, u_ref, d_ref, *refs):
-        own_ref, part_refs = refs[0], refs[1 : 1 + TP]
-        total_ref, normed_ref, acc_ref = refs[1 + TP :]
-        step = pl.program_id(0)
-
-        @pl.when(step == 0)
-        def _():
-            total, normed = add_and_norm(base_ref, (a, b, c, d), gain_ref)
-            total_ref[...] = total
-            normed_ref[...] = normed
-
-        normed = normed_ref[...]
-        g = jnp.dot(normed, g_ref[...], preferred_element_type=F32)
-        u = jnp.dot(normed, u_ref[...], preferred_element_type=F32)
-        inner = (jax.nn.silu(g) * u).astype(BF16)
-        term = lax.dot_general(inner, d_ref[...], NT, preferred_element_type=F32)
-
-        @pl.when(step == 0)
-        def _():
-            acc_ref[...] = term
-
-        @pl.when(step > 0)
-        def _():
-            acc_ref[...] += term
-
-        @pl.when(step == hidden // block - 1)
-        def _():
-            columns = lambda k: pl.ds(pl.multiple_of(index_ref[k] * piece, piece), piece)
-            own_ref[...] = total_ref[:, columns(0)]
-            for k in range(TP):
-                part_refs[k][...] = acc_ref[:, columns(k)].astype(BF16)
-
-    whole = pl.BlockSpec((rows, width), lambda f, i: (0, 0))
-    at = lambda first: pl.BlockSpec((width, block), lambda f, i: (0, first // block + f))
-    return pl.pallas_call(
-        body,
-        grid_spec=pltpu.PrefetchScalarGridSpec(
-            num_scalar_prefetch=1,
-            grid=(hidden // block,),
-            in_specs=[whole] * 5
-            + [pl.BlockSpec((1, width), lambda f, i: (0, 0)), at(gate), at(up), at(down)],
-            out_specs=[pl.BlockSpec((rows, piece), lambda f, i: (0, 0))] * (1 + TP),
-            scratch_shapes=[
-                pltpu.VMEM((rows, width), BF16),
-                pltpu.VMEM((rows, width), BF16),
-                pltpu.VMEM((rows, width), F32),
-            ],
-        ),
-        out_shape=[jax.ShapeDtypeStruct((rows, piece), BF16)] * (1 + TP),
+    def body(index_ref, base_ref, a, b, c, d, gain_ref, own_ref, normed_ref, total_ref):
+        total, normed = add_and_norm(base_ref, (a, b, c, d), gain_ref)
+        total_ref[...] = total
+        normed_ref[...] = normed
+        own_ref[...] = total_ref[:, pl.ds(pl.multiple_of(index_ref[0] * piece, piece), piece)]
+
+    vmem = pl.BlockSpec(memory_space=pltpu.VMEM)
+    return pl.pallas_call(
+        body,
+        in_specs=[pl.BlockSpec(memory_space=pltpu.SMEM)] + [vmem] * 6,
+        out_specs=[vmem] * 2,
+        out_shape=[
+            jax.ShapeDtypeStruct((rows, piece), BF16),
+            jax.ShapeDtypeStruct((rows, width), BF16),
+        ],
+        scratch_shapes=[pltpu.VMEM((rows, width), BF16)],
         compiler_params=params(),
-        cost_estimate=cost(6 * rows * width * hidden, 6 * width * hidden),
-    )(index, base, *terms, gain, weight, weight, weight)
+        cost_estimate=cost(0, 0),
+    )(index, base, *terms, gain)
+
+
+def mlp(spot, normed, weight):
+    rows, width = normed[0].shape
+    share = weight.shape[1] // 3
+    piece = width // TP
+
+    def body(spot_ref, *refs):
+        latents = jnp.concatenate([ref[...] for ref in refs[:BREADTH]], axis=0)
+        weight_ref, out_ref = refs[BREADTH:]
+        both = weight_ref[:, : 2 * share]
+        both = jnp.dot(latents, both, preferred_element_type=F32)
+        inner = (jax.nn.silu(both[:, :share]) * both[:, share:]).astype(BF16)
+        for t in range(TP):
+            term = lax.dot_general(
+                inner,
+                weight_ref[t * piece : (t + 1) * piece, 2 * share :],
+                NT,
+                preferred_element_type=F32,
+            ).astype(BF16)
+            for k in range(BREADTH):
+                chip = lax.rem(spot_ref[1] + BREADTH - k, BREADTH)
+                out_ref[chip * TP + t] = term[k * rows : (k + 1) * rows]
+
+    vmem = pl.BlockSpec(memory_space=pltpu.VMEM)
+    return pl.pallas_call(
+        body,
+        in_specs=[pl.BlockSpec(memory_space=pltpu.SMEM)] + [vmem] * (BREADTH + 1),
+        out_specs=vmem,
+        out_shape=jax.ShapeDtypeStruct((BREADTH * TP, rows, piece), BF16),
+        compiler_params=params(),
+        cost_estimate=cost(0, 0),
+    )(spot, *normed, weight)
 
 
 def local(
@@ -410,25 +414,21 @@
     seq = chip * CORES + core
     rows = latent_in.shape[0]
     width = w_query.shape[1]
-    hidden = w_gate_up.shape[2]
     positions = prefix.shape[0]
     steps = jnp.arange(TP, dtype=jnp.int32)
     source = (tp - steps) % TP
-    target = (tp + steps) % TP
 
     x = lax.axis_index("x")
-    late, *heads = pack(x.astype(jnp.int32)[None], w_self_qkv, w_self_out.T, w_gate_up, w_down.T)
+    heads = pack(x.astype(jnp.int32)[None], w_self_qkv, w_self_out.T, w_gate_up, w_down.T)
+    latent_pieces = everyone(latent_in)
+    latent_pieces, heads = lax.optimization_barrier((latent_pieces, heads))
     quad = jnp.stack(
         [heads[0]] + [shifted(heads[k], "x", k, BREADTH) for k in range(1, BREADTH)]
     )
-    quad, late = lax.optimization_barrier((quad, late))
-    quads = lax.all_gather(quad, "z", axis=0)
-    w_late = lax.all_gather(late, SEQ, axis=0, tiled=True)
-
-    latent_pieces = everyone(latent_in)
+
     prefix_pieces = everyone(prefix)
     queries, latents = gathered_matmul(source, latent_pieces, w_query[None], True)
-    queries, prefix_pieces = lax.optimization_barrier((queries, prefix_pieces))
+    queries, prefix_pieces, quad = lax.optimization_barrier((queries, prefix_pieces, quad))
     spread = jnp.broadcast_to(queries, (chips, rows, width))
     all_queries = lax.all_to_all(spread, ZX, 0, 0).reshape(chips * rows, width)
     (keyval,) = gathered_matmul(source, prefix_pieces, w_keyval, False)
@@ -440,34 +440,26 @@
     partial = cross_partial(bases, pos, all_queries, keyval, other_keyval)
     partial = lax.all_to_all(partial.reshape(chips, rows, -1), ZX, 0, 0)
     spot = jnp.stack([lax.axis_index("z"), x, core]).astype(jnp.int32)
-    w_head = assemble(spot, quads, shifted(quads, "core", 1, CORES))
-    partial, w_head = lax.optimization_barrier((partial, w_head))
+    rows_of = lax.all_gather(quad, ("z", "core"), axis=0).reshape(DEPTH, CORES, *quad.shape)
+    weights = assemble(spot, rows_of, (3 * HD, HD, quad.shape[-1] - 4 * HD))
+    partial, weights = lax.optimization_barrier((partial, weights))
+    w_qkv, w_out, w_mlp = weights
     cross_terms = combine_and_project(partial, w_cross_out)
 
     first, normed = norm(latents, everyone(cross_terms), attn_gain[None])
     group = [normed] + [shifted(normed, "x", k, BREADTH) for k in range(1, BREADTH)]
-    queries, keyval = project_head(group, w_head)
+    queries, keyval = project_head(group, w_qkv)
     spread = jnp.broadcast_to(keyval, (DEPTH, *keyval.shape))
     mine = lax.all_to_all(spread, "z", 0, 0).reshape(-1, keyval.shape[1])
     other = shifted(mine, "core", 1, CORES)
-    terms = self_attention(spot, rows, queries, mine, other, w_head)
+    terms = self_attention(spot, rows, queries, mine, other, w_out)
     terms = [terms[0]] + [shifted(terms[k], "x", BREADTH - k, BREADTH) for k in range(1, BREADTH)]
     out_terms = sum(term.astype(F32) for term in terms).astype(BF16)
 
-    own, *parts = mlp(
-        target,
-        first,
-        everyone(out_terms),
-        mlp_gain[None],
-        w_late,
-        0,
-        hidden,
-        2 * hidden,
-        hidden,
-    )
-    sums = [parts[0]] + [shifted(parts[k], "tp", k, TP) for k in range(1, TP)]
-    a, b, c, d = [x.astype(F32) for x in sums]
-    return (own.astype(F32) + ((a + c) + (b + d))).astype(BF16)
+    own, normed = norm_own(tp.astype(jnp.int32)[None], first, everyone(out_terms), mlp_gain[None])
+    group = [normed] + [shifted(normed, "x", k, BREADTH) for k in range(1, BREADTH)]
+    down_terms = lax.all_to_all(mlp(spot, group, w_mlp), ("x", "tp"), 0, 0)
+    return (own.astype(F32) + jnp.sum(down_terms.astype(F32), axis=0)).astype(BF16)
 
 
 def solution(mesh):

time: 195 us -> 181 us (0.928); the launches traced: 193 us -> 181 us
  Pallas kernels: 39.1 us -> 26.4 us
  blocking collectives: 16.3 us -> 28 us
  waiting for transfers between devices: 58.1 us -> 50.9 us
  local copies, waits for them, and re-layouts: 8.02 us -> 4.59 us
    all_to_all x1, waiting for transfers between devices: 15.4 us -> 0.01 us  [local(): partial = lax.all_to_all(partial.reshape(chips, rows, -1), ZX, 0, 0)]
    all_gather x2 -> x1, waiting for transfers between devices: 0.02 us -> 14.3 us  [local(): lax.all_gather(quad, ('z', 'core'), axis=0)]
    all_to_all x0 -> x1, blocking collectives: none -> 13.7 us  [local(): down_terms = lax.all_to_all(mlp(spot, group, w_mlp), ('x', 'tp'), 0, 0)]
    ppermute x27 -> x26, waiting for transfers between devices: 33.7 us -> 22.9 us  [shifted(): lax.ppermute(x, axis, [(i, (i + shift) % count) for i in range(count)])]
    all_to_all x1, waiting for transfers between devices: 8.26 us -> 13.7 us  [local(): all_queries = lax.all_to_all(spread, ZX, 0, 0).reshape(chips * rows, width)]
    pallas_call x2 -> x3, Pallas kernels: 11.7 us -> 7.36 us  [the longest x1 5.83 us: assemble(): pl.pallas_call(body, in_specs=[pl.BlockSpec(memory_space=pltpu.SMEM), pl....]
    ppermute x27 -> x26, starting transfers between devices: 37.2 us -> 40.4 us  [shifted(): lax.ppermute(x, axis, [(i, (i + shift) % count) for i in range(count)])]
    pallas_call x2, Pallas kernels: 10.2 us -> 7.33 us  [gathered_matmul(): pl.pallas_call(body, grid_spec=pltpu.PrefetchScalarGridSpec(num_scalar_pr...]
  transfers between devices with their start and end apart: 31 -> 29, of which waited for: 23 -> 20; matrix products, arithmetic and copies ran while one was open for 2% -> 2% of each run, Pallas kernels for 15% -> 12%
where the time goes in v3:
time: 181 us
  starting transfers between devices  54.1 us (30%)
  waiting for transfers between devices  50.9 us (28%)
  blocking collectives  28 us (15%)
  Pallas kernels  26.4 us (15%)
  between operations  13.6 us (8%)
  local copies, waits for them, and re-layouts  4.59 us (3%)
  other arithmetic  3.1 us (2%)
    ppermute x26, starting transfers between devices, shifted(): lax.ppermute(x, axis, [(i, (i + shift) % count) for i in range(count)])  40.4 us
    ppermute x26, waiting for transfers between devices, shifted(): lax.ppermute(x, axis, [(i, (i + shift) % count) for i in range(count)])  22.9 us
    all_gather x1, waiting for transfers between devices, local(): lax.all_gather(quad, ('z', 'core'), axis=0)  14.3 us
    all_to_all x1, blocking collectives, local(): mine = lax.all_to_all(spread, 'z', 0, 0).reshape(-1, keyval.shape[1])  14.3 us
    all_to_all x1, waiting for transfers between devices, local(): all_queries = lax.all_to_all(spread, ZX, 0, 0).reshape(chips * rows, width)  13.7 us
    all_to_all x1, blocking collectives, local(): down_terms = lax.all_to_all(mlp(spot, group, w_mlp), ('x', 'tp'), 0, 0)  13.7 us
    all_to_all x1, starting transfers between devices, local(): all_queries = lax.all_to_all(spread, ZX, 0, 0).reshape(chips * rows, width)  9.41 us
    pallas_call x2, Pallas kernels, gathered_matmul(): pl.pallas_call(body, grid_spec=pltpu.PrefetchScalarGridSpec(num_scalar_pr...  7.33 us
  transfers between devices with their start and end apart: 29, of which 20 were waited for; matrix products, arithmetic and copies ran while one was open for 2% of the time, Pallas kernels for 12%

profile of v3, /device:TPU:8, one launch (start us, length us, event | category | flops | bytes accessed | tf_op | source)
XLA Modules:
  0.0 180.7 jit_solution(13756928156324237720)
XLA Ops:
  6.5 1.6 collective-permute-start
  8.1 2.7 %collective-permute-start.1 = (bf16[16,512]{1,0:T(8,128)(2,1)}, bf16[16,512]{1,0:T(8,128)(2,1)S(1)}, u32[]{:S(2)}, u32[]{:S(2)}) collective-permute-start(bf16[16,512]{1,0:T(8,128)(2,1)} %refs_0_), channel_id=1, source_target_pairs={{0,2},{1,3},{2,0},{3,1},{4,6},{5,7},{6,4},{7,5},{8,10},{9,11},{10,... | collective-permute-start | bytes 49160 | tf_op jit(solution)/shard_map/ppermute | solution.py:27
  11.5 1.8 shard_map.118
  14.7 1.6 collective-permute-start.8
  17.6 2.6 %collective-permute-start.4 = (bf16[256,512]{1,0:T(8,128)(2,1)}, bf16[256,512]{1,0:T(8,128)(2,1)S(1)}, u32[]{:S(2)}, u32[]{:S(2)}) collective-permute-start(bf16[256,512]{1,0:T(8,128)(2,1)} %refs_0_.1), channel_id=1, source_target_pairs={{0,2},{1,3},{2,0},{3,1},{4,6},{5,7},{6,4},{7,5},{8,10},{9,11},{10,... | collective-permute-start | bytes 786440 | tf_op jit(solution)/shard_map/ppermute | solution.py:27
  20.2 2.0 %collective-permute-start.5 = (bf16[256,512]{1,0:T(8,128)(2,1)}, bf16[256,512]{1,0:T(8,128)(2,1)S(1)}, u32[]{:S(2)}, u32[]{:S(2)}) collective-permute-start(bf16[256,512]{1,0:T(8,128)(2,1)} %refs_0_.1), channel_id=1, source_target_pairs={{0,3},{1,0},{2,1},{3,2},{4,7},{5,4},{6,5},{7,6},{8,11},{9,8},{10,9... | collective-permute-start | bytes 786440 | tf_op jit(solution)/shard_map/ppermute | solution.py:27
  23.9 1.6 copy-done.1
  29.2 1.7 pad_maximum_fusion
  32.0 9.4 %all-to-all-start = ((bf16[32,16,512]{2,1,0:T(8,128)(2,1)}), bf16[32,16,512]{2,1,0:T(8,128)(2,1)S(1)}, u32[]{:S(2)}, u32[]{:S(2)}) async-start(bf16[32,16,512]{2,1,0:T(8,128)(2,1)} %broadcast_in_dim.29), calls=%async_computation | async-start | bytes 1048576 | tf_op jit(solution)/shard_map/all_to_all | solution.py:433
  41.4 6.0 %shard_map.120.mine_ref = bf16[2,256,512]{2,1,0:T(8,128)(2,1)} custom-call(s32[4]{0:T(128)} %copy-done.10, bf16[256,512]{1,0:T(8,128)(2,1)} %refs_0_.1, bf16[256,512]{1,0:T(8,128)(2,1)} %copy-done.11, bf16[256,512]{1,0:T(8,128)(2,1)} %copy-done.12, bf16[256,512]{1,0:T(8,128)(2,1)} %copy-done.13, bf16[2,2048,512]{2,1,0:T(8,128)(2,1)} %refs_4_.1), custom_call_target="tpu_custom_call" | custom-call | flops 1 | bytes 1 | tf_op jit(solution)/shard_map/pallas_call | solution.py:83
  47.8 1.8 collective-permute-done.9.other_ref
  49.6 13.7 %all-to-all-done = bf16[32,16,512]{2,1,0:T(8,128)(2,1)S(1)} async-done(((bf16[32,16,512]{2,1,0:T(8,128)(2,1)}), bf16[32,16,512]{2,1,0:T(8,128)(2,1)S(1)}, u32[]{:S(2)}, u32[]{:S(2)}) %all-to-all-start) | async-done | bytes 524320 | tf_op jit(solution)/shard_map/all_to_all | solution.py:433
  64.3 7.2 %shard_map.121 = bf16[512,640]{1,0:T(8,128)(2,1)} custom-call(s32[2]{0:T(128)S(1)} %add_multiply_fusion.base_ref, s32[1,512]{1,0:T(1,128)S(1)} %reshape.20.pos_ref, bf16[512,512]{1,0:T(8,128)(2,1)S(1)} %bitcast.21, bf16[2,256,512]{2,1,0:T(8,128)(2,1)S(1)} %copy-done.3, bf16[2,256,512]{2,1,0:T(8,128)(2,1)S(1)} %collective-permute-done.9.other_ref), custom_call_target="tpu_custom_call" | custom-call | flops 1 | bytes 1 | tf_op jit(solution)/shard_map/pallas_call | solution.py:132
  71.5 4.4 %all-to-all-start.1 = ((bf16[32,16,640]{2,1,0:T(8,128)(2,1)}), bf16[32,16,640]{2,1,0:T(8,128)(2,1)S(1)}, u32[]{:S(2)}, u32[]{:S(2)}) async-start(bf16[32,16,640]{2,1,0:T(8,128)(2,1)} %bitcast.13), calls=%async_computation.1 | async-start | bytes 1310720 | tf_op jit(solution)/shard_map/all_to_all | solution.py:441
  76.5 14.3 %all-gather.3.cloned.1.call-done = bf16[64,32,1280]{2,1,0:T(8,128)(2,1)} async-done(((bf16[4,32,1280]{2,1,0:T(8,128)(2,1)}), bf16[64,32,1280]{2,1,0:T(8,128)(2,1)}) %all-gather.3.cloned.1.call-update) | async-done | bytes 5242896 | tf_op jit(solution)/shard_map/all_gather | solution.py:443
  90.9 5.8 %shard_map.122 = (bf16[2048,384]{1,0:T(8,128)(2,1)}, bf16[2048,128]{1,0:T(8,128)(2,1)}, bf16[2048,768]{1,0:T(8,128)(2,1)}) custom-call(s32[3]{0:T(128)} %pad_add_fusion.spot_ref, bf16[8,2,4,32,1280]{4,3,2,1,0:T(8,128)(2,1)} %bitcast.27), custom_call_target="tpu_custom_call" | custom-call | flops 1 | bytes 1 | tf_op jit(solution)/shard_map/pallas_call | solution.py:251
  97.7 3.2 %collective-permute-start.10 = (bf16[16,2048]{1,0:T(8,128)(2,1)S(1)}, bf16[16,2048]{1,0:T(8,128)(2,1)S(1)}, u32[]{:S(2)}, u32[]{:S(2)}) collective-permute-start(bf16[16,2048]{1,0:T(8,128)(2,1)S(1)} %shard_map.123.a), channel_id=1, source_target_pairs={{0,1},{1,2},{2,3},{3,0},{4,5},{5,6},{6,7},{7,4},{8,9},{9,10},{10,1... | collective-permute-start | bytes 196616 | tf_op jit(solution)/shard_map/ppermute | solution.py:27
  101.4 1.9 %collective-permute-start.12 = (bf16[16,2048]{1,0:T(8,128)(2,1)S(1)}, bf16[16,2048]{1,0:T(8,128)(2,1)S(1)}, u32[]{:S(2)}, u32[]{:S(2)}) collective-permute-start(bf16[16,2048]{1,0:T(8,128)(2,1)S(1)} %shard_map.123.a), channel_id=1, source_target_pairs={{0,3},{1,0},{2,1},{3,2},{4,7},{5,4},{6,5},{7,6},{8,11},{9,8},{10,9... | collective-permute-start | bytes 196616 | tf_op jit(solution)/shard_map/ppermute | solution.py:27
  103.3 3.7 %collective-permute-done.11.c = bf16[16,2048]{1,0:T(8,128)(2,1)S(1)} collective-permute-done((bf16[16,2048]{1,0:T(8,128)(2,1)S(1)}, bf16[16,2048]{1,0:T(8,128)(2,1)S(1)}, u32[]{:S(2)}, u32[]{:S(2)}) %collective-permute-start.11) | collective-permute-done | bytes 65568 | tf_op jit(solution)/shard_map/ppermute | solution.py:27
  107.2 1.5 collective-permute-start.13
  108.7 2.9 %collective-permute-start.14 = (bf16[16,2048]{1,0:T(8,128)(2,1)S(1)}, bf16[16,2048]{1,0:T(8,128)(2,1)S(1)}, u32[]{:S(2)}, u32[]{:S(2)}) collective-permute-start(bf16[16,2048]{1,0:T(8,128)(2,1)S(1)} %get-tuple-element.67.refs_0_), channel_id=1, source_target_pairs={{0,16},{8,24},{16,0},{24,8},{1,17},{9,25},{17,1},{25,9},{2,18},{10... | collective-permute-start | bytes 196616 | tf_op jit(solution)/shard_map/ppermute | solution.py:27
  113.1 1.5 collective-permute-done.14.refs_2_
  116.3 14.3 %all_to_all.20 = bf16[8,64,256]{2,1,0:T(8,128)(2,1)S(1)} all-to-all(bf16[8,64,256]{2,1,0:T(8,128)(2,1)S(1)} %broadcast_in_dim.31), channel_id=1, replica_groups=mesh['z'=8,'x'=4,'core'=2,'tp'=4] {'z'}, dimensions={0} | all-to-all | bytes 524288 | tf_op jit(solution)/shard_map/all_to_all | solution.py:453
  130.6 1.5 collective-permute-done.16.other_ref
  134.7 3.8 %collective-permute-start.18 = (bf16[16,2048]{1,0:T(8,128)(2,1)S(1)}, bf16[16,2048]{1,0:T(8,128)(2,1)S(1)}, u32[]{:S(2)}, u32[]{:S(2)}) collective-permute-start(bf16[16,2048]{1,0:T(8,128)(2,1)S(1)} %get-tuple-element.74), channel_id=1, source_target_pairs={{0,16},{8,24},{16,0},{24,8},{1,17},{9,25},{17,1},{25,9},{2,18},{10... | collective-permute-start | bytes 196616 | tf_op jit(solution)/shard_map/ppermute | solution.py:27
  139.4 2.6 %collective-permute-done.18 = bf16[16,2048]{1,0:T(8,128)(2,1)S(1)} collective-permute-done((bf16[16,2048]{1,0:T(8,128)(2,1)S(1)}, bf16[16,2048]{1,0:T(8,128)(2,1)S(1)}, u32[]{:S(2)}, u32[]{:S(2)}) %collective-permute-start.18) | collective-permute-done | bytes 65568 | tf_op jit(solution)/shard_map/ppermute | solution.py:27
  144.2 1.7 collective-permute-start.21
  145.8 2.5 %collective-permute-start.22 = (bf16[16,2048]{1,0:T(8,128)(2,1)S(1)}, bf16[16,2048]{1,0:T(8,128)(2,1)S(1)}, u32[]{:S(2)}, u32[]{:S(2)}) collective-permute-start(bf16[16,2048]{1,0:T(8,128)(2,1)S(1)} %add_convert_fusion.a), channel_id=1, source_target_pairs={{0,3},{1,0},{2,1},{3,2},{4,7},{5,4},{6,5},{7,6},{8,11},{9,8},{10,9... | collective-permute-start | bytes 196616 | tf_op jit(solution)/shard_map/ppermute | solution.py:27
  148.4 1.6 collective-permute-done.21.c
  150.9 3.0 %collective-permute-start.24 = (bf16[16,2048]{1,0:T(8,128)(2,1)S(1)}, bf16[16,2048]{1,0:T(8,128)(2,1)S(1)}, u32[]{:S(2)}, u32[]{:S(2)}) collective-permute-start(bf16[16,2048]{1,0:T(8,128)(2,1)S(1)} %get-tuple-element.77.refs_0_), channel_id=1, source_target_pairs={{0,16},{8,24},{16,0},{24,8},{1,17},{9,25},{17,1},{25,9},{2,18},{10... | collective-permute-start | bytes 196616 | tf_op jit(solution)/shard_map/ppermute | solution.py:27
  155.0 2.0 %collective-permute-done.23.refs_1_ = bf16[16,2048]{1,0:T(8,128)(2,1)S(1)} collective-permute-done((bf16[16,2048]{1,0:T(8,128)(2,1)S(1)}, bf16[16,2048]{1,0:T(8,128)(2,1)S(1)}, u32[]{:S(2)}, u32[]{:S(2)}) %collective-permute-start.23) | collective-permute-done | bytes 65568 | tf_op jit(solution)/shard_map/ppermute | solution.py:27
  159.5 13.7 %all_to_all.21 = bf16[16,16,512]{2,1,0:T(8,128)(2,1)S(1)} all-to-all(bf16[16,16,512]{2,1,0:T(8,128)(2,1)S(1)} %shard_map.128), channel_id=1, replica_groups=mesh['z'=8,'x'=4,'core'=2,'tp'=4] {'x','tp'}, dimensions={0} | all-to-all | bytes 524288 | tf_op jit(solution)/shard_map/all_to_all | solution.py:461
  (82 shorter events, 27.5 us)
Async XLA Ops:
  6.5 84.3 %all-gather.3.cloned.1.call-start = ((), (), s32[]{:S(2)}) async-start(), calls=%async_computation.4 | async-start | bytes 5570560 | tf_op jit(solution)/shard_map/all_gather | solution.py:443
  6.5 6.7 %collective-permute-start = (bf16[16,512]{1,0:T(8,128)(2,1)}, bf16[16,512]{1,0:T(8,128)(2,1)S(1)}, u32[]{:S(2)}, u32[]{:S(2)}) collective-permute-start(bf16[16,512]{1,0:T(8,128)(2,1)} %refs_0_), channel_id=1, source_target_pairs={{0,1},{1,2},{2,3},{3,0},{4,5},{5,6},{6,7},{7,4},{8,9},{9,10},{10,1... | collective-permute-start | bytes 49160 | tf_op jit(solution)/shard_map/ppermute | solution.py:27
  8.1 5.5 %collective-permute-start.1 = (bf16[16,512]{1,0:T(8,128)(2,1)}, bf16[16,512]{1,0:T(8,128)(2,1)S(1)}, u32[]{:S(2)}, u32[]{:S(2)}) collective-permute-start(bf16[16,512]{1,0:T(8,128)(2,1)} %refs_0_), channel_id=1, source_target_pairs={{0,2},{1,3},{2,0},{3,1},{4,6},{5,7},{6,4},{7,5},{8,10},{9,11},{10,... | collective-permute-start | bytes 49160 | tf_op jit(solution)/shard_map/ppermute | solution.py:27
  10.8 3.9 %collective-permute-start.2 = (bf16[16,512]{1,0:T(8,128)(2,1)}, bf16[16,512]{1,0:T(8,128)(2,1)S(1)}, u32[]{:S(2)}, u32[]{:S(2)}) collective-permute-start(bf16[16,512]{1,0:T(8,128)(2,1)} %refs_0_), channel_id=1, source_target_pairs={{0,3},{1,0},{2,1},{3,2},{4,7},{5,4},{6,5},{7,6},{8,11},{9,8},{10,9... | collective-permute-start | bytes 49160 | tf_op jit(solution)/shard_map/ppermute | solution.py:27
  14.7 8.3 %collective-permute-start.8 = (bf16[32,1280]{1,0:T(8,128)(2,1)}, bf16[32,1280]{1,0:T(8,128)(2,1)S(1)}, u32[]{:S(2)}, u32[]{:S(2)}) collective-permute-start(bf16[32,1280]{1,0:T(8,128)(2,1)} %get-tuple-element.55), channel_id=1, source_target_pairs={{0,24},{8,0},{16,8},{24,16},{1,25},{9,1},{17,9},{25,17},{2,26},{10... | collective-permute-start | bytes 245768 | tf_op jit(solution)/shard_map/ppermute | solution.py:27
  16.3 14.6 %collective-permute-start.3 = (bf16[256,512]{1,0:T(8,128)(2,1)}, bf16[256,512]{1,0:T(8,128)(2,1)S(1)}, u32[]{:S(2)}, u32[]{:S(2)}) collective-permute-start(bf16[256,512]{1,0:T(8,128)(2,1)} %refs_0_.1), channel_id=1, source_target_pairs={{0,1},{1,2},{2,3},{3,0},{4,5},{5,6},{6,7},{7,4},{8,9},{9,10},{10,1... | collective-permute-start | bytes 786440 | tf_op jit(solution)/shard_map/ppermute | solution.py:27
  17.6 13.3 %collective-permute-start.4 = (bf16[256,512]{1,0:T(8,128)(2,1)}, bf16[256,512]{1,0:T(8,128)(2,1)S(1)}, u32[]{:S(2)}, u32[]{:S(2)}) collective-permute-start(bf16[256,512]{1,0:T(8,128)(2,1)} %refs_0_.1), channel_id=1, source_target_pairs={{0,2},{1,3},{2,0},{3,1},{4,6},{5,7},{6,4},{7,5},{8,10},{9,11},{10,... | collective-permute-start | bytes 786440 | tf_op jit(solution)/shard_map/ppermute | solution.py:27
  20.2 10.8 %collective-permute-start.5 = (bf16[256,512]{1,0:T(8,128)(2,1)}, bf16[256,512]{1,0:T(8,128)(2,1)S(1)}, u32[]{:S(2)}, u32[]{:S(2)}) collective-permute-start(bf16[256,512]{1,0:T(8,128)(2,1)} %refs_0_.1), channel_id=1, source_target_pairs={{0,3},{1,0},{2,1},{3,2},{4,7},{5,4},{6,5},{7,6},{8,11},{9,8},{10,9... | collective-permute-start | bytes 786440 | tf_op jit(solution)/shard_map/ppermute | solution.py:27
  22.2 6.2 %collective-permute-start.7 = (bf16[32,1280]{1,0:T(8,128)(2,1)}, bf16[32,1280]{1,0:T(8,128)(2,1)S(1)}, u32[]{:S(2)}, u32[]{:S(2)}) collective-permute-start(bf16[32,1280]{1,0:T(8,128)(2,1)} %get-tuple-element.54), channel_id=1, source_target_pairs={{0,16},{8,24},{16,0},{24,8},{1,17},{9,25},{17,1},{25,9},{2,18},{10... | collective-permute-start | bytes 245768 | tf_op jit(solution)/shard_map/ppermute | solution.py:27
  23.0 6.2 %collective-permute-start.6 = (bf16[32,1280]{1,0:T(8,128)(2,1)}, bf16[32,1280]{1,0:T(8,128)(2,1)S(1)}, u32[]{:S(2)}, u32[]{:S(2)}) collective-permute-start(bf16[32,1280]{1,0:T(8,128)(2,1)} %get-tuple-element.53), channel_id=1, source_target_pairs={{0,8},{8,16},{16,24},{24,0},{1,9},{9,17},{17,25},{25,1},{2,10},{10... | collective-permute-start | bytes 245768 | tf_op jit(solution)/shard_map/ppermute | solution.py:27
  32.0 31.3 %all-to-all-start = ((bf16[32,16,512]{2,1,0:T(8,128)(2,1)}), bf16[32,16,512]{2,1,0:T(8,128)(2,1)S(1)}, u32[]{:S(2)}, u32[]{:S(2)}) async-start(bf16[32,16,512]{2,1,0:T(8,128)(2,1)} %broadcast_in_dim.29), calls=%async_computation | async-start | bytes 1048576 | tf_op jit(solution)/shard_map/all_to_all | solution.py:433
  47.5 2.1 %collective-permute-start.9 = (bf16[2,256,512]{2,1,0:T(8,128)(2,1)}, bf16[2,256,512]{2,1,0:T(8,128)(2,1)S(1)}, u32[]{:S(2)}, u32[]{:S(2)}) collective-permute-start(bf16[2,256,512]{2,1,0:T(8,128)(2,1)} %shard_map.120.mine_ref), channel_id=1, source_target_pairs={{0,4},{4,0},{1,5},{5,1},{2,6},{6,2},{3,7},{7,3},{8,12},{12,8},{9,1... | collective-permute-start | bytes 1572872 | tf_op jit(solution)/shard_map/ppermute | solution.py:27
  71.5 25.2 %all-to-all-start.1 = ((bf16[32,16,640]{2,1,0:T(8,128)(2,1)}), bf16[32,16,640]{2,1,0:T(8,128)(2,1)S(1)}, u32[]{:S(2)}, u32[]{:S(2)}) async-start(bf16[32,16,640]{2,1,0:T(8,128)(2,1)} %bitcast.13), calls=%async_computation.1 | async-start | bytes 1310720 | tf_op jit(solution)/shard_map/all_to_all | solution.py:441
  96.7 35.4 %copy-start.5 = (bf16[2048,128]{1,0:T(8,128)(2,1)S(1)}, bf16[2048,128]{1,0:T(8,128)(2,1)}, u32[]{:S(2)}) copy-start(bf16[2048,128]{1,0:T(8,128)(2,1)} %get-tuple-element.71.weight_ref) | copy-start | bytes 1572868
  96.7 53.9 %copy-start.8 = (f32[2048]{0:T(1024)S(1)}, f32[2048]{0:T(1024)}, u32[]{:S(2)}) copy-start(f32[2048]{0:T(1024)} %param.21) | copy-start | bytes 24580
  96.8 61.4 %copy-start = (bf16[2048,768]{1,0:T(8,128)(2,1)S(1)}, bf16[2048,768]{1,0:T(8,128)(2,1)}, u32[]{:S(2)}) copy-start(bf16[2048,768]{1,0:T(8,128)(2,1)} %get-tuple-element.78.refs_4_) | copy-start | bytes 9437188
  97.7 5.6 %collective-permute-start.10 = (bf16[16,2048]{1,0:T(8,128)(2,1)S(1)}, bf16[16,2048]{1,0:T(8,128)(2,1)S(1)}, u32[]{:S(2)}, u32[]{:S(2)}) collective-permute-start(bf16[16,2048]{1,0:T(8,128)(2,1)S(1)} %shard_map.123.a), channel_id=1, source_target_pairs={{0,1},{1,2},{2,3},{3,0},{4,5},{5,6},{6,7},{7,4},{8,9},{9,10},{10,1... | collective-permute-start | bytes 196616 | tf_op jit(solution)/shard_map/ppermute | solution.py:27
  100.9 6.2 %collective-permute-start.11 = (bf16[16,2048]{1,0:T(8,128)(2,1)S(1)}, bf16[16,2048]{1,0:T(8,128)(2,1)S(1)}, u32[]{:S(2)}, u32[]{:S(2)}) collective-permute-start(bf16[16,2048]{1,0:T(8,128)(2,1)S(1)} %shard_map.123.a), channel_id=1, source_target_pairs={{0,2},{1,3},{2,0},{3,1},{4,6},{5,7},{6,4},{7,5},{8,10},{9,11},{10,... | collective-permute-start | bytes 196616 | tf_op jit(solution)/shard_map/ppermute | solution.py:27
  101.4 5.6 %collective-permute-start.12 = (bf16[16,2048]{1,0:T(8,128)(2,1)S(1)}, bf16[16,2048]{1,0:T(8,128)(2,1)S(1)}, u32[]{:S(2)}, u32[]{:S(2)}) collective-permute-start(bf16[16,2048]{1,0:T(8,128)(2,1)S(1)} %shard_map.123.a), channel_id=1, source_target_pairs={{0,3},{1,0},{2,1},{3,2},{4,7},{5,4},{6,5},{7,6},{8,11},{9,8},{10,9... | collective-permute-start | bytes 196616 | tf_op jit(solution)/shard_map/ppermute | solution.py:27
  107.2 5.9 %collective-permute-start.13 = (bf16[16,2048]{1,0:T(8,128)(2,1)S(1)}, bf16[16,2048]{1,0:T(8,128)(2,1)S(1)}, u32[]{:S(2)}, u32[]{:S(2)}) collective-permute-start(bf16[16,2048]{1,0:T(8,128)(2,1)S(1)} %get-tuple-element.67.refs_0_), channel_id=1, source_target_pairs={{0,8},{8,16},{16,24},{24,0},{1,9},{9,17},{17,25},{25,1},{2,10},{10... | collective-permute-start | bytes 196616 | tf_op jit(solution)/shard_map/ppermute | solution.py:27
  108.7 5.9 %collective-permute-start.14 = (bf16[16,2048]{1,0:T(8,128)(2,1)S(1)}, bf16[16,2048]{1,0:T(8,128)(2,1)S(1)}, u32[]{:S(2)}, u32[]{:S(2)}) collective-permute-start(bf16[16,2048]{1,0:T(8,128)(2,1)S(1)} %get-tuple-element.67.refs_0_), channel_id=1, source_target_pairs={{0,16},{8,24},{16,0},{24,8},{1,17},{9,25},{17,1},{25,9},{2,18},{10... | collective-permute-start | bytes 196616 | tf_op jit(solution)/shard_map/ppermute | solution.py:27
  111.7 4.3 %collective-permute-start.15 = (bf16[16,2048]{1,0:T(8,128)(2,1)S(1)}, bf16[16,2048]{1,0:T(8,128)(2,1)S(1)}, u32[]{:S(2)}, u32[]{:S(2)}) collective-permute-start(bf16[16,2048]{1,0:T(8,128)(2,1)S(1)} %get-tuple-element.67.refs_0_), channel_id=1, source_target_pairs={{0,24},{8,0},{16,8},{24,16},{1,25},{9,1},{17,9},{25,17},{2,26},{10... | collective-permute-start | bytes 196616 | tf_op jit(solution)/shard_map/ppermute | solution.py:27
  130.6 1.5 collective-permute-start.16
  133.5 6.0 %collective-permute-start.19 = (bf16[16,2048]{1,0:T(8,128)(2,1)S(1)}, bf16[16,2048]{1,0:T(8,128)(2,1)S(1)}, u32[]{:S(2)}, u32[]{:S(2)}) collective-permute-start(bf16[16,2048]{1,0:T(8,128)(2,1)S(1)} %get-tuple-element.75), channel_id=1, source_target_pairs={{0,8},{8,16},{16,24},{24,0},{1,9},{9,17},{17,25},{25,1},{2,10},{10... | collective-permute-start | bytes 196616 | tf_op jit(solution)/shard_map/ppermute | solution.py:27
  134.7 7.3 %collective-permute-start.18 = (bf16[16,2048]{1,0:T(8,128)(2,1)S(1)}, bf16[16,2048]{1,0:T(8,128)(2,1)S(1)}, u32[]{:S(2)}, u32[]{:S(2)}) collective-permute-start(bf16[16,2048]{1,0:T(8,128)(2,1)S(1)} %get-tuple-element.74), channel_id=1, source_target_pairs={{0,16},{8,24},{16,0},{24,8},{1,17},{9,25},{17,1},{25,9},{2,18},{10... | collective-permute-start | bytes 196616 | tf_op jit(solution)/shard_map/ppermute | solution.py:27
  138.5 4.3 %collective-permute-start.17 = (bf16[16,2048]{1,0:T(8,128)(2,1)S(1)}, bf16[16,2048]{1,0:T(8,128)(2,1)S(1)}, u32[]{:S(2)}, u32[]{:S(2)}) collective-permute-start(bf16[16,2048]{1,0:T(8,128)(2,1)S(1)} %get-tuple-element.73), channel_id=1, source_target_pairs={{0,24},{8,0},{16,8},{24,16},{1,25},{9,1},{17,9},{25,17},{2,26},{10... | collective-permute-start | bytes 196616 | tf_op jit(solution)/shard_map/ppermute | solution.py:27
  142.8 5.5 %collective-permute-start.20 = (bf16[16,2048]{1,0:T(8,128)(2,1)S(1)}, bf16[16,2048]{1,0:T(8,128)(2,1)S(1)}, u32[]{:S(2)}, u32[]{:S(2)}) collective-permute-start(bf16[16,2048]{1,0:T(8,128)(2,1)S(1)} %add_convert_fusion.a), channel_id=1, source_target_pairs={{0,1},{1,2},{2,3},{3,0},{4,5},{5,6},{6,7},{7,4},{8,9},{9,10},{10,1... | collective-permute-start | bytes 196616 | tf_op jit(solution)/shard_map/ppermute | solution.py:27
  144.2 5.8 %collective-permute-start.21 = (bf16[16,2048]{1,0:T(8,128)(2,1)S(1)}, bf16[16,2048]{1,0:T(8,128)(2,1)S(1)}, u32[]{:S(2)}, u32[]{:S(2)}) collective-permute-start(bf16[16,2048]{1,0:T(8,128)(2,1)S(1)} %add_convert_fusion.a), channel_id=1, source_target_pairs={{0,2},{1,3},{2,0},{3,1},{4,6},{5,7},{6,4},{7,5},{8,10},{9,11},{10,... | collective-permute-start | bytes 196616 | tf_op jit(solution)/shard_map/ppermute | solution.py:27
  145.8 4.8 %collective-permute-start.22 = (bf16[16,2048]{1,0:T(8,128)(2,1)S(1)}, bf16[16,2048]{1,0:T(8,128)(2,1)S(1)}, u32[]{:S(2)}, u32[]{:S(2)}) collective-permute-start(bf16[16,2048]{1,0:T(8,128)(2,1)S(1)} %add_convert_fusion.a), channel_id=1, source_target_pairs={{0,3},{1,0},{2,1},{3,2},{4,7},{5,4},{6,5},{7,6},{8,11},{9,8},{10,9... | collective-permute-start | bytes 196616 | tf_op jit(solution)/shard_map/ppermute | solution.py:27
  150.8 6.3 %collective-permute-start.23 = (bf16[16,2048]{1,0:T(8,128)(2,1)S(1)}, bf16[16,2048]{1,0:T(8,128)(2,1)S(1)}, u32[]{:S(2)}, u32[]{:S(2)}) collective-permute-start(bf16[16,2048]{1,0:T(8,128)(2,1)S(1)} %get-tuple-element.77.refs_0_), channel_id=1, source_target_pairs={{0,8},{8,16},{16,24},{24,0},{1,9},{9,17},{17,25},{25,1},{2,10},{10... | collective-permute-start | bytes 196616 | tf_op jit(solution)/shard_map/ppermute | solution.py:27
  150.9 6.2 %collective-permute-start.24 = (bf16[16,2048]{1,0:T(8,128)(2,1)S(1)}, bf16[16,2048]{1,0:T(8,128)(2,1)S(1)}, u32[]{:S(2)}, u32[]{:S(2)}) collective-permute-start(bf16[16,2048]{1,0:T(8,128)(2,1)S(1)} %get-tuple-element.77.refs_0_), channel_id=1, source_target_pairs={{0,16},{8,24},{16,0},{24,8},{1,17},{9,25},{17,1},{25,9},{2,18},{10... | collective-permute-start | bytes 196616 | tf_op jit(solution)/shard_map/ppermute | solution.py:27
  153.8 4.3 %collective-permute-start.25 = (bf16[16,2048]{1,0:T(8,128)(2,1)S(1)}, bf16[16,2048]{1,0:T(8,128)(2,1)S(1)}, u32[]{:S(2)}, u32[]{:S(2)}) collective-permute-start(bf16[16,2048]{1,0:T(8,128)(2,1)S(1)} %get-tuple-element.77.refs_0_), channel_id=1, source_target_pairs={{0,24},{8,0},{16,8},{24,16},{1,25},{9,1},{17,9},{25,17},{2,26},{10... | collective-permute-start | bytes 196616 | tf_op jit(solution)/shard_map/ppermute | solution.py:27
  (12 other events, 154.3 us)
Sparse Core Ops, SparseCore 0:
  31.2 59.6 all-gather.2

commit v4 on v3

--- a/solution.py
+++ b/solution.py
@@ -10,6 +10,7 @@
 NEG = -1e30
 EPS = 1e-05
 SCALE = HD ** (-0.5)
+LOG2E = 1.4426950408889634
 TP = 4
 CORES = 2
 DEPTH = 8
@@ -52,83 +53,109 @@
     return pl.CostEstimate(flops=1, bytes_accessed=1, transcendentals=0)
 
 
-def gathered_matmul(index, pieces, weight, keep):
+def project_gathered(index, pieces, weight, body, out_shape, mib):
     rows, width = pieces[0].shape
     groups, _, cols = weight.shape
 
-    def body(index_ref, *refs):
+    def kernel(index_ref, *refs):
         piece_refs, weight_ref = refs[:TP], refs[TP]
-        out_ref, acc_ref = refs[TP + 1], refs[-1]
-        step = pl.program_id(0)
-        for k, piece_ref in enumerate(piece_refs):
-
-            @pl.when(step == k)
-            def _():
-                piece = piece_ref[...]
-                for g in range(groups):
-                    term = jnp.dot(piece, weight_ref[g], preferred_element_type=F32)
-                    acc_ref[g] = term if k == 0 else acc_ref[g] + term
-                if keep:
-                    refs[TP + 2][...] = piece
-
-        @pl.when(step == TP - 1)
-        def _():
-            out_ref[...] = acc_ref[...].astype(BF16)
-
-    out_shape = [jax.ShapeDtypeStruct((groups, rows, cols), BF16)]
-    out_specs = [pl.BlockSpec((groups, rows, cols), lambda k, i: (0, 0, 0))]
-    if keep:
-        out_shape.append(jax.ShapeDtypeStruct((rows, TP * width), BF16))
-        out_specs.append(pl.BlockSpec((rows, width), lambda k, i: (0, i[k])))
-    return pl.pallas_call(
-        body,
-        grid_spec=pltpu.PrefetchScalarGridSpec(
-            num_scalar_prefetch=1,
-            grid=(TP,),
-            in_specs=[pl.BlockSpec((rows, width), lambda k, i: (0, 0))] * TP
-            + [pl.BlockSpec((groups, width, cols), lambda k, i: (0, i[k], 0))],
-            out_specs=out_specs,
-            scratch_shapes=[pltpu.VMEM((groups, rows, cols), F32)],
-        ),
+        out_refs, held_ref, acc_ref, sems = refs[TP + 1 : -3], refs[-3], refs[-2], refs[-1]
+        copies = {}
+        for k in range(TP):
+            at = pl.ds(pl.multiple_of(index_ref[k] * width, width), width)
+            for g in range(groups):
+                copies[k, g] = pltpu.make_async_copy(
+                    weight_ref.at[g, at, :], held_ref.at[k, g], sems.at[k, g]
+                )
+                copies[k, g].start()
+        for k in range(TP):
+            piece = piece_refs[k][...]
+            for g in range(groups):
+                copies[k, g].wait()
+                term = jnp.dot(piece, held_ref[k, g], preferred_element_type=F32)
+                acc_ref[g] = term if k == 0 else acc_ref[g] + term
+        body(index_ref, piece_refs, acc_ref, out_refs)
+
+    vmem = pl.BlockSpec(memory_space=pltpu.VMEM)
+    return pl.pallas_call(
+        kernel,
+        in_specs=[pl.BlockSpec(memory_space=pltpu.SMEM)]
+        + [vmem] * TP
+        + [pl.BlockSpec(memory_space=pl.ANY)],
+        out_specs=[vmem] * len(out_shape),
         out_shape=out_shape,
-        compiler_params=params(48 if keep else 58),
-        cost_estimate=cost(2 * rows * weight.size, 2 * weight.size),
+        scratch_shapes=[
+            pltpu.VMEM((TP, groups, width, cols), BF16),
+            pltpu.VMEM((groups, rows, cols), F32),
+            pltpu.SemaphoreType.DMA((TP, groups)),
+        ],
+        compiler_params=params(mib),
+        cost_estimate=cost(0, 0),
     )(index, *pieces, weight)
 
 
-def cross_partial(bases, pos, queries, mine, other):
-    count, width = queries.shape
-    heads = width // HD
+def project_queries(index, pieces, weight):
+    rows, width = pieces[0].shape
+    heads = weight.shape[1] // HD
+
+    def body(index_ref, piece_refs, acc_ref, out_refs):
+        query_ref, whole_ref = out_refs
+        for k, ref in enumerate(piece_refs):
+            columns = pl.ds(pl.multiple_of(index_ref[k] * width, width), width)
+            whole_ref[:, columns] = ref[...]
+        for h in range(heads):
+            query_ref[h] = acc_ref[0, :, h * HD : (h + 1) * HD].astype(BF16)
+
+    out_shape = [
+        jax.ShapeDtypeStruct((heads, rows, HD), BF16),
+        jax.ShapeDtypeStruct((rows, TP * width), BF16),
+    ]
+    return project_gathered(index, pieces, weight[None], body, out_shape, 58)
+
+
+def project_keyval(index, pieces, weight):
+    rows, _ = pieces[0].shape
+    groups, _, _ = weight.shape
+
+    def body(index_ref, piece_refs, acc_ref, out_refs):
+        for k, ref in enumerate(out_refs):
+            head = lax.rem(index_ref[TP] + k, BREADTH)
+            columns = pl.ds(pl.multiple_of(head * HD, HD), HD)
+            for g in range(groups):
+                ref[g] = acc_ref[g, :, columns].astype(BF16)
+
+    out_shape = [jax.ShapeDtypeStruct((groups, rows, HD), BF16)] * BREADTH
+    return project_gathered(index, pieces, weight, body, out_shape, 58)
+
+
+def cross_partial(bases, pos, queries, pieces):
+    count = queries.shape[0]
     rows = 128
 
-    def body(base_ref, pos_ref, q_ref, mine_ref, other_ref, out_ref, stat_ref):
-        pos = pos_ref[...]
+    def body(base_ref, pos_ref, q_ref, *refs):
+        piece_refs, out_ref, stat_ref = refs[: len(pieces)], refs[-2], refs[-1]
+        pos, q = pos_ref[...], q_ref[...]
+        found = []
+        for n, ref in enumerate(piece_refs):
+            s = lax.dot_general(ref[0], q, NT, preferred_element_type=F32)
+            key = base_ref[n] + lax.broadcasted_iota(jnp.int32, s.shape, 0)
+            found.append(jnp.where(key <= pos, s, NEG))
+        floor = jnp.full((1, rows), NEG * 0.5, F32)
+        for s in found:
+            floor = jnp.maximum(floor, jnp.max(s, axis=0, keepdims=True))
+        total = jnp.zeros((1, rows), F32)
+        summed = jnp.zeros((HD, rows), F32)
+        for s, ref in zip(found, piece_refs):
+            weights = jnp.exp2((s - floor) * (SCALE * LOG2E))
+            total = total + jnp.sum(weights, axis=0, keepdims=True)
+            for part in split(weights):
+                summed = summed + lax.dot_general(ref[1], part, TN, preferred_element_type=F32)
+        out_ref[:, :HD] = summed.T.astype(BF16)
         stat_ref[...] = jnp.zeros_like(stat_ref)
-        for h in range(heads):
-            cols = slice(h * HD, (h + 1) * HD)
-            q = q_ref[:, cols]
-            found = []
-            for n, ref in enumerate((mine_ref, other_ref)):
-                s = lax.dot_general(ref[0, :, cols], q, NT, preferred_element_type=F32) * SCALE
-                key = base_ref[n] + lax.broadcasted_iota(jnp.int32, s.shape, 0)
-                found.append(jnp.where(key <= pos, s, NEG))
-            peak = jnp.maximum(*[jnp.max(s, axis=0, keepdims=True) for s in found])
-            floor = jnp.maximum(peak, NEG * 0.5)
-            total = jnp.zeros_like(peak)
-            summed = jnp.zeros((HD, rows), F32)
-            for s, ref in zip(found, (mine_ref, other_ref)):
-                weights = jnp.exp(s - floor)
-                total = total + jnp.sum(weights, axis=0, keepdims=True)
-                for part in split(weights):
-                    summed = summed + lax.dot_general(
-                        ref[1, :, cols], part, TN, preferred_element_type=F32
-                    )
-            out_ref[:, cols] = summed.T.astype(BF16)
-            for n, term in enumerate(three_terms(floor) + three_terms(total)):
-                stat_ref[n * heads + h : n * heads + h + 1, :] = term
-        out_ref[:, width:] = stat_ref[...].T.astype(BF16)
-
-    keyval = pl.BlockSpec(mine.shape, lambda r, b: (0, 0, 0))
+        for n, term in enumerate(three_terms(floor * SCALE) + three_terms(total)):
+            stat_ref[n : n + 1, :] = term
+        out_ref[:, HD:] = stat_ref[...].T.astype(BF16)
+
     return pl.pallas_call(
         body,
         grid_spec=pltpu.PrefetchScalarGridSpec(
@@ -136,35 +163,30 @@
             grid=(count // rows,),
             in_specs=[
                 pl.BlockSpec((1, rows), lambda r, b: (0, r)),
-                pl.BlockSpec((rows, width), lambda r, b: (r, 0)),
-                keyval,
-                keyval,
-            ],
-            out_specs=pl.BlockSpec((rows, width + LANES), lambda r, b: (r, 0)),
+                pl.BlockSpec((rows, HD), lambda r, b: (r, 0)),
+            ]
+            + [pl.BlockSpec(piece.shape, lambda r, b: (0, 0, 0)) for piece in pieces],
+            out_specs=pl.BlockSpec((rows, HD + LANES), lambda r, b: (r, 0)),
             scratch_shapes=[pltpu.VMEM((LANES, rows), F32)],
         ),
-        out_shape=jax.ShapeDtypeStruct((count, width + LANES), BF16),
+        out_shape=jax.ShapeDtypeStruct((count, HD + LANES), BF16),
         compiler_params=params(),
-        cost_estimate=cost(6 * count * 2 * mine.shape[1] * width, 4 * count * width),
-    )(bases, pos, queries, mine, other)
+        cost_estimate=cost(0, 0),
+    )(bases, pos, queries, *pieces)
 
 
 def combine_and_project(terms, weight):
-    count, rows, packed = terms.shape
-    width = packed - LANES
-    heads = width // HD
+    _, heads, rows, _ = terms.shape
 
     def body(x_ref, w_ref, out_ref, context_ref):
-        stats = x_ref[:, :, width:].astype(F32)
-        field = [stats[:, :, n * heads : (n + 1) * heads] for n in range(6)]
-        peak = field[0] + field[1] + field[2]
-        total = field[3] + field[4] + field[5]
-        factor = jnp.exp(peak - jnp.max(peak, axis=0, keepdims=True))
-        total = jnp.sum(factor * total, axis=0)
         for h in range(heads):
-            cols = slice(h * HD, (h + 1) * HD)
-            summed = jnp.sum(factor[:, :, h : h + 1] * x_ref[:, :, cols].astype(F32), axis=0)
-            context_ref[:, cols] = (summed / total[:, h : h + 1]).astype(BF16)
+            stats = x_ref[:, h, :, HD:].astype(F32)
+            field = [stats[:, :, n : n + 1] for n in range(6)]
+            peak = field[0] + field[1] + field[2]
+            factor = jnp.exp(peak - jnp.max(peak, axis=0, keepdims=True))
+            total = jnp.sum(factor * (field[3] + field[4] + field[5]), axis=0)
+            summed = jnp.sum(factor * x_ref[:, h, :, :HD].astype(F32), axis=0)
+            context_ref[:, h * HD : (h + 1) * HD] = (summed / total).astype(BF16)
         out_ref[...] = jnp.dot(
             context_ref[...], w_ref[...], preferred_element_type=F32
         ).astype(BF16)
@@ -172,9 +194,9 @@
     return pl.pallas_call(
         body,
         out_shape=jax.ShapeDtypeStruct((rows, weight.shape[1]), BF16),
-        scratch_shapes=[pltpu.VMEM((rows, width), BF16)],
+        scratch_shapes=[pltpu.VMEM((rows, heads * HD), BF16)],
         compiler_params=params(),
-        cost_estimate=cost(2 * rows * weight.size, 2 * weight.size),
+        cost_estimate=cost(0, 0),
     )(terms, weight)
 
 
@@ -206,48 +228,60 @@
     groups, depth, _ = w_self_qkv.shape
     share = w_down.shape[1] // BREADTH
 
-    def body(x_ref, qkv_ref, out_ref, gate_up_ref, down_ref, *refs):
-        for k, ref in enumerate(refs):
+    def body(x_ref, qkv_ref, out_ref, gate_up_ref, down_ref, head_ref, unit_ref, *refs):
+        for k in range(BREADTH):
             chip = lax.rem(x_ref[0] + k, BREADTH)
             head = pl.ds(pl.multiple_of(chip * HD, HD), HD)
             units = pl.ds(pl.multiple_of(chip * share, share), share)
             parts = [qkv_ref[g, :, head] for g in range(groups)] + [out_ref[:, head]]
-            parts += [gate_up_ref[g, :, units] for g in range(2)] + [down_ref[:, units]]
-            ref[...] = jnp.concatenate(parts, axis=1)
+            more = [gate_up_ref[g, :, units] for g in range(2)] + [down_ref[:, units]]
+            if k == 0:
+                head_ref[...] = jnp.concatenate(parts, axis=1)
+                unit_ref[...] = jnp.concatenate(more, axis=1)
+            else:
+                refs[k - 1][...] = jnp.concatenate(parts + more, axis=1)
 
     vmem = pl.BlockSpec(memory_space=pltpu.VMEM)
+    widths = (4 * HD, 3 * share) + (4 * HD + 3 * share,) * (BREADTH - 1)
     return pl.pallas_call(
         body,
         in_specs=[pl.BlockSpec(memory_space=pltpu.SMEM)] + [vmem] * 4,
-        out_specs=[vmem] * BREADTH,
-        out_shape=[jax.ShapeDtypeStruct((depth, 4 * HD + 3 * share), BF16)] * BREADTH,
+        out_specs=[vmem] * len(widths),
+        out_shape=[jax.ShapeDtypeStruct((depth, width), BF16) for width in widths],
         cost_estimate=cost(0, 0),
     )(x, w_self_qkv, w_self_out, w_gate_up, w_down)
 
 
+def start_copies(x, rows_ref, out_refs, sems):
+    depth = rows_ref.shape[3]
+    for z in range(DEPTH):
+        for core in range(CORES):
+            for k in range(BREADTH):
+                at_x = lax.rem(x + BREADTH - k, BREADTH)
+                place = ((z * BREADTH + at_x) * CORES + core) * depth
+                at = pl.ds(pl.multiple_of(place, depth), depth)
+                first = 0
+                for n, out_ref in enumerate(out_refs):
+                    width = out_ref.shape[1]
+                    pltpu.make_async_copy(
+                        rows_ref.at[z, core, k, :, pl.ds(first, width)],
+                        out_ref.at[at],
+                        sems.at[n],
+                    ).start()
+                    first += width
+
+
+def wait_copies(out_refs, sems):
+    for n, out_ref in enumerate(out_refs):
+        pltpu.make_async_copy(out_ref, out_ref, sems.at[n]).wait()
+
+
 def assemble(spot, rows, splits):
-    depth = rows.shape[3]
-
     def body(spot_ref, rows_ref, *refs):
-        sems = refs[len(splits)]
-        for z in range(DEPTH):
-            for core in range(CORES):
-                for k in range(BREADTH):
-                    at_x = lax.rem(spot_ref[1] + BREADTH - k, BREADTH)
-                    place = ((z * BREADTH + at_x) * CORES + core) * depth
-                    at = pl.ds(pl.multiple_of(place, depth), depth)
-                    first = 0
-                    for n, width in enumerate(splits):
-                        pltpu.make_async_copy(
-                            rows_ref.at[z, core, k, :, pl.ds(first, width)],
-                            refs[n].at[at],
-                            sems.at[n],
-                        ).start()
-                        first += width
-        for n in range(len(splits)):
-            pltpu.make_async_copy(refs[n], refs[n], sems.at[n]).wait()
-
-    count = DEPTH * BREADTH * CORES * depth
+        start_copies(spot_ref[1], rows_ref, refs[:-1], refs[-1])
+        wait_copies(refs[:-1], refs[-1])
+
+    count = DEPTH * BREADTH * CORES * rows.shape[3]
     return pl.pallas_call(
         body,
         in_specs=[pl.BlockSpec(memory_space=pltpu.SMEM), pl.BlockSpec(memory_space=pl.ANY)],
@@ -362,12 +396,14 @@
 
 def mlp(spot, normed, weight):
     rows, width = normed[0].shape
-    share = weight.shape[1] // 3
+    share = weight.shape[-1] // 3
     piece = width // TP
 
     def body(spot_ref, *refs):
+        rows_ref, out_ref, weight_ref, sems = refs[BREADTH:]
+        start_copies(spot_ref[1], rows_ref, [weight_ref], sems)
         latents = jnp.concatenate([ref[...] for ref in refs[:BREADTH]], axis=0)
-        weight_ref, out_ref = refs[BREADTH:]
+        wait_copies([weight_ref], sems)
         both = weight_ref[:, : 2 * share]
         both = jnp.dot(latents, both, preferred_element_type=F32)
         inner = (jax.nn.silu(both[:, :share]) * both[:, share:]).astype(BF16)
@@ -385,10 +421,16 @@
     vmem = pl.BlockSpec(memory_space=pltpu.VMEM)
     return pl.pallas_call(
         body,
-        in_specs=[pl.BlockSpec(memory_space=pltpu.SMEM)] + [vmem] * (BREADTH + 1),
+        in_specs=[pl.BlockSpec(memory_space=pltpu.SMEM)]
+        + [vmem] * BREADTH
+        + [pl.BlockSpec(memory_space=pl.ANY)],
         out_specs=vmem,
         out_shape=jax.ShapeDtypeStruct((BREADTH * TP, rows, piece), BF16),
-        compiler_params=params(),
+        scratch_shapes=[
+            pltpu.VMEM((width, 3 * share), BF16),
+            pltpu.SemaphoreType.DMA((1,)),
+        ],
+        compiler_params=params(58),
         cost_estimate=cost(0, 0),
     )(spot, *normed, weight)
 
@@ -408,12 +450,9 @@
     w_down,
 ):
     chips = lax.axis_size(ZX)
-    chip = lax.axis_index(ZX)
     core = lax.axis_index("core")
     tp = lax.axis_index("tp")
-    seq = chip * CORES + core
     rows = latent_in.shape[0]
-    width = w_query.shape[1]
     positions = prefix.shape[0]
     steps = jnp.arange(TP, dtype=jnp.int32)
     source = (tp - steps) % TP
@@ -422,28 +461,38 @@
     heads = pack(x.astype(jnp.int32)[None], w_self_qkv, w_self_out.T, w_gate_up, w_down.T)
     latent_pieces = everyone(latent_in)
     latent_pieces, heads = lax.optimization_barrier((latent_pieces, heads))
-    quad = jnp.stack(
-        [heads[0]] + [shifted(heads[k], "x", k, BREADTH) for k in range(1, BREADTH)]
+    beside = [shifted(heads[k + 1], "x", k, BREADTH) for k in range(1, BREADTH)]
+    head_rows = jnp.stack([heads[0]] + [piece[:, : 4 * HD] for piece in beside])
+    unit_rows = jnp.stack([heads[1]] + [piece[:, 4 * HD :] for piece in beside])
+
+    prefix_pieces = everyone(prefix)
+    queries, latents = project_queries(source, latent_pieces, w_query)
+    queries, prefix_pieces, head_rows, unit_rows = lax.optimization_barrier(
+        (queries, prefix_pieces, head_rows, unit_rows)
     )
-
-    prefix_pieces = everyone(prefix)
-    queries, latents = gathered_matmul(source, latent_pieces, w_query[None], True)
-    queries, prefix_pieces, quad = lax.optimization_barrier((queries, prefix_pieces, quad))
-    spread = jnp.broadcast_to(queries, (chips, rows, width))
-    all_queries = lax.all_to_all(spread, ZX, 0, 0).reshape(chips * rows, width)
-    (keyval,) = gathered_matmul(source, prefix_pieces, w_keyval, False)
-    other_keyval = shifted(keyval, "core", 1, CORES)
+    spread = jnp.broadcast_to(queries, (DEPTH, *queries.shape)).reshape(chips, rows, HD)
+    all_queries = lax.all_to_all(spread, ZX, 0, 0).reshape(chips * rows, HD)
+    head_rows = lax.all_gather(head_rows, ("z", "core"), axis=0)
+    unit_rows = lax.all_gather(unit_rows, ("z", "core"), axis=0)
+
+    keyval = project_keyval(jnp.concatenate([source, x[None]]), prefix_pieces, w_keyval)
+    keyval = [keyval[0]] + [shifted(keyval[k], "x", k, BREADTH) for k in range(1, BREADTH)]
+    keyval = keyval + [shifted(piece, "core", 1, CORES) for piece in keyval]
+    z = lax.axis_index("z")
+    beside = jnp.concatenate([(x - steps) % BREADTH] * CORES)
+    at_core = jnp.repeat(jnp.stack([core, 1 - core]), BREADTH)
+    bases = ((z * BREADTH + beside) * CORES + at_core).astype(jnp.int32) * positions
     pos = lax.dynamic_index_in_dim(
         latent_pos.reshape(chips, CORES, rows), core, axis=1, keepdims=False
     ).reshape(1, chips * rows)
-    bases = jnp.stack([seq, chip * CORES + 1 - core]).astype(jnp.int32) * positions
-    partial = cross_partial(bases, pos, all_queries, keyval, other_keyval)
+    partial = cross_partial(bases, pos, all_queries, keyval)
     partial = lax.all_to_all(partial.reshape(chips, rows, -1), ZX, 0, 0)
-    spot = jnp.stack([lax.axis_index("z"), x, core]).astype(jnp.int32)
-    rows_of = lax.all_gather(quad, ("z", "core"), axis=0).reshape(DEPTH, CORES, *quad.shape)
-    weights = assemble(spot, rows_of, (3 * HD, HD, quad.shape[-1] - 4 * HD))
+    partial = partial.reshape(DEPTH, BREADTH, rows, -1)
+    spot = jnp.stack([z, x, core]).astype(jnp.int32)
+    split_cores = lambda x: x.reshape(DEPTH, CORES, *x.shape[1:])
+    weights = assemble(spot, split_cores(head_rows), (3 * HD, HD))
     partial, weights = lax.optimization_barrier((partial, weights))
-    w_qkv, w_out, w_mlp = weights
+    w_qkv, w_out = weights
     cross_terms = combine_and_project(partial, w_cross_out)
 
     first, normed = norm(latents, everyone(cross_terms), attn_gain[None])
@@ -458,7 +507,7 @@
 
     own, normed = norm_own(tp.astype(jnp.int32)[None], first, everyone(out_terms), mlp_gain[None])
     group = [normed] + [shifted(normed, "x", k, BREADTH) for k in range(1, BREADTH)]
-    down_terms = lax.all_to_all(mlp(spot, group, w_mlp), ("x", "tp"), 0, 0)
+    down_terms = lax.all_to_all(mlp(spot, group, split_cores(unit_rows)), ("x", "tp"), 0, 0)
     return (own.astype(F32) + jnp.sum(down_terms.astype(F32), axis=0)).astype(BF16)
 
 

time: 181 us -> 171 us (0.945)
  waiting for transfers between devices: 50.9 us -> 41.5 us
  local copies, waits for them, and re-layouts: 4.59 us -> 2.71 us
    all_gather x1 -> x2, waiting for transfers between devices: 14.3 us -> 0.01 us  [the longest x1 0.01 us: local(): head_rows = lax.all_gather(head_rows, ('z', 'core'), axis=0)]
    all_to_all x1, waiting for transfers between devices: 0.01 us -> 7.41 us  [local(): partial = lax.all_to_all(partial.reshape(chips, rows, -1), ZX, 0, 0)]
    all_to_all x1, waiting for transfers between devices: 13.7 us -> 9.58 us  [local(): all_queries = lax.all_to_all(spread, ZX, 0, 0).reshape(chips * rows, HD)]
    pallas_call x1, Pallas kernels: 1.38 us -> 4.36 us  [mlp(): pl.pallas_call(body, in_specs=[pl.BlockSpec(memory_space=pltpu.SMEM)] + [...]
    pallas_call x1, Pallas kernels: 7.18 us -> 5.01 us  [cross_partial(): pl.pallas_call(body, grid_spec=pltpu.PrefetchScalarGridSpec(num_scalar_pr...]
    pallas_call x1, Pallas kernels: 5.83 us -> 3.81 us  [assemble(): pl.pallas_call(body, in_specs=[pl.BlockSpec(memory_space=pltpu.SMEM), pl....]
    ppermute x26 -> x32, waiting for transfers between devices: 22.9 us -> 23.8 us  [shifted(): lax.ppermute(x, axis, [(i, (i + shift) % count) for i in range(count)])]
    ppermute x26 -> x32, starting transfers between devices: 40.4 us -> 40 us  [shifted(): lax.ppermute(x, axis, [(i, (i + shift) % count) for i in range(count)])]
  transfers between devices with their start and end apart: 29 -> 36, of which waited for: 20 -> 19; matrix products, arithmetic and copies ran while one was open for 2% -> 3% of each run, Pallas kernels for 12% -> 13%
where the time goes in v4:
time: 171 us; the launch traced here: 170 us
  starting transfers between devices  54.2 us (32%)
  waiting for transfers between devices  41.5 us (24%)
  blocking collectives  28 us (16%)
  Pallas kernels  25.8 us (15%)
  between operations  13.8 us (8%)
  other arithmetic  4.01 us (2%)
  local copies, waits for them, and re-layouts  2.71 us (2%)
    ppermute x32, starting transfers between devices, shifted(): lax.ppermute(x, axis, [(i, (i + shift) % count) for i in range(count)])  40 us
    ppermute x32, waiting for transfers between devices, shifted(): lax.ppermute(x, axis, [(i, (i + shift) % count) for i in range(count)])  23.8 us
    all_to_all x1, blocking collectives, local(): mine = lax.all_to_all(spread, 'z', 0, 0).reshape(-1, keyval.shape[1])  14.4 us
    all_to_all x1, blocking collectives, local(): lax.all_to_all(mlp(spot, group, split_cores(unit_rows)), ('x', 'tp'), 0, 0)  13.6 us
    all_to_all x1, starting transfers between devices, local(): all_queries = lax.all_to_all(spread, ZX, 0, 0).reshape(chips * rows, HD)  10.3 us
    all_to_all x1, waiting for transfers between devices, local(): all_queries = lax.all_to_all(spread, ZX, 0, 0).reshape(chips * rows, HD)  9.58 us
    pallas_call x2, Pallas kernels, project_gathered(): pl.pallas_call(kernel, in_specs=[pl.BlockSpec(memory_space=pltpu.SMEM)] +...  8.2 us
    all_to_all x1, waiting for transfers between devices, local(): partial = lax.all_to_all(partial.reshape(chips, rows, -1), ZX, 0, 0)  7.41 us
  transfers between devices with their start and end apart: 36, of which 19 were waited for; matrix products, arithmetic and copies ran while one was open for 3% of the time, Pallas kernels for 13%

profile of v4, /device:TPU:8, one launch (start us, length us, event | category | flops | bytes accessed | tf_op | source)
XLA Modules:
  0.0 169.9 jit_solution(17589680540324512739)
XLA Ops:
  6.5 1.6 collective-permute-start
  8.1 2.7 %collective-permute-start.1 = (bf16[16,512]{1,0:T(8,128)(2,1)}, bf16[16,512]{1,0:T(8,128)(2,1)S(1)}, u32[]{:S(2)}, u32[]{:S(2)}) collective-permute-start(bf16[16,512]{1,0:T(8,128)(2,1)} %refs_0_), channel_id=1, source_target_pairs={{0,2},{1,3},{2,0},{3,1},{4,6},{5,7},{6,4},{7,5},{8,10},{9,11},{10,... | collective-permute-start | bytes 49160 | tf_op jit(solution)/shard_map/ppermute | solution.py:28
  12.8 2.1 %collective-permute-start.4 = (bf16[256,512]{1,0:T(8,128)(2,1)}, bf16[256,512]{1,0:T(8,128)(2,1)S(1)}, u32[]{:S(2)}, u32[]{:S(2)}) collective-permute-start(bf16[256,512]{1,0:T(8,128)(2,1)} %refs_0_.1), channel_id=1, source_target_pairs={{0,2},{1,3},{2,0},{3,1},{4,6},{5,7},{6,4},{7,5},{8,10},{9,11},{10,... | collective-permute-start | bytes 786440 | tf_op jit(solution)/shard_map/ppermute | solution.py:28
  14.9 1.7 %shard_map.118 = (bf16[32,512]{1,0:T(8,128)(2,1)}, bf16[32,768]{1,0:T(8,128)(2,1)}, bf16[32,1280]{1,0:T(8,128)(2,1)}, bf16[32,1280]{1,0:T(8,128)(2,1)}, bf16[32,1280]{1,0:T(8,128)(2,1)}) custom-call(s32[1]{0:T(128)} %bitcast.1.x_ref, bf16[3,32,512]{2,1,0:T(8,128)(2,1)} %qkv_ref.1, bf16[32,512]{1,0:T(8,128)(2,1)} %bitcast.42, ...), custom_call_target="tpu_custom_call" | custom-call | flops 1 | bytes 1 | tf_op jit(solution)/shard_map/pallas_call | solution.py:246
  16.8 2.8 %collective-permute-start.8 = (bf16[32,1280]{1,0:T(8,128)(2,1)}, bf16[32,1280]{1,0:T(8,128)(2,1)S(1)}, u32[]{:S(2)}, u32[]{:S(2)}) collective-permute-start(bf16[32,1280]{1,0:T(8,128)(2,1)} %get-tuple-element.61), channel_id=1, source_target_pairs={{0,24},{8,0},{16,8},{24,16},{1,25},{9,1},{17,9},{25,17},{2,26},{10... | collective-permute-start | bytes 245768 | tf_op jit(solution)/shard_map/ppermute | solution.py:28
  21.0 3.1 %shard_map.119 = (bf16[4,16,128]{2,1,0:T(8,128)(2,1)}, bf16[16,2048]{1,0:T(8,128)(2,1)}) custom-call(s32[4]{0:T(128)} %and_select_fusion.1.index_ref, bf16[16,512]{1,0:T(8,128)(2,1)} %refs_0_, bf16[16,512]{1,0:T(8,128)(2,1)} %copy-done.17, bf16[16,512]{1,0:T(8,128)(2,1)} %copy-done.18, bf16[16,512]{1,0:T(8,128)(2,1)} %copy-done.19, ...), custom_call_target="tpu_custom_call" | custom-call | flops 1 | bytes 1 | tf_op jit(solution)/shard_map/pallas_call | solution.py:80
  25.2 1.8 %collective-permute-done.7 = bf16[32,1280]{1,0:T(8,128)(2,1)S(1)} collective-permute-done((bf16[32,1280]{1,0:T(8,128)(2,1)}, bf16[32,1280]{1,0:T(8,128)(2,1)S(1)}, u32[]{:S(2)}, u32[]{:S(2)}) %collective-permute-start.7) | collective-permute-done | bytes 81952 | tf_op jit(solution)/shard_map/ppermute | solution.py:28
  27.0 2.9 %collective-permute-done.6 = bf16[32,1280]{1,0:T(8,128)(2,1)S(1)} collective-permute-done((bf16[32,1280]{1,0:T(8,128)(2,1)S(1)}, bf16[32,1280]{1,0:T(8,128)(2,1)S(1)}, u32[]{:S(2)}, u32[]{:S(2)}) %collective-permute-start.6) | collective-permute-done | bytes 81952 | tf_op jit(solution)/shard_map/ppermute | solution.py:28
  32.8 5.1 %shard_map.120 = (bf16[2,256,128]{2,1,0:T(8,128)(2,1)}, bf16[2,256,128]{2,1,0:T(8,128)(2,1)}, bf16[2,256,128]{2,1,0:T(8,128)(2,1)}, bf16[2,256,128]{2,1,0:T(8,128)(2,1)}) custom-call(s32[5]{0:T(128)} %pad_add_fusion.1.index_ref, bf16[256,512]{1,0:T(8,128)(2,1)} %refs_0_.1, bf16[256,512]{1,0:T(8,128)(2,1)} %copy-done.9, bf16[256,512]{1,0:T(8,128)(2,1)} %copy-done.10, ...), custom_call_target="tpu_custom_call" | custom-call | flops 1 | bytes 1 | tf_op jit(solution)/shard_map/pallas_call | solution.py:80
  37.9 1.8 %collective-permute-start.10 = (bf16[2,256,128]{2,1,0:T(8,128)(2,1)}, bf16[2,256,128]{2,1,0:T(8,128)(2,1)S(1)}, u32[]{:S(2)}, u32[]{:S(2)}) collective-permute-start(bf16[2,256,128]{2,1,0:T(8,128)(2,1)} %get-tuple-element.70), channel_id=1, source_target_pairs={{0,16},{8,24},{16,0},{24,8},{1,17},{9,25},{17,1},{25,9},{2,18},{10... | collective-permute-start | bytes 393224 | tf_op jit(solution)/shard_map/ppermute | solution.py:28
  39.7 2.3 %collective-permute-start.11 = (bf16[2,256,128]{2,1,0:T(8,128)(2,1)}, bf16[2,256,128]{2,1,0:T(8,128)(2,1)S(1)}, u32[]{:S(2)}, u32[]{:S(2)}) collective-permute-start(bf16[2,256,128]{2,1,0:T(8,128)(2,1)} %get-tuple-element.71), channel_id=1, source_target_pairs={{0,24},{8,0},{16,8},{24,16},{1,25},{9,1},{17,9},{25,17},{2,26},{10... | collective-permute-start | bytes 393224 | tf_op jit(solution)/shard_map/ppermute | solution.py:28
  42.8 10.3 %all-to-all-start = ((bf16[32,16,128]{2,1,0:T(8,128)(2,1)}), bf16[32,16,128]{2,1,0:T(8,128)(2,1)S(1)}, u32[]{:S(2)}, u32[]{:S(2)}) async-start(bf16[32,16,128]{2,1,0:T(8,128)(2,1)} %bitcast.15), calls=%async_computation | async-start | bytes 262144 | tf_op jit(solution)/shard_map/all_to_all | solution.py:474
  55.2 9.6 %all-to-all-done = bf16[32,16,128]{2,1,0:T(8,128)(2,1)S(1)} async-done(((bf16[32,16,128]{2,1,0:T(8,128)(2,1)}), bf16[32,16,128]{2,1,0:T(8,128)(2,1)S(1)}, u32[]{:S(2)}, u32[]{:S(2)}) %all-to-all-start) | async-done | bytes 131104 | tf_op jit(solution)/shard_map/all_to_all | solution.py:474
  65.7 5.0 %shard_map.121 = bf16[512,256]{1,0:T(8,128)(2,1)} custom-call(s32[8]{0:T(128)S(1)} %fusion.4.base_ref, s32[1,512]{1,0:T(1,128)S(1)} %reshape.33.pos_ref, bf16[512,128]{1,0:T(8,128)(2,1)S(1)} %bitcast.34, bf16[2,256,128]{2,1,0:T(8,128)(2,1)S(1)} %copy-done.3, bf16[2,256,128]{2,1,0:T(8,128)(2,1)S(1)} %collective-permute-done.9.refs_1_, ...), custom_call_target="tpu_custom_call" | custom-call | flops 1 | bytes 1 | tf_op jit(solution)/shard_map/pallas_call | solution.py:159
  70.7 3.9 %all-to-all-start.1 = ((bf16[32,16,256]{2,1,0:T(8,128)(2,1)}), bf16[32,16,256]{2,1,0:T(8,128)(2,1)S(1)}, u32[]{:S(2)}, u32[]{:S(2)}) async-start(bf16[32,16,256]{2,1,0:T(8,128)(2,1)} %bitcast.17), calls=%async_computation.1 | async-start | bytes 524288 | tf_op jit(solution)/shard_map/all_to_all | solution.py:489
  75.2 3.8 %shard_map.122 = (bf16[2048,384]{1,0:T(8,128)(2,1)}, bf16[2048,128]{1,0:T(8,128)(2,1)}) custom-call(s32[3]{0:T(128)} %pad_add_fusion.2.spot_ref, bf16[8,2,4,32,512]{4,3,2,1,0:T(8,128)(2,1)} %bitcast.39), custom_call_target="tpu_custom_call" | custom-call | flops 1 | bytes 1 | tf_op jit(solution)/shard_map/pallas_call | solution.py:285
  79.0 7.4 %all-to-all-done.1 = bf16[32,16,256]{2,1,0:T(8,128)(2,1)S(1)} async-done(((bf16[32,16,256]{2,1,0:T(8,128)(2,1)}), bf16[32,16,256]{2,1,0:T(8,128)(2,1)S(1)}, u32[]{:S(2)}, u32[]{:S(2)}) %all-to-all-start.1) | async-done | bytes 262176 | tf_op jit(solution)/shard_map/all_to_all | solution.py:489
  87.0 1.6 collective-permute-start.16
  91.4 3.2 %collective-permute-done.17.c = bf16[16,2048]{1,0:T(8,128)(2,1)S(1)} collective-permute-done((bf16[16,2048]{1,0:T(8,128)(2,1)S(1)}, bf16[16,2048]{1,0:T(8,128)(2,1)S(1)}, u32[]{:S(2)}, u32[]{:S(2)}) %collective-permute-start.17) | collective-permute-done | bytes 65568 | tf_op jit(solution)/shard_map/ppermute | solution.py:28
  95.3 2.6 %collective-permute-start.20 = (bf16[16,2048]{1,0:T(8,128)(2,1)S(1)}, bf16[16,2048]{1,0:T(8,128)(2,1)S(1)}, u32[]{:S(2)}, u32[]{:S(2)}) collective-permute-start(bf16[16,2048]{1,0:T(8,128)(2,1)S(1)} %get-tuple-element.77.refs_0_), channel_id=1, source_target_pairs={{0,16},{8,24},{16,0},{24,8},{1,17},{9,25},{17,1},{25,9},{2,18},{10... | collective-permute-start | bytes 196616 | tf_op jit(solution)/shard_map/ppermute | solution.py:28
  99.2 2.2 %collective-permute-done.19.refs_1_ = bf16[16,2048]{1,0:T(8,128)(2,1)S(1)} collective-permute-done((bf16[16,2048]{1,0:T(8,128)(2,1)S(1)}, bf16[16,2048]{1,0:T(8,128)(2,1)S(1)}, u32[]{:S(2)}, u32[]{:S(2)}) %collective-permute-start.19) | collective-permute-done | bytes 65568 | tf_op jit(solution)/shard_map/ppermute | solution.py:28
  102.7 14.4 %all_to_all.20 = bf16[8,64,256]{2,1,0:T(8,128)(2,1)S(1)} all-to-all(bf16[8,64,256]{2,1,0:T(8,128)(2,1)S(1)} %broadcast_in_dim.31), channel_id=1, replica_groups=mesh['z'=8,'x'=4,'core'=2,'tp'=4] {'z'}, dimensions={0} | all-to-all | bytes 524288 | tf_op jit(solution)/shard_map/all_to_all | solution.py:502
  117.1 1.5 collective-permute-done.22.other_ref
  120.0 1.5 collective-permute-start.25
  121.4 2.7 %collective-permute-start.24 = (bf16[16,2048]{1,0:T(8,128)(2,1)S(1)}, bf16[16,2048]{1,0:T(8,128)(2,1)S(1)}, u32[]{:S(2)}, u32[]{:S(2)}) collective-permute-start(bf16[16,2048]{1,0:T(8,128)(2,1)S(1)} %get-tuple-element.84), channel_id=1, source_target_pairs={{0,16},{8,24},{16,0},{24,8},{1,17},{9,25},{17,1},{25,9},{2,18},{10... | collective-permute-start | bytes 196616 | tf_op jit(solution)/shard_map/ppermute | solution.py:28
  125.5 2.2 %collective-permute-done.24 = bf16[16,2048]{1,0:T(8,128)(2,1)S(1)} collective-permute-done((bf16[16,2048]{1,0:T(8,128)(2,1)S(1)}, bf16[16,2048]{1,0:T(8,128)(2,1)S(1)}, u32[]{:S(2)}, u32[]{:S(2)}) %collective-permute-start.24) | collective-permute-done | bytes 65568 | tf_op jit(solution)/shard_map/ppermute | solution.py:28
  129.6 1.5 collective-permute-start.27
  131.1 2.5 %collective-permute-start.28 = (bf16[16,2048]{1,0:T(8,128)(2,1)S(1)}, bf16[16,2048]{1,0:T(8,128)(2,1)S(1)}, u32[]{:S(2)}, u32[]{:S(2)}) collective-permute-start(bf16[16,2048]{1,0:T(8,128)(2,1)S(1)} %add_convert_fusion.a), channel_id=1, source_target_pairs={{0,3},{1,0},{2,1},{3,2},{4,7},{5,4},{6,5},{7,6},{8,11},{9,8},{10,9... | collective-permute-start | bytes 196616 | tf_op jit(solution)/shard_map/ppermute | solution.py:28
  133.6 1.9 %collective-permute-done.27.c = bf16[16,2048]{1,0:T(8,128)(2,1)S(1)} collective-permute-done((bf16[16,2048]{1,0:T(8,128)(2,1)S(1)}, bf16[16,2048]{1,0:T(8,128)(2,1)S(1)}, u32[]{:S(2)}, u32[]{:S(2)}) %collective-permute-start.27) | collective-permute-done | bytes 65568 | tf_op jit(solution)/shard_map/ppermute | solution.py:28
  136.6 3.0 %collective-permute-start.30 = (bf16[16,2048]{1,0:T(8,128)(2,1)S(1)}, bf16[16,2048]{1,0:T(8,128)(2,1)S(1)}, u32[]{:S(2)}, u32[]{:S(2)}) collective-permute-start(bf16[16,2048]{1,0:T(8,128)(2,1)S(1)} %get-tuple-element.87.refs_0_), channel_id=1, source_target_pairs={{0,16},{8,24},{16,0},{24,8},{1,17},{9,25},{17,1},{25,9},{2,18},{10... | collective-permute-start | bytes 196616 | tf_op jit(solution)/shard_map/ppermute | solution.py:28
  144.5 4.4 %shard_map.128 = bf16[16,16,512]{2,1,0:T(8,128)(2,1)} custom-call(s32[3]{0:T(128)} %pad_add_fusion.2.spot_ref, bf16[16,2048]{1,0:T(8,128)(2,1)} %copy-done.4, bf16[16,2048]{1,0:T(8,128)(2,1)} %copy-done.12, bf16[16,2048]{1,0:T(8,128)(2,1)} %copy-done.13, bf16[16,2048]{1,0:T(8,128)(2,1)} %copy-done.14, bf16[8,2,4,32,768]{4,3,2,1,0:T(8,128)(2,1)} %bitcast.37), custom_call_target="tpu_custom_call" | custom-call | flops 1 | bytes 1 | tf_op jit(solution)/shard_map/pallas_call | solution.py:422
  148.8 13.6 %all_to_all.21 = bf16[16,16,512]{2,1,0:T(8,128)(2,1)S(1)} all-to-all(bf16[16,16,512]{2,1,0:T(8,128)(2,1)} %shard_map.128), channel_id=1, replica_groups=mesh['z'=8,'x'=4,'core'=2,'tp'=4] {'x','tp'}, dimensions={0} | all-to-all | bytes 524288 | tf_op jit(solution)/shard_map/all_to_all | solution.py:510
  (127 shorter events, 29.5 us)
Async XLA Ops:
  6.5 68.6 %all-gather.5.cloned.1.call-start = ((), (), s32[]{:S(2)}) async-start(), calls=%async_computation.4 | async-start | bytes 2228224 | tf_op jit(solution)/shard_map/all_gather | solution.py:475
  6.5 10.1 %collective-permute-start = (bf16[16,512]{1,0:T(8,128)(2,1)}, bf16[16,512]{1,0:T(8,128)(2,1)S(1)}, u32[]{:S(2)}, u32[]{:S(2)}) collective-permute-start(bf16[16,512]{1,0:T(8,128)(2,1)} %refs_0_), channel_id=1, source_target_pairs={{0,1},{1,2},{2,3},{3,0},{4,5},{5,6},{6,7},{7,4},{8,9},{9,10},{10,1... | collective-permute-start | bytes 49160 | tf_op jit(solution)/shard_map/ppermute | solution.py:28
  8.1 8.6 %collective-permute-start.1 = (bf16[16,512]{1,0:T(8,128)(2,1)}, bf16[16,512]{1,0:T(8,128)(2,1)S(1)}, u32[]{:S(2)}, u32[]{:S(2)}) collective-permute-start(bf16[16,512]{1,0:T(8,128)(2,1)} %refs_0_), channel_id=1, source_target_pairs={{0,2},{1,3},{2,0},{3,1},{4,6},{5,7},{6,4},{7,5},{8,10},{9,11},{10,... | collective-permute-start | bytes 49160 | tf_op jit(solution)/shard_map/ppermute | solution.py:28
  10.8 6.0 %collective-permute-start.2 = (bf16[16,512]{1,0:T(8,128)(2,1)}, bf16[16,512]{1,0:T(8,128)(2,1)S(1)}, u32[]{:S(2)}, u32[]{:S(2)}) collective-permute-start(bf16[16,512]{1,0:T(8,128)(2,1)} %refs_0_), channel_id=1, source_target_pairs={{0,3},{1,0},{2,1},{3,2},{4,7},{5,4},{6,5},{7,6},{8,11},{9,8},{10,9... | collective-permute-start | bytes 49160 | tf_op jit(solution)/shard_map/ppermute | solution.py:28
  11.5 19.9 %collective-permute-start.3 = (bf16[256,512]{1,0:T(8,128)(2,1)}, bf16[256,512]{1,0:T(8,128)(2,1)S(1)}, u32[]{:S(2)}, u32[]{:S(2)}) collective-permute-start(bf16[256,512]{1,0:T(8,128)(2,1)} %refs_0_.1), channel_id=1, source_target_pairs={{0,1},{1,2},{2,3},{3,0},{4,5},{5,6},{6,7},{7,4},{8,9},{9,10},{10,1... | collective-permute-start | bytes 786440 | tf_op jit(solution)/shard_map/ppermute | solution.py:28
  12.8 18.5 %collective-permute-start.4 = (bf16[256,512]{1,0:T(8,128)(2,1)}, bf16[256,512]{1,0:T(8,128)(2,1)S(1)}, u32[]{:S(2)}, u32[]{:S(2)}) collective-permute-start(bf16[256,512]{1,0:T(8,128)(2,1)} %refs_0_.1), channel_id=1, source_target_pairs={{0,2},{1,3},{2,0},{3,1},{4,6},{5,7},{6,4},{7,5},{8,10},{9,11},{10,... | collective-permute-start | bytes 786440 | tf_op jit(solution)/shard_map/ppermute | solution.py:28
  16.7 14.7 %collective-permute-start.5 = (bf16[256,512]{1,0:T(8,128)(2,1)}, bf16[256,512]{1,0:T(8,128)(2,1)S(1)}, u32[]{:S(2)}, u32[]{:S(2)}) collective-permute-start(bf16[256,512]{1,0:T(8,128)(2,1)} %refs_0_.1), channel_id=1, source_target_pairs={{0,3},{1,0},{2,1},{3,2},{4,7},{5,4},{6,5},{7,6},{8,11},{9,8},{10,9... | collective-permute-start | bytes 786440 | tf_op jit(solution)/shard_map/ppermute | solution.py:28
  16.8 7.4 %collective-permute-start.8 = (bf16[32,1280]{1,0:T(8,128)(2,1)}, bf16[32,1280]{1,0:T(8,128)(2,1)S(1)}, u32[]{:S(2)}, u32[]{:S(2)}) collective-permute-start(bf16[32,1280]{1,0:T(8,128)(2,1)} %get-tuple-element.61), channel_id=1, source_target_pairs={{0,24},{8,0},{16,8},{24,16},{1,25},{9,1},{17,9},{25,17},{2,26},{10... | collective-permute-start | bytes 245768 | tf_op jit(solution)/shard_map/ppermute | solution.py:28
  20.2 6.8 %collective-permute-start.7 = (bf16[32,1280]{1,0:T(8,128)(2,1)}, bf16[32,1280]{1,0:T(8,128)(2,1)S(1)}, u32[]{:S(2)}, u32[]{:S(2)}) collective-permute-start(bf16[32,1280]{1,0:T(8,128)(2,1)} %get-tuple-element.60), channel_id=1, source_target_pairs={{0,16},{8,24},{16,0},{24,8},{1,17},{9,25},{17,1},{25,9},{2,18},{10... | collective-permute-start | bytes 245768 | tf_op jit(solution)/shard_map/ppermute | solution.py:28
  24.2 5.7 %collective-permute-start.6 = (bf16[32,1280]{1,0:T(8,128)(2,1)S(1)}, bf16[32,1280]{1,0:T(8,128)(2,1)S(1)}, u32[]{:S(2)}, u32[]{:S(2)}) collective-permute-start(bf16[32,1280]{1,0:T(8,128)(2,1)S(1)} %copy-done.23), channel_id=1, source_target_pairs={{0,8},{8,16},{16,24},{24,0},{1,9},{9,17},{17,25},{25,1},{2,10},{10... | collective-permute-start | bytes 245768 | tf_op jit(solution)/shard_map/ppermute | solution.py:28
  31.4 112.4 %all-gather.7.cloned.1.call-start = ((), (), s32[]{:S(2)}) async-start(), calls=%async_computation.5 | async-start | bytes 3342336 | tf_op jit(solution)/shard_map/all_gather | solution.py:476
  37.9 15.8 %collective-permute-start.9 = (bf16[2,256,128]{2,1,0:T(8,128)(2,1)}, bf16[2,256,128]{2,1,0:T(8,128)(2,1)S(1)}, u32[]{:S(2)}, u32[]{:S(2)}) collective-permute-start(bf16[2,256,128]{2,1,0:T(8,128)(2,1)} %get-tuple-element.69), channel_id=1, source_target_pairs={{0,8},{8,16},{16,24},{24,0},{1,9},{9,17},{17,25},{25,1},{2,10},{10... | collective-permute-start | bytes 393224 | tf_op jit(solution)/shard_map/ppermute | solution.py:28
  37.9 16.2 %collective-permute-start.10 = (bf16[2,256,128]{2,1,0:T(8,128)(2,1)}, bf16[2,256,128]{2,1,0:T(8,128)(2,1)S(1)}, u32[]{:S(2)}, u32[]{:S(2)}) collective-permute-start(bf16[2,256,128]{2,1,0:T(8,128)(2,1)} %get-tuple-element.70), channel_id=1, source_target_pairs={{0,16},{8,24},{16,0},{24,8},{1,17},{9,25},{17,1},{25,9},{2,18},{10... | collective-permute-start | bytes 393224 | tf_op jit(solution)/shard_map/ppermute | solution.py:28
  39.7 14.7 %collective-permute-start.11 = (bf16[2,256,128]{2,1,0:T(8,128)(2,1)}, bf16[2,256,128]{2,1,0:T(8,128)(2,1)S(1)}, u32[]{:S(2)}, u32[]{:S(2)}) collective-permute-start(bf16[2,256,128]{2,1,0:T(8,128)(2,1)} %get-tuple-element.71), channel_id=1, source_target_pairs={{0,24},{8,0},{16,8},{24,16},{1,25},{9,1},{17,9},{25,17},{2,26},{10... | collective-permute-start | bytes 393224 | tf_op jit(solution)/shard_map/ppermute | solution.py:28
  42.8 22.0 %all-to-all-start = ((bf16[32,16,128]{2,1,0:T(8,128)(2,1)}), bf16[32,16,128]{2,1,0:T(8,128)(2,1)S(1)}, u32[]{:S(2)}, u32[]{:S(2)}) async-start(bf16[32,16,128]{2,1,0:T(8,128)(2,1)} %bitcast.15), calls=%async_computation | async-start | bytes 262144 | tf_op jit(solution)/shard_map/all_to_all | solution.py:474
  53.6 11.1 %collective-permute-start.13 = (bf16[2,256,128]{2,1,0:T(8,128)(2,1)S(1)}, bf16[2,256,128]{2,1,0:T(8,128)(2,1)S(1)}, u32[]{:S(2)}, u32[]{:S(2)}) collective-permute-start(bf16[2,256,128]{2,1,0:T(8,128)(2,1)S(1)} %collective-permute-done.9.refs_1_), channel_id=1, source_target_pairs={{0,4},{4,0},{1,5},{5,1},{2,6},{6,2},{3,7},{7,3},{8,12},{12,8},{9,1... | collective-permute-start | bytes 393224 | tf_op jit(solution)/shard_map/ppermute | solution.py:28
  54.1 10.6 %collective-permute-start.14 = (bf16[2,256,128]{2,1,0:T(8,128)(2,1)S(1)}, bf16[2,256,128]{2,1,0:T(8,128)(2,1)S(1)}, u32[]{:S(2)}, u32[]{:S(2)}) collective-permute-start(bf16[2,256,128]{2,1,0:T(8,128)(2,1)S(1)} %collective-permute-done.10.refs_2_), channel_id=1, source_target_pairs={{0,4},{4,0},{1,5},{5,1},{2,6},{6,2},{3,7},{7,3},{8,12},{12,8},{9,1... | collective-permute-start | bytes 393224 | tf_op jit(solution)/shard_map/ppermute | solution.py:28
  54.4 10.4 %collective-permute-start.15 = (bf16[2,256,128]{2,1,0:T(8,128)(2,1)S(1)}, bf16[2,256,128]{2,1,0:T(8,128)(2,1)S(1)}, u32[]{:S(2)}, u32[]{:S(2)}) collective-permute-start(bf16[2,256,128]{2,1,0:T(8,128)(2,1)S(1)} %collective-permute-done.11.refs_3_), channel_id=1, source_target_pairs={{0,4},{4,0},{1,5},{5,1},{2,6},{6,2},{3,7},{7,3},{8,12},{12,8},{9,1... | collective-permute-start | bytes 393224 | tf_op jit(solution)/shard_map/ppermute | solution.py:28
  70.7 15.7 %all-to-all-start.1 = ((bf16[32,16,256]{2,1,0:T(8,128)(2,1)}), bf16[32,16,256]{2,1,0:T(8,128)(2,1)S(1)}, u32[]{:S(2)}, u32[]{:S(2)}) async-start(bf16[32,16,256]{2,1,0:T(8,128)(2,1)} %bitcast.17), calls=%async_computation.1 | async-start | bytes 524288 | tf_op jit(solution)/shard_map/all_to_all | solution.py:489
  87.0 4.3 %collective-permute-start.16 = (bf16[16,2048]{1,0:T(8,128)(2,1)S(1)}, bf16[16,2048]{1,0:T(8,128)(2,1)S(1)}, u32[]{:S(2)}, u32[]{:S(2)}) collective-permute-start(bf16[16,2048]{1,0:T(8,128)(2,1)S(1)} %shard_map.123.a), channel_id=1, source_target_pairs={{0,1},{1,2},{2,3},{3,0},{4,5},{5,6},{6,7},{7,4},{8,9},{9,10},{10,1... | collective-permute-start | bytes 196616 | tf_op jit(solution)/shard_map/ppermute | solution.py:28
  88.7 5.9 %collective-permute-start.17 = (bf16[16,2048]{1,0:T(8,128)(2,1)S(1)}, bf16[16,2048]{1,0:T(8,128)(2,1)S(1)}, u32[]{:S(2)}, u32[]{:S(2)}) collective-permute-start(bf16[16,2048]{1,0:T(8,128)(2,1)S(1)} %shard_map.123.a), channel_id=1, source_target_pairs={{0,2},{1,3},{2,0},{3,1},{4,6},{5,7},{6,4},{7,5},{8,10},{9,11},{10,... | collective-permute-start | bytes 196616 | tf_op jit(solution)/shard_map/ppermute | solution.py:28
  90.0 5.0 %collective-permute-start.18 = (bf16[16,2048]{1,0:T(8,128)(2,1)S(1)}, bf16[16,2048]{1,0:T(8,128)(2,1)S(1)}, u32[]{:S(2)}, u32[]{:S(2)}) collective-permute-start(bf16[16,2048]{1,0:T(8,128)(2,1)S(1)} %shard_map.123.a), channel_id=1, source_target_pairs={{0,3},{1,0},{2,1},{3,2},{4,7},{5,4},{6,5},{7,6},{8,11},{9,8},{10,9... | collective-permute-start | bytes 196616 | tf_op jit(solution)/shard_map/ppermute | solution.py:28
  95.2 6.3 %collective-permute-start.19 = (bf16[16,2048]{1,0:T(8,128)(2,1)S(1)}, bf16[16,2048]{1,0:T(8,128)(2,1)S(1)}, u32[]{:S(2)}, u32[]{:S(2)}) collective-permute-start(bf16[16,2048]{1,0:T(8,128)(2,1)S(1)} %get-tuple-element.77.refs_0_), channel_id=1, source_target_pairs={{0,8},{8,16},{16,24},{24,0},{1,9},{9,17},{17,25},{25,1},{2,10},{10... | collective-permute-start | bytes 196616 | tf_op jit(solution)/shard_map/ppermute | solution.py:28
  95.3 6.2 %collective-permute-start.20 = (bf16[16,2048]{1,0:T(8,128)(2,1)S(1)}, bf16[16,2048]{1,0:T(8,128)(2,1)S(1)}, u32[]{:S(2)}, u32[]{:S(2)}) collective-permute-start(bf16[16,2048]{1,0:T(8,128)(2,1)S(1)} %get-tuple-element.77.refs_0_), channel_id=1, source_target_pairs={{0,16},{8,24},{16,0},{24,8},{1,17},{9,25},{17,1},{25,9},{2,18},{10... | collective-permute-start | bytes 196616 | tf_op jit(solution)/shard_map/ppermute | solution.py:28
  97.8 4.5 %collective-permute-start.21 = (bf16[16,2048]{1,0:T(8,128)(2,1)S(1)}, bf16[16,2048]{1,0:T(8,128)(2,1)S(1)}, u32[]{:S(2)}, u32[]{:S(2)}) collective-permute-start(bf16[16,2048]{1,0:T(8,128)(2,1)S(1)} %get-tuple-element.77.refs_0_), channel_id=1, source_target_pairs={{0,24},{8,0},{16,8},{24,16},{1,25},{9,1},{17,9},{25,17},{2,26},{10... | collective-permute-start | bytes 196616 | tf_op jit(solution)/shard_map/ppermute | solution.py:28
  120.0 5.6 %collective-permute-start.25 = (bf16[16,2048]{1,0:T(8,128)(2,1)S(1)}, bf16[16,2048]{1,0:T(8,128)(2,1)S(1)}, u32[]{:S(2)}, u32[]{:S(2)}) collective-permute-start(bf16[16,2048]{1,0:T(8,128)(2,1)S(1)} %get-tuple-element.85), channel_id=1, source_target_pairs={{0,8},{8,16},{16,24},{24,0},{1,9},{9,17},{17,25},{25,1},{2,10},{10... | collective-permute-start | bytes 196616 | tf_op jit(solution)/shard_map/ppermute | solution.py:28
  121.4 6.3 %collective-permute-start.24 = (bf16[16,2048]{1,0:T(8,128)(2,1)S(1)}, bf16[16,2048]{1,0:T(8,128)(2,1)S(1)}, u32[]{:S(2)}, u32[]{:S(2)}) collective-permute-start(bf16[16,2048]{1,0:T(8,128)(2,1)S(1)} %get-tuple-element.84), channel_id=1, source_target_pairs={{0,16},{8,24},{16,0},{24,8},{1,17},{9,25},{17,1},{25,9},{2,18},{10... | collective-permute-start | bytes 196616 | tf_op jit(solution)/shard_map/ppermute | solution.py:28
  128.5 5.1 %collective-permute-start.26 = (bf16[16,2048]{1,0:T(8,128)(2,1)S(1)}, bf16[16,2048]{1,0:T(8,128)(2,1)S(1)}, u32[]{:S(2)}, u32[]{:S(2)}) collective-permute-start(bf16[16,2048]{1,0:T(8,128)(2,1)S(1)} %add_convert_fusion.a), channel_id=1, source_target_pairs={{0,1},{1,2},{2,3},{3,0},{4,5},{5,6},{6,7},{7,4},{8,9},{9,10},{10,1... | collective-permute-start | bytes 196616 | tf_op jit(solution)/shard_map/ppermute | solution.py:28
  129.6 5.9 %collective-permute-start.27 = (bf16[16,2048]{1,0:T(8,128)(2,1)S(1)}, bf16[16,2048]{1,0:T(8,128)(2,1)S(1)}, u32[]{:S(2)}, u32[]{:S(2)}) collective-permute-start(bf16[16,2048]{1,0:T(8,128)(2,1)S(1)} %add_convert_fusion.a), channel_id=1, source_target_pairs={{0,2},{1,3},{2,0},{3,1},{4,6},{5,7},{6,4},{7,5},{8,10},{9,11},{10,... | collective-permute-start | bytes 196616 | tf_op jit(solution)/shard_map/ppermute | solution.py:28
  131.1 5.0 %collective-permute-start.28 = (bf16[16,2048]{1,0:T(8,128)(2,1)S(1)}, bf16[16,2048]{1,0:T(8,128)(2,1)S(1)}, u32[]{:S(2)}, u32[]{:S(2)}) collective-permute-start(bf16[16,2048]{1,0:T(8,128)(2,1)S(1)} %add_convert_fusion.a), channel_id=1, source_target_pairs={{0,3},{1,0},{2,1},{3,2},{4,7},{5,4},{6,5},{7,6},{8,11},{9,8},{10,9... | collective-permute-start | bytes 196616 | tf_op jit(solution)/shard_map/ppermute | solution.py:28
  136.2 5.6 %collective-permute-start.29 = (bf16[16,2048]{1,0:T(8,128)(2,1)S(1)}, bf16[16,2048]{1,0:T(8,128)(2,1)S(1)}, u32[]{:S(2)}, u32[]{:S(2)}) collective-permute-start(bf16[16,2048]{1,0:T(8,128)(2,1)S(1)} %get-tuple-element.87.refs_0_), channel_id=1, source_target_pairs={{0,8},{8,16},{16,24},{24,0},{1,9},{9,17},{17,25},{25,1},{2,10},{10... | collective-permute-start | bytes 196616 | tf_op jit(solution)/shard_map/ppermute | solution.py:28
  136.6 5.9 %collective-permute-start.30 = (bf16[16,2048]{1,0:T(8,128)(2,1)S(1)}, bf16[16,2048]{1,0:T(8,128)(2,1)S(1)}, u32[]{:S(2)}, u32[]{:S(2)}) collective-permute-start(bf16[16,2048]{1,0:T(8,128)(2,1)S(1)} %get-tuple-element.87.refs_0_), channel_id=1, source_target_pairs={{0,16},{8,24},{16,0},{24,8},{1,17},{9,25},{17,1},{25,9},{2,18},{10... | collective-permute-start | bytes 196616 | tf_op jit(solution)/shard_map/ppermute | solution.py:28
  (28 other events, 311.1 us)
Sparse Core Ops, SparseCore 0:
  31.5 41.4 all-gather.4
  74.9 42.4 all-gather.6

commit v5 on v4

v5 whole, which is shorter than its diff:
```python
import jax
import jax.numpy as jnp
from jax import lax
from jax.experimental import pallas as pl
from jax.experimental.pallas import tpu as pltpu
from jax.sharding import Mesh
from jax.sharding import PartitionSpec as P

HD = 128
NEG = -1e30
EPS = 1e-05
SCALE = HD ** (-0.5)
LOG2E = 1.4426950408889634
TP = 4
CORES = 2
DEPTH = 8
BREADTH = 4
LANES = 128
ZX = ("z", "x")
SEQ = ("z", "x", "core")
BF16 = jnp.bfloat16
F32 = jnp.float32
NT = (((1,), (1,)), ((), ()))
TN = (((0,), (0,)), ((), ()))


def shifted(x, axis, shift, count):
    return lax.ppermute(x, axis, [(i, (i + shift) % count) for i in range(count)])


def everyone(x):
    return [x] + [shifted(x, "tp", k, TP) for k in range(1, TP)]


def split(weights):
    high = weights.astype(BF16)
    low = (weights - high.astype(F32)).astype(BF16)
    return high, low


def three_terms(x):
    one = x.astype(BF16).astype(F32)
    two = (x - one).astype(BF16).astype(F32)
    three = (x - one - two).astype(BF16).astype(F32)
    return one, two, three


def params(mib=48):
    return pltpu.CompilerParams(vmem_limit_bytes=mib * 1024 * 1024)


def cost():
    return pl.CostEstimate(flops=1, bytes_accessed=1, transcendentals=0)


def behind(at, steps, count):
    return lax.rem(at + count - steps, count)


def project_gathered(pieces, used, weight, body, out_shape):
    first, last = used
    rows, width = last - first, pieces[0].shape[1]
    groups, _, cols = weight.shape

    def kernel(*refs):
        tp = lax.axis_index("tp")
        piece_refs, weight_ref = refs[:TP], refs[TP]
        out_refs = refs[TP + 1 : -5]
        own_ref, held_ref, acc_ref, own_sems, sems = refs[-5:]
        copies = {}
        for k in range(TP):
            copies[k] = pltpu.make_async_copy(
                piece_refs[k].at[pl.ds(first, rows), :], own_ref.at[k], own_sems.at[k]
            )
            copies[k].start()
            at = pl.ds(pl.multiple_of(behind(tp, k, TP) * width, width), width)
            for g in range(groups):
                copies[k, g] = pltpu.make_async_copy(
                    weight_ref.at[g, at, :], held_ref.at[k, g], sems.at[k, g]
                )
                copies[k, g].start()
        for k in range(TP):
            copies[k].wait()
            piece = own_ref[k]
            for g in range(groups):
                copies[k, g].wait()
                term = jnp.dot(piece, held_ref[k, g], preferred_element_type=F32)
                acc_ref[g] = term if k == 0 else acc_ref[g] + term
        body(own_ref, acc_ref, out_refs)

    vmem = pl.BlockSpec(memory_space=pltpu.VMEM)
    return pl.pallas_call(
        kernel,
        in_specs=[pl.BlockSpec(memory_space=pl.ANY)] * (TP + 1),
        out_specs=[vmem] * len(out_shape),
        out_shape=out_shape,
        scratch_shapes=[
            pltpu.VMEM((TP, rows, width), BF16),
            pltpu.VMEM((TP, groups, width, cols), BF16),
            pltpu.VMEM((groups, rows, cols), F32),
            pltpu.SemaphoreType.DMA((TP,)),
            pltpu.SemaphoreType.DMA((TP, groups)),
        ],
        compiler_params=params(58),
        cost_estimate=cost(),
    )(*pieces, weight)


def project_queries(pieces, used, weight):
    first, last = used
    rows, width = last - first, pieces[0].shape[1]
    heads = weight.shape[1] // HD

    def body(own_ref, acc_ref, out_refs):
        tp = lax.axis_index("tp")
        query_ref, whole_ref = out_refs
        for k in range(TP):
            at = behind(tp, k, TP)
            columns = pl.ds(pl.multiple_of(at * width, width), width)
            whole_ref[:, columns] = own_ref[k]
        for h in range(heads):
            query = acc_ref[0, :, h * HD : (h + 1) * HD].astype(BF16)
            for z in range(DEPTH):
                query_ref[z * heads + h] = query

    out_shape = [
        jax.ShapeDtypeStruct((DEPTH * heads, rows, HD), BF16),
        jax.ShapeDtypeStruct((rows, TP * width), BF16),
    ]
    return project_gathered(pieces, used, weight[None], body, out_shape)


def project_keyval(pieces, used, weight):
    rows = used[1] - used[0]
    groups, _, _ = weight.shape

    def body(own_ref, acc_ref, out_refs):
        x = lax.axis_index("x")
        for k, ref in enumerate(out_refs):
            head = lax.rem(x + k, BREADTH)
            columns = pl.ds(pl.multiple_of(head * HD, HD), HD)
            for g in range(groups):
                ref[g] = acc_ref[g, :, columns].astype(BF16)

    out_shape = [jax.ShapeDtypeStruct((groups, rows, HD), BF16)] * BREADTH
    return project_gathered(pieces, used, weight, body, out_shape)


def cross_partial(pos, queries, pieces):
    count = queries.shape[0]
    positions = pieces[0].shape[1]
    rows = 128

    def body(pos_ref, q_ref, *refs):
        piece_refs, out_ref, stat_ref = refs[: len(pieces)], refs[-2], refs[-1]
        z, x, core = [lax.axis_index(name) for name in SEQ]
        pos, q = pos_ref[...], q_ref[...]
        found = []
        for n, ref in enumerate(piece_refs):
            s = lax.dot_general(ref[0], q, NT, preferred_element_type=F32)
            at_core = core if n < BREADTH else 1 - core
            chip = z * BREADTH + behind(x, n % BREADTH, BREADTH)
            key = (chip * CORES + at_core) * positions
            key = key + lax.broadcasted_iota(jnp.int32, s.shape, 0)
            found.append(jnp.where(key <= pos, s, NEG))
        floor = jnp.full((1, rows), NEG * 0.5, F32)
        for s in found:
            floor = jnp.maximum(floor, jnp.max(s, axis=0, keepdims=True))
        total = jnp.zeros((1, rows), F32)
        summed = jnp.zeros((HD, rows), F32)
        for s, ref in zip(found, piece_refs):
            weights = jnp.exp2((s - floor) * (SCALE * LOG2E))
            total = total + jnp.sum(weights, axis=0, keepdims=True)
            for part in split(weights):
                summed = summed + lax.dot_general(ref[1], part, TN, preferred_element_type=F32)
        out_ref[:, :HD] = summed.T.astype(BF16)
        stat_ref[...] = jnp.zeros_like(stat_ref)
        for n, term in enumerate(three_terms(floor * SCALE) + three_terms(total)):
            stat_ref[n : n + 1, :] = term
        out_ref[:, HD:] = stat_ref[...].T.astype(BF16)

    return pl.pallas_call(
        body,
        grid=(count // rows,),
        in_specs=[
            pl.BlockSpec((1, rows), lambda r: (0, r)),
            pl.BlockSpec((rows, HD), lambda r: (r, 0)),
        ]
        + [pl.BlockSpec(piece.shape, lambda r: (0, 0, 0)) for piece in pieces],
        out_specs=pl.BlockSpec((rows, HD + LANES), lambda r: (r, 0)),
        scratch_shapes=[pltpu.VMEM((LANES, rows), F32)],
        out_shape=jax.ShapeDtypeStruct((count, HD + LANES), BF16),
        compiler_params=params(),
        cost_estimate=cost(),
    )(pos, queries, *pieces)


def combine_and_project(terms, weight):
    _, heads, rows, _ = terms.shape

    def body(x_ref, w_ref, out_ref, context_ref):
        for h in range(heads):
            stats = x_ref[:, h, :, HD:].astype(F32)
            field = [stats[:, :, n : n + 1] for n in range(6)]
            peak = field[0] + field[1] + field[2]
            factor = jnp.exp(peak - jnp.max(peak, axis=0, keepdims=True))
            total = jnp.sum(factor * (field[3] + field[4] + field[5]), axis=0)
            summed = jnp.sum(factor * x_ref[:, h, :, :HD].astype(F32), axis=0)
            context_ref[:, h * HD : (h + 1) * HD] = (summed / total).astype(BF16)
        out_ref[...] = jnp.dot(
            context_ref[...], w_ref[...], preferred_element_type=F32
        ).astype(BF16)

    return pl.pallas_call(
        body,
        out_shape=jax.ShapeDtypeStruct((rows, weight.shape[1]), BF16),
        scratch_shapes=[pltpu.VMEM((rows, heads * HD), BF16)],
        compiler_params=params(),
        cost_estimate=cost(),
    )(terms, weight)


def add_and_norm(base_ref, term_refs, gain_ref):
    a, b, c, d = [ref[...].astype(F32) for ref in term_refs]
    total = (base_ref[...].astype(F32) + ((a + c) + (b + d))).astype(BF16)
    x = total.astype(F32)
    scale = lax.rsqrt(jnp.mean(x * x, axis=-1, keepdims=True) + EPS)
    return total, (x * scale * gain_ref[...]).astype(BF16)


def norm(base, terms, gain):
    rows, width = base.shape

    def body(base_ref, a, b, c, d, gain_ref, total_ref, normed_ref):
        total, normed = add_and_norm(base_ref, (a, b, c, d), gain_ref)
        total_ref[...] = total
        normed_ref[...] = normed

    return pl.pallas_call(
        body,
        out_shape=[jax.ShapeDtypeStruct((rows, width), BF16)] * 2,
        compiler_params=params(),
        cost_estimate=cost(),
    )(base, *terms, gain)


def pack(prefix, latent_in, w_self_qkv, w_self_out, w_gate_up, w_down):
    groups, depth, _ = w_self_qkv.shape
    share = w_down.shape[1] // BREADTH
    positions, features = prefix.shape
    joined = positions + latent_in.shape[0]

    def body(prefix_ref, latent_ref, qkv_ref, out_ref, gate_up_ref, down_ref, *refs):
        joined_ref, head_ref, unit_ref, *refs = refs
        x = lax.axis_index("x")
        joined_ref[:positions] = prefix_ref[...]
        joined_ref[positions:] = latent_ref[...]
        for k in range(BREADTH):
            chip = lax.rem(x + k, BREADTH)
            head = pl.ds(pl.multiple_of(chip * HD, HD), HD)
            units = pl.ds(pl.multiple_of(chip * share, share), share)
            parts = [qkv_ref[g, :, head] for g in range(groups)] + [out_ref[:, head]]
            more = [gate_up_ref[g, :, units] for g in range(2)] + [down_ref[:, units]]
            if k == 0:
                head_ref[...] = jnp.concatenate(parts, axis=1)
                unit_ref[...] = jnp.concatenate(more, axis=1)
            else:
                refs[k - 1][...] = jnp.concatenate(parts + more, axis=1)

    vmem = pl.BlockSpec(memory_space=pltpu.VMEM)
    widths = (4 * HD, 3 * share) + (4 * HD + 3 * share,) * (BREADTH - 1)
    return pl.pallas_call(
        body,
        in_specs=[vmem] * 6,
        out_specs=[vmem] * (1 + len(widths)),
        out_shape=[jax.ShapeDtypeStruct((joined, features), BF16)]
        + [jax.ShapeDtypeStruct((depth, width), BF16) for width in widths],
        cost_estimate=cost(),
    )(prefix, latent_in, w_self_qkv, w_self_out, w_gate_up, w_down)


def start_copies(rows_ref, out_refs, sems):
    depth = rows_ref.shape[3]
    x = lax.axis_index("x")
    first = 0
    for n, out_ref in enumerate(out_refs):
        columns = pl.ds(first, out_ref.shape[1])
        first += out_ref.shape[1]
        for z in range(DEPTH):
            for core in range(CORES):
                for k in range(BREADTH):
                    chip = z * BREADTH + behind(x, k, BREADTH)
                    at = pl.multiple_of((chip * CORES + core) * depth, depth)
                    pltpu.make_async_copy(
                        rows_ref.at[z, core, k, :, columns],
                        out_ref.at[pl.ds(at, depth)],
                        sems.at[n],
                    ).start()


def wait_copies(out_ref, sem):
    pltpu.make_async_copy(out_ref, out_ref, sem).wait()


def assemble(rows, splits):
    def body(rows_ref, *refs):
        out_refs, sems = refs[:-1], refs[-1]
        start_copies(rows_ref, out_refs, sems)
        for n, out_ref in enumerate(out_refs):
            wait_copies(out_ref, sems.at[n])

    count = DEPTH * BREADTH * CORES * rows.shape[3]
    return pl.pallas_call(
        body,
        in_specs=[pl.BlockSpec(memory_space=pl.ANY)],
        out_specs=[pl.BlockSpec(memory_space=pltpu.VMEM)] * len(splits),
        out_shape=[jax.ShapeDtypeStruct((count, width), BF16) for width in splits],
        scratch_shapes=[pltpu.SemaphoreType.DMA((len(splits),))],
        compiler_params=params(58),
        cost_estimate=cost(),
    )(rows)


def project_head(normed, weight):
    rows, width = normed[0].shape

    def body(*refs):
        latents = jnp.concatenate([ref[...] for ref in refs[:BREADTH]], axis=0)
        weight_ref, query_ref, keyval_ref = refs[BREADTH:]
        out = jnp.dot(latents, weight_ref[...], preferred_element_type=F32).astype(BF16)
        query_ref[...] = out[:, :HD]
        for z in range(DEPTH):
            keyval_ref[z] = out[:, HD:]

    whole = lambda *shape: pl.BlockSpec(shape, lambda i: (0, 0))
    return pl.pallas_call(
        body,
        grid=(1,),
        in_specs=[whole(rows, width)] * BREADTH + [whole(width, 3 * HD)],
        out_specs=[
            whole(BREADTH * rows, HD),
            pl.BlockSpec((DEPTH, BREADTH * rows, 2 * HD), lambda i: (0, 0, 0)),
        ],
        out_shape=[
            jax.ShapeDtypeStruct((BREADTH * rows, HD), BF16),
            jax.ShapeDtypeStruct((DEPTH, BREADTH * rows, 2 * HD), BF16),
        ],
        compiler_params=params(48),
        cost_estimate=cost(),
    )(*normed, weight)


def self_attention(rows, queries, mine, other, weight):
    total_rows, width = queries.shape
    count = mine.shape[0]
    features = weight.shape[0]

    def index(n, x, core):
        at_z, at_x = n // total_rows, (x + BREADTH - (n // rows) % BREADTH) % BREADTH
        return ((at_z * BREADTH + at_x) * CORES + core) * rows + n % rows

    def body(q_ref, mine_ref, other_ref, weight_ref, *out_refs):
        z, x, core = [lax.axis_index(name) for name in SEQ]
        n = lax.broadcasted_iota(jnp.int32, (1, count), 1)
        key = index(n, x, core)
        keys = (key, key + (1 - 2 * core) * rows)
        n = z * total_rows + lax.broadcasted_iota(jnp.int32, (total_rows, 1), 0)
        row = index(n, x, core)
        found = []
        for ref, key in zip((mine_ref, other_ref), keys):
            s = lax.dot_general(q_ref[...], ref[:, :width], NT, preferred_element_type=F32)
            found.append(jnp.where(key <= row, s * SCALE, NEG))
        peak = jnp.maximum(*[jnp.max(s, axis=1, keepdims=True) for s in found])
        total = jnp.zeros_like(peak)
        summed = jnp.zeros((total_rows, width), F32)
        for s, ref in zip(found, (mine_ref, other_ref)):
            weights = jnp.exp(s - peak)
            total = total + jnp.sum(weights, axis=1, keepdims=True)
            for part in split(weights):
                summed = summed + jnp.dot(part, ref[:, width:], preferred_element_type=F32)
        context = (summed / total).astype(BF16)
        out = lax.dot_general(context, weight_ref[...], NT, preferred_element_type=F32)
        out = out.astype(BF16)
        for k, ref in enumerate(out_refs):
            ref[...] = out[k * rows : (k + 1) * rows]

    return pl.pallas_call(
        body,
        out_shape=[jax.ShapeDtypeStruct((rows, features), BF16)] * BREADTH,
        compiler_params=params(48),
        cost_estimate=cost(),
    )(queries, mine, other, weight)


def norm_own(base, terms, gain):
    rows, width = base.shape
    piece = width // TP

    def body(base_ref, a, b, c, d, gain_ref, own_ref, normed_ref, total_ref):
        tp = lax.axis_index("tp")
        total, normed = add_and_norm(base_ref, (a, b, c, d), gain_ref)
        total_ref[...] = total
        normed_ref[...] = normed
        own_ref[...] = total_ref[:, pl.ds(pl.multiple_of(tp * piece, piece), piece)]

    vmem = pl.BlockSpec(memory_space=pltpu.VMEM)
    return pl.pallas_call(
        body,
        in_specs=[vmem] * 6,
        out_specs=[vmem] * 2,
        out_shape=[
            jax.ShapeDtypeStruct((rows, piece), BF16),
            jax.ShapeDtypeStruct((rows, width), BF16),
        ],
        scratch_shapes=[pltpu.VMEM((rows, width), BF16)],
        compiler_params=params(),
        cost_estimate=cost(),
    )(base, *terms, gain)


def mlp(normed, weight):
    rows, width = normed[0].shape
    share = weight.shape[-1] // 3
    piece = width // TP

    def body(*refs):
        rows_ref, out_ref, both_ref, down_ref, sems = refs[BREADTH:]
        x = lax.axis_index("x")
        start_copies(rows_ref, (both_ref, down_ref), sems)
        latents = jnp.concatenate([ref[...] for ref in refs[:BREADTH]], axis=0)
        wait_copies(both_ref, sems.at[0])
        both = jnp.dot(latents, both_ref[...], preferred_element_type=F32)
        inner = (jax.nn.silu(both[:, :share]) * both[:, share:]).astype(BF16)
        wait_copies(down_ref, sems.at[1])
        for t in range(TP):
            term = lax.dot_general(
                inner,
                down_ref[t * piece : (t + 1) * piece, :],
                NT,
                preferred_element_type=F32,
            ).astype(BF16)
            for k in range(BREADTH):
                out_ref[behind(x, k, BREADTH) * TP + t] = term[k * rows : (k + 1) * rows]

    vmem = pl.BlockSpec(memory_space=pltpu.VMEM)
    return pl.pallas_call(
        body,
        in_specs=[vmem] * BREADTH
        + [pl.BlockSpec(memory_space=pl.ANY)],
        out_specs=vmem,
        out_shape=jax.ShapeDtypeStruct((BREADTH * TP, rows, piece), BF16),
        scratch_shapes=[
            pltpu.VMEM((width, 2 * share), BF16),
            pltpu.VMEM((width, share), BF16),
            pltpu.SemaphoreType.DMA((2,)),
        ],
        compiler_params=params(58),
        cost_estimate=cost(),
    )(*normed, weight)


def local(
    prefix,
    latent_in,
    latent_pos,
    w_query,
    w_keyval,
    w_cross_out,
    attn_gain,
    w_self_qkv,
    w_self_out,
    mlp_gain,
    w_gate_up,
    w_down,
):
    chips = lax.axis_size(ZX)
    core = lax.axis_index("core")
    rows = latent_in.shape[0]
    joined, *heads = pack(prefix, latent_in, w_self_qkv, w_self_out.T, w_gate_up, w_down.T)
    pieces = everyone(joined)
    positions = prefix.shape[0]
    beside = [shifted(heads[k + 1], "x", k, BREADTH) for k in range(1, BREADTH)]
    head_rows = jnp.stack([heads[0]] + [piece[:, : 4 * HD] for piece in beside])
    unit_rows = jnp.stack([heads[1]] + [piece[:, 4 * HD :] for piece in beside])

    used = (positions, positions + rows)
    queries, latents = project_queries( pieces, used, w_query)
    queries, pieces, head_rows = lax.optimization_barrier((queries, pieces, head_rows))
    all_queries = lax.all_to_all(queries, ZX, 0, 0).reshape(chips * rows, HD)
    head_rows = lax.all_gather(head_rows, ("z", "core"), axis=0)

    keyval = project_keyval( pieces, (0, positions), w_keyval)
    keyval = [keyval[0]] + [shifted(keyval[k], "x", k, BREADTH) for k in range(1, BREADTH)]
    keyval = keyval + [shifted(piece, "core", 1, CORES) for piece in keyval]
    pos = lax.dynamic_index_in_dim(
        latent_pos.reshape(chips, CORES, rows), core, axis=1, keepdims=False
    ).reshape(1, chips * rows)
    partial = cross_partial(pos, all_queries, keyval)
    partial = lax.all_to_all(partial.reshape(chips, rows, -1), ZX, 0, 0)
    partial = partial.reshape(DEPTH, BREADTH, rows, -1)
    split_cores = lambda x: x.reshape(DEPTH, CORES, *x.shape[1:])
    weights = assemble(split_cores(head_rows), (3 * HD, HD))
    partial, weights, unit_rows = lax.optimization_barrier((partial, weights, unit_rows))
    unit_rows = lax.all_gather(unit_rows, ("z", "core"), axis=0)
    w_qkv, w_out = weights
    cross_terms = combine_and_project(partial, w_cross_out)

    first, normed = norm(latents, everyone(cross_terms), attn_gain[None])
    group = [normed] + [shifted(normed, "x", k, BREADTH) for k in range(1, BREADTH)]
    queries, keyval = project_head(group, w_qkv)
    mine = lax.all_to_all(keyval, "z", 0, 0).reshape(-1, keyval.shape[2])
    other = shifted(mine, "core", 1, CORES)
    terms = self_attention(rows, queries, mine, other, w_out)
    terms = [terms[0]] + [shifted(terms[k], "x", BREADTH - k, BREADTH) for k in range(1, BREADTH)]
    out_terms = sum(term.astype(F32) for term in terms).astype(BF16)

    own, normed = norm_own(first, everyone(out_terms), mlp_gain[None])
    group = [normed] + [shifted(normed, "x", k, BREADTH) for k in range(1, BREADTH)]
    down_terms = lax.all_to_all(mlp(group, split_cores(unit_rows)), ("x", "tp"), 0, 0)
    return (own.astype(F32) + jnp.sum(down_terms.astype(F32), axis=0)).astype(BF16)


def solution(mesh):
    z, x, core, y = DEPTH, BREADTH, CORES, TP
    grid = Mesh(mesh.devices.reshape(z, x, core, y), ("z", "x", "core", "tp"))
    return jax.shard_map(
        local,
        mesh=grid,
        in_specs=(
            P(SEQ, "tp"),
            P(SEQ, "tp"),
            P(),
            P(None, "tp"),
            P(None, None, "tp"),
            P("tp", None),
            P(),
            P(None, SEQ, "tp"),
            P("tp", SEQ),
            P(),
            P(None, SEQ, "tp"),
            P("tp", SEQ),
        ),
        out_specs=P(SEQ, "tp"),
        check_vma=False,
    )
```

time: 171 us -> 166 us (0.971)
  starting transfers between devices: 54.2 us -> 50.5 us
  Pallas kernels: 25.8 us -> 22.4 us
  waiting for transfers between devices: 41.5 us -> 44.3 us
    ppermute x32 -> x29, starting transfers between devices: 40 us -> 35.4 us  [shifted(): lax.ppermute(x, axis, [(i, (i + shift) % count) for i in range(count)])]
    pallas_call x8, Pallas kernels: 24.6 us -> 21.2 us  [the longest x2 6.75 us: project_gathered(): pl.pallas_call(kernel, in_specs=[pl.BlockSpec(memory_space=pl.ANY)] * (TP...]
    ppermute x32 -> x29, waiting for transfers between devices: 23.8 us -> 26.8 us  [shifted(): lax.ppermute(x, axis, [(i, (i + shift) % count) for i in range(count)])]
  transfers between devices with their start and end apart: 36 -> 33, of which waited for: 19 -> 20; matrix products, arithmetic and copies ran while one was open for 3% -> 1% of each run, Pallas kernels for 13% -> 8%
where the time goes in v5:
time: 166 us
  starting transfers between devices  50.5 us (30%)
  waiting for transfers between devices  44.3 us (27%)
  blocking collectives  29.4 us (18%)
  Pallas kernels  22.4 us (13%)
  between operations  13.7 us (8%)
  other arithmetic  2.81 us (2%)
  local copies, waits for them, and re-layouts  2.52 us (2%)
    ppermute x29, starting transfers between devices, shifted(): lax.ppermute(x, axis, [(i, (i + shift) % count) for i in range(count)])  35.4 us
    ppermute x29, waiting for transfers between devices, shifted(): lax.ppermute(x, axis, [(i, (i + shift) % count) for i in range(count)])  26.8 us
    all_to_all x1, blocking collectives, local(): mine = lax.all_to_all(keyval, 'z', 0, 0).reshape(-1, keyval.shape[2])  15.7 us
    all_to_all x1, blocking collectives, local(): lax.all_to_all(mlp(group, split_cores(unit_rows)), ('x', 'tp'), 0, 0)  13.7 us
    all_to_all x1, starting transfers between devices, local(): all_queries = lax.all_to_all(queries, ZX, 0, 0).reshape(chips * rows, HD)  11 us
    all_to_all x1, waiting for transfers between devices, local(): all_queries = lax.all_to_all(queries, ZX, 0, 0).reshape(chips * rows, HD)  9.69 us
    all_to_all x1, waiting for transfers between devices, local(): partial = lax.all_to_all(partial.reshape(chips, rows, -1), ZX, 0, 0)  7.76 us
    pallas_call x2, Pallas kernels, project_gathered(): pl.pallas_call(kernel, in_specs=[pl.BlockSpec(memory_space=pl.ANY)] * (TP...  6.75 us
  transfers between devices with their start and end apart: 33, of which 20 were waited for; matrix products, arithmetic and copies ran while one was open for 1% of the time, Pallas kernels for 8%

profile of v5, /device:TPU:8, one launch (start us, length us, event | category | flops | bytes accessed | tf_op | source)
XLA Modules:
  0.0 165.7 jit_solution(11249790498042959741)
XLA Ops:
  6.5 2.0 %shard_map.118 = (bf16[272,512]{1,0:T(8,128)(2,1)}, bf16[32,512]{1,0:T(8,128)(2,1)}, bf16[32,768]{1,0:T(8,128)(2,1)}, bf16[32,1280]{1,0:T(8,128)(2,1)}, bf16[32,...) custom-call(bf16[256,512]{1,0:T(8,128)(2,1)} %prefix_ref.1, bf16[16,512]{1,0:T(8,128)(2,1)} %latent_ref.1, ...), custom_call_target="tpu_custom_call" | custom-call | flops 1 | bytes 1 | tf_op jit(solution)/shard_map/pallas_call | solution.py:272
  8.5 2.8 %collective-permute-start.5 = (bf16[32,1280]{1,0:T(8,128)(2,1)}, bf16[32,1280]{1,0:T(8,128)(2,1)S(1)}, u32[]{:S(2)}, u32[]{:S(2)}) collective-permute-start(bf16[32,1280]{1,0:T(8,128)(2,1)} %get-tuple-element.45), channel_id=1, source_target_pairs={{0,24},{8,0},{16,8},{24,16},{1,25},{9,1},{17,9},{25,17},{2,26},{10... | collective-permute-start | bytes 245768 | tf_op jit(solution)/shard_map/ppermute | solution.py:28
  11.3 1.6 collective-permute-start
  13.8 2.4 %collective-permute-start.2 = (bf16[272,512]{1,0:T(8,128)(2,1)}, bf16[272,512]{1,0:T(8,128)(2,1)S(1)}, u32[]{:S(2)}, u32[]{:S(2)}) collective-permute-start(bf16[272,512]{1,0:T(8,128)(2,1)} %get-tuple-element.47.refs_0_), channel_id=1, source_target_pairs={{0,3},{1,0},{2,1},{3,2},{4,7},{5,4},{6,5},{7,6},{8,11},{9,8},{10,9... | collective-permute-start | bytes 835592 | tf_op jit(solution)/shard_map/ppermute | solution.py:28
  17.9 4.5 %collective-permute-done.4 = bf16[32,1280]{1,0:T(8,128)(2,1)S(1)} collective-permute-done((bf16[32,1280]{1,0:T(8,128)(2,1)}, bf16[32,1280]{1,0:T(8,128)(2,1)S(1)}, u32[]{:S(2)}, u32[]{:S(2)}) %collective-permute-start.4) | collective-permute-done | bytes 81952 | tf_op jit(solution)/shard_map/ppermute | solution.py:28
  23.3 1.4 pad_maximum_fusion.1
  24.7 2.9 %collective-permute-done.2.refs_3_ = bf16[272,512]{1,0:T(8,128)(2,1)S(1)} collective-permute-done((bf16[272,512]{1,0:T(8,128)(2,1)}, bf16[272,512]{1,0:T(8,128)(2,1)S(1)}, u32[]{:S(2)}, u32[]{:S(2)}) %collective-permute-start.2) | collective-permute-done | bytes 278560 | tf_op jit(solution)/shard_map/ppermute | solution.py:28
  28.3 2.5 %shard_map.119 = (bf16[32,16,128]{2,1,0:T(8,128)(2,1)}, bf16[16,2048]{1,0:T(8,128)(2,1)}) custom-call(bf16[272,512]{1,0:T(8,128)(2,1)} %get-tuple-element.47.refs_0_, bf16[272,512]{1,0:T(8,128)(2,1)} %copy-done.8, bf16[272,512]{1,0:T(8,128)(2,1)} %copy-done.9, bf16[272,512]{1,0:T(8,128)(2,1)} %copy-done.10, bf16[1,2048,512]{2,1,0:T(8,128)(2,1)} %bitcast.32), custom_call_target="tpu_custom_call" | custom-call | flops 1 | bytes 1 | tf_op jit(solution)/shard_map/pallas_call | solution.py:92
  30.9 4.3 %shard_map.120 = (bf16[2,256,128]{2,1,0:T(8,128)(2,1)}, bf16[2,256,128]{2,1,0:T(8,128)(2,1)}, bf16[2,256,128]{2,1,0:T(8,128)(2,1)}, bf16[2,256,128]{2,1,0:T(8,128)(2,1)}) custom-call(bf16[272,512]{1,0:T(8,128)(2,1)} %get-tuple-element.47.refs_0_, bf16[272,512]{1,0:T(8,128)(2,1)} %copy-done.8, bf16[272,512]{1,0:T(8,128)(2,1)} %copy-done.9, ...), custom_call_target="tpu_custom_call" | custom-call | flops 1 | bytes 1 | tf_op jit(solution)/shard_map/pallas_call | solution.py:92
  35.2 2.3 %collective-permute-start.7 = (bf16[2,256,128]{2,1,0:T(8,128)(2,1)}, bf16[2,256,128]{2,1,0:T(8,128)(2,1)S(1)}, u32[]{:S(2)}, u32[]{:S(2)}) collective-permute-start(bf16[2,256,128]{2,1,0:T(8,128)(2,1)} %get-tuple-element.53), channel_id=1, source_target_pairs={{0,16},{8,24},{16,0},{24,8},{1,17},{9,25},{17,1},{25,9},{2,18},{10... | collective-permute-start | bytes 393224 | tf_op jit(solution)/shard_map/ppermute | solution.py:28
  38.7 11.0 %all-to-all-start = ((bf16[32,16,128]{2,1,0:T(8,128)(2,1)}), bf16[32,16,128]{2,1,0:T(8,128)(2,1)S(1)}, u32[]{:S(2)}, u32[]{:S(2)}) async-start(bf16[32,16,128]{2,1,0:T(8,128)(2,1)} %get-tuple-element.46), calls=%async_computation | async-start | bytes 262144 | tf_op jit(solution)/shard_map/all_to_all | solution.py:489
  51.5 9.7 %all-to-all-done = bf16[32,16,128]{2,1,0:T(8,128)(2,1)S(1)} async-done(((bf16[32,16,128]{2,1,0:T(8,128)(2,1)}), bf16[32,16,128]{2,1,0:T(8,128)(2,1)S(1)}, u32[]{:S(2)}, u32[]{:S(2)}) %all-to-all-start) | async-done | bytes 131104 | tf_op jit(solution)/shard_map/all_to_all | solution.py:489
  62.1 4.5 %shard_map.121 = bf16[512,256]{1,0:T(8,128)(2,1)} custom-call(s32[1,512]{1,0:T(1,128)S(1)} %reshape.26.pos_ref, bf16[512,128]{1,0:T(8,128)(2,1)S(1)} %bitcast.28, bf16[2,256,128]{2,1,0:T(8,128)(2,1)S(1)} %copy-done.3, bf16[2,256,128]{2,1,0:T(8,128)(2,1)S(1)} %collective-permute-done.6.refs_1_, bf16[2,256,128]{2,1,0:T(8,128)(2,1)S(1)} %collective-permute-done.7.refs_2_, ...), custom_call_target="tpu_custom_call" | custom-call | flops 1 | bytes 1 | tf_op jit(solution)/shard_map/pallas_call | solution.py:182
  66.6 3.9 %all-to-all-start.1 = ((bf16[32,16,256]{2,1,0:T(8,128)(2,1)}), bf16[32,16,256]{2,1,0:T(8,128)(2,1)S(1)}, u32[]{:S(2)}, u32[]{:S(2)}) async-start(bf16[32,16,256]{2,1,0:T(8,128)(2,1)} %bitcast.8), calls=%async_computation.1 | async-start | bytes 524288 | tf_op jit(solution)/shard_map/all_to_all | solution.py:499
  71.5 3.0 %shard_map.122 = (bf16[2048,384]{1,0:T(8,128)(2,1)}, bf16[2048,128]{1,0:T(8,128)(2,1)}) custom-call(bf16[8,2,4,32,512]{4,3,2,1,0:T(8,128)(2,1)} %bitcast.33), custom_call_target="tpu_custom_call" | custom-call | flops 1 | bytes 1 | tf_op jit(solution)/shard_map/pallas_call | solution.py:313
  74.5 7.8 %all-to-all-done.1 = bf16[32,16,256]{2,1,0:T(8,128)(2,1)S(1)} async-done(((bf16[32,16,256]{2,1,0:T(8,128)(2,1)}), bf16[32,16,256]{2,1,0:T(8,128)(2,1)S(1)}, u32[]{:S(2)}, u32[]{:S(2)}) %all-to-all-start.1) | async-done | bytes 262176 | tf_op jit(solution)/shard_map/all_to_all | solution.py:499
  83.0 1.5 collective-permute-start.13
  84.5 1.4 collective-permute-start.14
  87.3 3.1 %collective-permute-done.14.c = bf16[16,2048]{1,0:T(8,128)(2,1)S(1)} collective-permute-done((bf16[16,2048]{1,0:T(8,128)(2,1)S(1)}, bf16[16,2048]{1,0:T(8,128)(2,1)S(1)}, u32[]{:S(2)}, u32[]{:S(2)}) %collective-permute-start.14) | collective-permute-done | bytes 65568 | tf_op jit(solution)/shard_map/ppermute | solution.py:28
  91.2 2.6 %collective-permute-start.17 = (bf16[16,2048]{1,0:T(8,128)(2,1)S(1)}, bf16[16,2048]{1,0:T(8,128)(2,1)S(1)}, u32[]{:S(2)}, u32[]{:S(2)}) collective-permute-start(bf16[16,2048]{1,0:T(8,128)(2,1)S(1)} %get-tuple-element.61.refs_0_), channel_id=1, source_target_pairs={{0,16},{8,24},{16,0},{24,8},{1,17},{9,25},{17,1},{25,9},{2,18},{10... | collective-permute-start | bytes 196616 | tf_op jit(solution)/shard_map/ppermute | solution.py:28
  93.8 1.4 collective-permute-start.18
  95.2 2.2 %collective-permute-done.16.refs_1_ = bf16[16,2048]{1,0:T(8,128)(2,1)S(1)} collective-permute-done((bf16[16,2048]{1,0:T(8,128)(2,1)S(1)}, bf16[16,2048]{1,0:T(8,128)(2,1)S(1)}, u32[]{:S(2)}, u32[]{:S(2)}) %collective-permute-start.16) | collective-permute-done | bytes 65568 | tf_op jit(solution)/shard_map/ppermute | solution.py:28
  98.6 15.7 %all_to_all.20 = bf16[8,64,256]{2,1,0:T(8,128)(2,1)S(1)} all-to-all(bf16[8,64,256]{2,1,0:T(8,128)(2,1)S(1)} %get-tuple-element.64), channel_id=1, replica_groups=mesh['z'=8,'x'=4,'core'=2,'tp'=4] {'z'}, dimensions={0} | all-to-all | bytes 524288 | tf_op jit(solution)/shard_map/all_to_all | solution.py:511
  114.2 1.5 collective-permute-done.19.other_ref
  116.9 3.8 %collective-permute-start.21 = (bf16[16,2048]{1,0:T(8,128)(2,1)S(1)}, bf16[16,2048]{1,0:T(8,128)(2,1)S(1)}, u32[]{:S(2)}, u32[]{:S(2)}) collective-permute-start(bf16[16,2048]{1,0:T(8,128)(2,1)S(1)} %get-tuple-element.68), channel_id=1, source_target_pairs={{0,16},{8,24},{16,0},{24,8},{1,17},{9,25},{17,1},{25,9},{2,18},{10... | collective-permute-start | bytes 196616 | tf_op jit(solution)/shard_map/ppermute | solution.py:28
  120.7 1.4 collective-permute-done.22
  122.1 2.1 %collective-permute-done.21 = bf16[16,2048]{1,0:T(8,128)(2,1)S(1)} collective-permute-done((bf16[16,2048]{1,0:T(8,128)(2,1)S(1)}, bf16[16,2048]{1,0:T(8,128)(2,1)S(1)}, u32[]{:S(2)}, u32[]{:S(2)}) %collective-permute-start.21) | collective-permute-done | bytes 65568 | tf_op jit(solution)/shard_map/ppermute | solution.py:28
  125.5 2.2 %collective-permute-start.24 = (bf16[16,2048]{1,0:T(8,128)(2,1)S(1)}, bf16[16,2048]{1,0:T(8,128)(2,1)S(1)}, u32[]{:S(2)}, u32[]{:S(2)}) collective-permute-start(bf16[16,2048]{1,0:T(8,128)(2,1)S(1)} %add_convert_fusion.a), channel_id=1, source_target_pairs={{0,2},{1,3},{2,0},{3,1},{4,6},{5,7},{6,4},{7,5},{8,10},{9,11},{10,... | collective-permute-start | bytes 196616 | tf_op jit(solution)/shard_map/ppermute | solution.py:28
  127.7 2.3 %collective-permute-start.25 = (bf16[16,2048]{1,0:T(8,128)(2,1)S(1)}, bf16[16,2048]{1,0:T(8,128)(2,1)S(1)}, u32[]{:S(2)}, u32[]{:S(2)}) collective-permute-start(bf16[16,2048]{1,0:T(8,128)(2,1)S(1)} %add_convert_fusion.a), channel_id=1, source_target_pairs={{0,3},{1,0},{2,1},{3,2},{4,7},{5,4},{6,5},{7,6},{8,11},{9,8},{10,9... | collective-permute-start | bytes 196616 | tf_op jit(solution)/shard_map/ppermute | solution.py:28
  132.6 2.9 %collective-permute-start.27 = (bf16[16,2048]{1,0:T(8,128)(2,1)S(1)}, bf16[16,2048]{1,0:T(8,128)(2,1)S(1)}, u32[]{:S(2)}, u32[]{:S(2)}) collective-permute-start(bf16[16,2048]{1,0:T(8,128)(2,1)S(1)} %get-tuple-element.71.refs_0_), channel_id=1, source_target_pairs={{0,16},{8,24},{16,0},{24,8},{1,17},{9,25},{17,1},{25,9},{2,18},{10... | collective-permute-start | bytes 196616 | tf_op jit(solution)/shard_map/ppermute | solution.py:28
  140.3 4.1 %shard_map.128 = bf16[16,16,512]{2,1,0:T(8,128)(2,1)} custom-call(bf16[16,2048]{1,0:T(8,128)(2,1)} %copy-done.4, bf16[16,2048]{1,0:T(8,128)(2,1)} %copy-done.11, bf16[16,2048]{1,0:T(8,128)(2,1)} %copy-done.12, bf16[16,2048]{1,0:T(8,128)(2,1)} %copy-done.13, bf16[8,2,4,32,768]{4,3,2,1,0:T(8,128)(2,1)} %bitcast.31), custom_call_target="tpu_custom_call" | custom-call | flops 1 | bytes 1 | tf_op jit(solution)/shard_map/pallas_call | solution.py:446
  144.4 13.7 %all_to_all.21 = bf16[16,16,512]{2,1,0:T(8,128)(2,1)S(1)} all-to-all(bf16[16,16,512]{2,1,0:T(8,128)(2,1)} %shard_map.128), channel_id=1, replica_groups=mesh['z'=8,'x'=4,'core'=2,'tp'=4] {'x','tp'}, dimensions={0} | all-to-all | bytes 524288 | tf_op jit(solution)/shard_map/all_to_all | solution.py:519
  (95 shorter events, 23.6 us)
Async XLA Ops:
  6.5 64.9 %all-gather.5.cloned.1.call-start = ((), (), s32[]{:S(2)}) async-start(), calls=%async_computation.4 | async-start | bytes 2228224 | tf_op jit(solution)/shard_map/all_gather | solution.py:490
  8.5 8.5 %collective-permute-start.5 = (bf16[32,1280]{1,0:T(8,128)(2,1)}, bf16[32,1280]{1,0:T(8,128)(2,1)S(1)}, u32[]{:S(2)}, u32[]{:S(2)}) collective-permute-start(bf16[32,1280]{1,0:T(8,128)(2,1)} %get-tuple-element.45), channel_id=1, source_target_pairs={{0,24},{8,0},{16,8},{24,16},{1,25},{9,1},{17,9},{25,17},{2,26},{10... | collective-permute-start | bytes 245768 | tf_op jit(solution)/shard_map/ppermute | solution.py:28
  11.3 13.4 %collective-permute-start = (bf16[272,512]{1,0:T(8,128)(2,1)}, bf16[272,512]{1,0:T(8,128)(2,1)S(1)}, u32[]{:S(2)}, u32[]{:S(2)}) collective-permute-start(bf16[272,512]{1,0:T(8,128)(2,1)} %get-tuple-element.47.refs_0_), channel_id=1, source_target_pairs={{0,1},{1,2},{2,3},{3,0},{4,5},{5,6},{6,7},{7,4},{8,9},{9,10},{10,1... | collective-permute-start | bytes 835592 | tf_op jit(solution)/shard_map/ppermute | solution.py:28
  12.9 11.8 %collective-permute-start.1 = (bf16[272,512]{1,0:T(8,128)(2,1)}, bf16[272,512]{1,0:T(8,128)(2,1)S(1)}, u32[]{:S(2)}, u32[]{:S(2)}) collective-permute-start(bf16[272,512]{1,0:T(8,128)(2,1)} %get-tuple-element.47.refs_0_), channel_id=1, source_target_pairs={{0,2},{1,3},{2,0},{3,1},{4,6},{5,7},{6,4},{7,5},{8,10},{9,11},{10,... | collective-permute-start | bytes 835592 | tf_op jit(solution)/shard_map/ppermute | solution.py:28
  13.8 13.8 %collective-permute-start.2 = (bf16[272,512]{1,0:T(8,128)(2,1)}, bf16[272,512]{1,0:T(8,128)(2,1)S(1)}, u32[]{:S(2)}, u32[]{:S(2)}) collective-permute-start(bf16[272,512]{1,0:T(8,128)(2,1)} %get-tuple-element.47.refs_0_), channel_id=1, source_target_pairs={{0,3},{1,0},{2,1},{3,2},{4,7},{5,4},{6,5},{7,6},{8,11},{9,8},{10,9... | collective-permute-start | bytes 835592 | tf_op jit(solution)/shard_map/ppermute | solution.py:28
  16.2 6.2 %collective-permute-start.4 = (bf16[32,1280]{1,0:T(8,128)(2,1)}, bf16[32,1280]{1,0:T(8,128)(2,1)S(1)}, u32[]{:S(2)}, u32[]{:S(2)}) collective-permute-start(bf16[32,1280]{1,0:T(8,128)(2,1)} %get-tuple-element.44), channel_id=1, source_target_pairs={{0,16},{8,24},{16,0},{24,8},{1,17},{9,25},{17,1},{25,9},{2,18},{10... | collective-permute-start | bytes 245768 | tf_op jit(solution)/shard_map/ppermute | solution.py:28
  17.0 6.2 %collective-permute-start.3 = (bf16[32,1280]{1,0:T(8,128)(2,1)}, bf16[32,1280]{1,0:T(8,128)(2,1)S(1)}, u32[]{:S(2)}, u32[]{:S(2)}) collective-permute-start(bf16[32,1280]{1,0:T(8,128)(2,1)} %get-tuple-element.43), channel_id=1, source_target_pairs={{0,8},{8,16},{16,24},{24,0},{1,9},{9,17},{17,25},{25,1},{2,10},{10... | collective-permute-start | bytes 245768 | tf_op jit(solution)/shard_map/ppermute | solution.py:28
  35.2 14.8 %collective-permute-start.6 = (bf16[2,256,128]{2,1,0:T(8,128)(2,1)}, bf16[2,256,128]{2,1,0:T(8,128)(2,1)S(1)}, u32[]{:S(2)}, u32[]{:S(2)}) collective-permute-start(bf16[2,256,128]{2,1,0:T(8,128)(2,1)} %get-tuple-element.52), channel_id=1, source_target_pairs={{0,8},{8,16},{16,24},{24,0},{1,9},{9,17},{17,25},{25,1},{2,10},{10... | collective-permute-start | bytes 393224 | tf_op jit(solution)/shard_map/ppermute | solution.py:28
  35.2 15.3 %collective-permute-start.7 = (bf16[2,256,128]{2,1,0:T(8,128)(2,1)}, bf16[2,256,128]{2,1,0:T(8,128)(2,1)S(1)}, u32[]{:S(2)}, u32[]{:S(2)}) collective-permute-start(bf16[2,256,128]{2,1,0:T(8,128)(2,1)} %get-tuple-element.53), channel_id=1, source_target_pairs={{0,16},{8,24},{16,0},{24,8},{1,17},{9,25},{17,1},{25,9},{2,18},{10... | collective-permute-start | bytes 393224 | tf_op jit(solution)/shard_map/ppermute | solution.py:28
  37.5 13.1 %collective-permute-start.8 = (bf16[2,256,128]{2,1,0:T(8,128)(2,1)}, bf16[2,256,128]{2,1,0:T(8,128)(2,1)S(1)}, u32[]{:S(2)}, u32[]{:S(2)}) collective-permute-start(bf16[2,256,128]{2,1,0:T(8,128)(2,1)} %get-tuple-element.54), channel_id=1, source_target_pairs={{0,24},{8,0},{16,8},{24,16},{1,25},{9,1},{17,9},{25,17},{2,26},{10... | collective-permute-start | bytes 393224 | tf_op jit(solution)/shard_map/ppermute | solution.py:28
  38.7 22.6 %all-to-all-start = ((bf16[32,16,128]{2,1,0:T(8,128)(2,1)}), bf16[32,16,128]{2,1,0:T(8,128)(2,1)S(1)}, u32[]{:S(2)}, u32[]{:S(2)}) async-start(bf16[32,16,128]{2,1,0:T(8,128)(2,1)} %get-tuple-element.46), calls=%async_computation | async-start | bytes 262144 | tf_op jit(solution)/shard_map/all_to_all | solution.py:489
  50.0 1.6 collective-permute-start.9
  50.0 11.2 %collective-permute-start.10 = (bf16[2,256,128]{2,1,0:T(8,128)(2,1)S(1)}, bf16[2,256,128]{2,1,0:T(8,128)(2,1)S(1)}, u32[]{:S(2)}, u32[]{:S(2)}) collective-permute-start(bf16[2,256,128]{2,1,0:T(8,128)(2,1)S(1)} %collective-permute-done.6.refs_1_), channel_id=1, source_target_pairs={{0,4},{4,0},{1,5},{5,1},{2,6},{6,2},{3,7},{7,3},{8,12},{12,8},{9,1... | collective-permute-start | bytes 393224 | tf_op jit(solution)/shard_map/ppermute | solution.py:28
  50.5 10.7 %collective-permute-start.11 = (bf16[2,256,128]{2,1,0:T(8,128)(2,1)S(1)}, bf16[2,256,128]{2,1,0:T(8,128)(2,1)S(1)}, u32[]{:S(2)}, u32[]{:S(2)}) collective-permute-start(bf16[2,256,128]{2,1,0:T(8,128)(2,1)S(1)} %collective-permute-done.7.refs_2_), channel_id=1, source_target_pairs={{0,4},{4,0},{1,5},{5,1},{2,6},{6,2},{3,7},{7,3},{8,12},{12,8},{9,1... | collective-permute-start | bytes 393224 | tf_op jit(solution)/shard_map/ppermute | solution.py:28
  50.6 10.6 %collective-permute-start.12 = (bf16[2,256,128]{2,1,0:T(8,128)(2,1)S(1)}, bf16[2,256,128]{2,1,0:T(8,128)(2,1)S(1)}, u32[]{:S(2)}, u32[]{:S(2)}) collective-permute-start(bf16[2,256,128]{2,1,0:T(8,128)(2,1)S(1)} %collective-permute-done.8.refs_3_), channel_id=1, source_target_pairs={{0,4},{4,0},{1,5},{5,1},{2,6},{6,2},{3,7},{7,3},{8,12},{12,8},{9,1... | collective-permute-start | bytes 393224 | tf_op jit(solution)/shard_map/ppermute | solution.py:28
  66.6 15.6 %all-to-all-start.1 = ((bf16[32,16,256]{2,1,0:T(8,128)(2,1)}), bf16[32,16,256]{2,1,0:T(8,128)(2,1)S(1)}, u32[]{:S(2)}, u32[]{:S(2)}) async-start(bf16[32,16,256]{2,1,0:T(8,128)(2,1)} %bitcast.8), calls=%async_computation.1 | async-start | bytes 524288 | tf_op jit(solution)/shard_map/all_to_all | solution.py:499
  70.5 69.2 %all-gather.7.cloned.1.call-start = ((), (), s32[]{:S(2)}) async-start(), calls=%async_computation.5 | async-start | bytes 3342336 | tf_op jit(solution)/shard_map/all_gather | solution.py:504
  83.0 4.3 %collective-permute-start.13 = (bf16[16,2048]{1,0:T(8,128)(2,1)S(1)}, bf16[16,2048]{1,0:T(8,128)(2,1)S(1)}, u32[]{:S(2)}, u32[]{:S(2)}) collective-permute-start(bf16[16,2048]{1,0:T(8,128)(2,1)S(1)} %shard_map.123.a), channel_id=1, source_target_pairs={{0,1},{1,2},{2,3},{3,0},{4,5},{5,6},{6,7},{7,4},{8,9},{9,10},{10,1... | collective-permute-start | bytes 196616 | tf_op jit(solution)/shard_map/ppermute | solution.py:28
  84.5 5.9 %collective-permute-start.14 = (bf16[16,2048]{1,0:T(8,128)(2,1)S(1)}, bf16[16,2048]{1,0:T(8,128)(2,1)S(1)}, u32[]{:S(2)}, u32[]{:S(2)}) collective-permute-start(bf16[16,2048]{1,0:T(8,128)(2,1)S(1)} %shard_map.123.a), channel_id=1, source_target_pairs={{0,2},{1,3},{2,0},{3,1},{4,6},{5,7},{6,4},{7,5},{8,10},{9,11},{10,... | collective-permute-start | bytes 196616 | tf_op jit(solution)/shard_map/ppermute | solution.py:28
  86.0 5.0 %collective-permute-start.15 = (bf16[16,2048]{1,0:T(8,128)(2,1)S(1)}, bf16[16,2048]{1,0:T(8,128)(2,1)S(1)}, u32[]{:S(2)}, u32[]{:S(2)}) collective-permute-start(bf16[16,2048]{1,0:T(8,128)(2,1)S(1)} %shard_map.123.a), channel_id=1, source_target_pairs={{0,3},{1,0},{2,1},{3,2},{4,7},{5,4},{6,5},{7,6},{8,11},{9,8},{10,9... | collective-permute-start | bytes 196616 | tf_op jit(solution)/shard_map/ppermute | solution.py:28
  91.1 6.3 %collective-permute-start.16 = (bf16[16,2048]{1,0:T(8,128)(2,1)S(1)}, bf16[16,2048]{1,0:T(8,128)(2,1)S(1)}, u32[]{:S(2)}, u32[]{:S(2)}) collective-permute-start(bf16[16,2048]{1,0:T(8,128)(2,1)S(1)} %get-tuple-element.61.refs_0_), channel_id=1, source_target_pairs={{0,8},{8,16},{16,24},{24,0},{1,9},{9,17},{17,25},{25,1},{2,10},{10... | collective-permute-start | bytes 196616 | tf_op jit(solution)/shard_map/ppermute | solution.py:28
  91.2 6.2 %collective-permute-start.17 = (bf16[16,2048]{1,0:T(8,128)(2,1)S(1)}, bf16[16,2048]{1,0:T(8,128)(2,1)S(1)}, u32[]{:S(2)}, u32[]{:S(2)}) collective-permute-start(bf16[16,2048]{1,0:T(8,128)(2,1)S(1)} %get-tuple-element.61.refs_0_), channel_id=1, source_target_pairs={{0,16},{8,24},{16,0},{24,8},{1,17},{9,25},{17,1},{25,9},{2,18},{10... | collective-permute-start | bytes 196616 | tf_op jit(solution)/shard_map/ppermute | solution.py:28
  93.8 4.4 %collective-permute-start.18 = (bf16[16,2048]{1,0:T(8,128)(2,1)S(1)}, bf16[16,2048]{1,0:T(8,128)(2,1)S(1)}, u32[]{:S(2)}, u32[]{:S(2)}) collective-permute-start(bf16[16,2048]{1,0:T(8,128)(2,1)S(1)} %get-tuple-element.61.refs_0_), channel_id=1, source_target_pairs={{0,24},{8,0},{16,8},{24,16},{1,25},{9,1},{17,9},{25,17},{2,26},{10... | collective-permute-start | bytes 196616 | tf_op jit(solution)/shard_map/ppermute | solution.py:28
  116.5 5.6 %collective-permute-start.22 = (bf16[16,2048]{1,0:T(8,128)(2,1)S(1)}, bf16[16,2048]{1,0:T(8,128)(2,1)S(1)}, u32[]{:S(2)}, u32[]{:S(2)}) collective-permute-start(bf16[16,2048]{1,0:T(8,128)(2,1)S(1)} %get-tuple-element.69), channel_id=1, source_target_pairs={{0,8},{8,16},{16,24},{24,0},{1,9},{9,17},{17,25},{25,1},{2,10},{10... | collective-permute-start | bytes 196616 | tf_op jit(solution)/shard_map/ppermute | solution.py:28
  116.9 7.3 %collective-permute-start.21 = (bf16[16,2048]{1,0:T(8,128)(2,1)S(1)}, bf16[16,2048]{1,0:T(8,128)(2,1)S(1)}, u32[]{:S(2)}, u32[]{:S(2)}) collective-permute-start(bf16[16,2048]{1,0:T(8,128)(2,1)S(1)} %get-tuple-element.68), channel_id=1, source_target_pairs={{0,16},{8,24},{16,0},{24,8},{1,17},{9,25},{17,1},{25,9},{2,18},{10... | collective-permute-start | bytes 196616 | tf_op jit(solution)/shard_map/ppermute | solution.py:28
  120.7 4.3 %collective-permute-start.20 = (bf16[16,2048]{1,0:T(8,128)(2,1)S(1)}, bf16[16,2048]{1,0:T(8,128)(2,1)S(1)}, u32[]{:S(2)}, u32[]{:S(2)}) collective-permute-start(bf16[16,2048]{1,0:T(8,128)(2,1)S(1)} %get-tuple-element.67), channel_id=1, source_target_pairs={{0,24},{8,0},{16,8},{24,16},{1,25},{9,1},{17,9},{25,17},{2,26},{10... | collective-permute-start | bytes 196616 | tf_op jit(solution)/shard_map/ppermute | solution.py:28
  125.0 5.0 %collective-permute-start.23 = (bf16[16,2048]{1,0:T(8,128)(2,1)S(1)}, bf16[16,2048]{1,0:T(8,128)(2,1)S(1)}, u32[]{:S(2)}, u32[]{:S(2)}) collective-permute-start(bf16[16,2048]{1,0:T(8,128)(2,1)S(1)} %add_convert_fusion.a), channel_id=1, source_target_pairs={{0,1},{1,2},{2,3},{3,0},{4,5},{5,6},{6,7},{7,4},{8,9},{9,10},{10,1... | collective-permute-start | bytes 196616 | tf_op jit(solution)/shard_map/ppermute | solution.py:28
  125.5 5.8 %collective-permute-start.24 = (bf16[16,2048]{1,0:T(8,128)(2,1)S(1)}, bf16[16,2048]{1,0:T(8,128)(2,1)S(1)}, u32[]{:S(2)}, u32[]{:S(2)}) collective-permute-start(bf16[16,2048]{1,0:T(8,128)(2,1)S(1)} %add_convert_fusion.a), channel_id=1, source_target_pairs={{0,2},{1,3},{2,0},{3,1},{4,6},{5,7},{6,4},{7,5},{8,10},{9,11},{10,... | collective-permute-start | bytes 196616 | tf_op jit(solution)/shard_map/ppermute | solution.py:28
  127.7 4.3 %collective-permute-start.25 = (bf16[16,2048]{1,0:T(8,128)(2,1)S(1)}, bf16[16,2048]{1,0:T(8,128)(2,1)S(1)}, u32[]{:S(2)}, u32[]{:S(2)}) collective-permute-start(bf16[16,2048]{1,0:T(8,128)(2,1)S(1)} %add_convert_fusion.a), channel_id=1, source_target_pairs={{0,3},{1,0},{2,1},{3,2},{4,7},{5,4},{6,5},{7,6},{8,11},{9,8},{10,9... | collective-permute-start | bytes 196616 | tf_op jit(solution)/shard_map/ppermute | solution.py:28
  132.1 5.6 %collective-permute-start.26 = (bf16[16,2048]{1,0:T(8,128)(2,1)S(1)}, bf16[16,2048]{1,0:T(8,128)(2,1)S(1)}, u32[]{:S(2)}, u32[]{:S(2)}) collective-permute-start(bf16[16,2048]{1,0:T(8,128)(2,1)S(1)} %get-tuple-element.71.refs_0_), channel_id=1, source_target_pairs={{0,8},{8,16},{16,24},{24,0},{1,9},{9,17},{17,25},{25,1},{2,10},{10... | collective-permute-start | bytes 196616 | tf_op jit(solution)/shard_map/ppermute | solution.py:28
  132.6 5.8 %collective-permute-start.27 = (bf16[16,2048]{1,0:T(8,128)(2,1)S(1)}, bf16[16,2048]{1,0:T(8,128)(2,1)S(1)}, u32[]{:S(2)}, u32[]{:S(2)}) collective-permute-start(bf16[16,2048]{1,0:T(8,128)(2,1)S(1)} %get-tuple-element.71.refs_0_), channel_id=1, source_target_pairs={{0,16},{8,24},{16,0},{24,8},{1,17},{9,25},{17,1},{25,9},{2,18},{10... | collective-permute-start | bytes 196616 | tf_op jit(solution)/shard_map/ppermute | solution.py:28
  135.5 4.3 %collective-permute-start.28 = (bf16[16,2048]{1,0:T(8,128)(2,1)S(1)}, bf16[16,2048]{1,0:T(8,128)(2,1)S(1)}, u32[]{:S(2)}, u32[]{:S(2)}) collective-permute-start(bf16[16,2048]{1,0:T(8,128)(2,1)S(1)} %get-tuple-element.71.refs_0_), channel_id=1, source_target_pairs={{0,24},{8,0},{16,8},{24,16},{1,25},{9,1},{17,9},{25,17},{2,26},{10... | collective-permute-start | bytes 196616 | tf_op jit(solution)/shard_map/ppermute | solution.py:28
  (17 other events, 232.5 us)
Sparse Core Ops, SparseCore 0:
  31.0 40.2 all-gather.4
  82.4 38.8 all-gather.6

commit v6 on v5

--- a/solution.py
+++ b/solution.py
@@ -57,93 +57,82 @@
     return lax.rem(at + count - steps, count)
 
 
-def project_gathered(pieces, used, weight, body, out_shape):
-    first, last = used
-    rows, width = last - first, pieces[0].shape[1]
-    groups, _, cols = weight.shape
-
-    def kernel(*refs):
-        tp = lax.axis_index("tp")
-        piece_refs, weight_ref = refs[:TP], refs[TP]
-        out_refs = refs[TP + 1 : -5]
-        own_ref, held_ref, acc_ref, own_sems, sems = refs[-5:]
-        copies = {}
+def project_gathered(pieces, positions, w_query, w_keyval):
+    total, width = pieces[0].shape
+    rows = total - positions
+    groups, _, cols = w_keyval.shape
+    heads = cols // HD
+
+    def body(*refs):
+        piece_refs, query_weight_ref, keyval_weight_ref = refs[:TP], refs[TP], refs[TP + 1]
+        query_ref, whole_ref, *keyval_refs = refs[TP + 2 : -8]
+        own_ref, held_query_ref, held_keyval_ref, acc_query_ref, acc_keyval_ref = refs[-8:-3]
+        own_sems, query_sems, keyval_sems = refs[-3:]
+        x, tp = lax.axis_index("x"), lax.axis_index("tp")
+        columns = [
+            pl.ds(pl.multiple_of(behind(tp, k, TP) * width, width), width) for k in range(TP)
+        ]
+        own, query, keyval = {}, {}, {}
         for k in range(TP):
-            copies[k] = pltpu.make_async_copy(
-                piece_refs[k].at[pl.ds(first, rows), :], own_ref.at[k], own_sems.at[k]
+            own[k] = pltpu.make_async_copy(piece_refs[k], own_ref.at[k], own_sems.at[k])
+            own[k].start()
+            for g in range(groups):
+                keyval[k, g] = pltpu.make_async_copy(
+                    keyval_weight_ref.at[g, columns[k], :],
+                    held_keyval_ref.at[k, g],
+                    keyval_sems.at[k, g],
+                )
+                keyval[k, g].start()
+        for k in range(TP):
+            query[k] = pltpu.make_async_copy(
+                query_weight_ref.at[columns[k], :], held_query_ref.at[k], query_sems.at[k]
             )
-            copies[k].start()
-            at = pl.ds(pl.multiple_of(behind(tp, k, TP) * width, width), width)
+            query[k].start()
+        for k in range(TP):
+            own[k].wait()
+            piece = own_ref[k, :positions, :]
             for g in range(groups):
-                copies[k, g] = pltpu.make_async_copy(
-                    weight_ref.at[g, at, :], held_ref.at[k, g], sems.at[k, g]
-                )
-                copies[k, g].start()
+                keyval[k, g].wait()
+                term = jnp.dot(piece, held_keyval_ref[k, g], preferred_element_type=F32)
+                acc_keyval_ref[g] = term if k == 0 else acc_keyval_ref[g] + term
         for k in range(TP):
-            copies[k].wait()
-            piece = own_ref[k]
+            query[k].wait()
+            piece = own_ref[k, positions:, :]
+            whole_ref[:, columns[k]] = piece
+            term = jnp.dot(piece, held_query_ref[k], preferred_element_type=F32)
+            acc_query_ref[...] = term if k == 0 else acc_query_ref[...] + term
+        for k, ref in enumerate(keyval_refs):
+            head = pl.multiple_of(lax.rem(x + k, BREADTH) * HD, HD)
             for g in range(groups):
-                copies[k, g].wait()
-                term = jnp.dot(piece, held_ref[k, g], preferred_element_type=F32)
-                acc_ref[g] = term if k == 0 else acc_ref[g] + term
-        body(own_ref, acc_ref, out_refs)
+                ref[g] = acc_keyval_ref[g, :, pl.ds(head, HD)].astype(BF16)
+        for h in range(heads):
+            part = acc_query_ref[:, h * HD : (h + 1) * HD].astype(BF16)
+            for z in range(DEPTH):
+                query_ref[z * heads + h] = part
 
     vmem = pl.BlockSpec(memory_space=pltpu.VMEM)
-    return pl.pallas_call(
-        kernel,
-        in_specs=[pl.BlockSpec(memory_space=pl.ANY)] * (TP + 1),
+    out_shape = [
+        jax.ShapeDtypeStruct((DEPTH * heads, rows, HD), BF16),
+        jax.ShapeDtypeStruct((rows, TP * width), BF16),
+    ] + [jax.ShapeDtypeStruct((groups, positions, HD), BF16)] * BREADTH
+    return pl.pallas_call(
+        body,
+        in_specs=[pl.BlockSpec(memory_space=pl.ANY)] * (TP + 2),
         out_specs=[vmem] * len(out_shape),
         out_shape=out_shape,
         scratch_shapes=[
-            pltpu.VMEM((TP, rows, width), BF16),
+            pltpu.VMEM((TP, total, width), BF16),
+            pltpu.VMEM((TP, width, cols), BF16),
             pltpu.VMEM((TP, groups, width, cols), BF16),
-            pltpu.VMEM((groups, rows, cols), F32),
+            pltpu.VMEM((rows, cols), F32),
+            pltpu.VMEM((groups, positions, cols), F32),
+            pltpu.SemaphoreType.DMA((TP,)),
             pltpu.SemaphoreType.DMA((TP,)),
             pltpu.SemaphoreType.DMA((TP, groups)),
         ],
         compiler_params=params(58),
         cost_estimate=cost(),
-    )(*pieces, weight)
-
-
-def project_queries(pieces, used, weight):
-    first, last = used
-    rows, width = last - first, pieces[0].shape[1]
-    heads = weight.shape[1] // HD
-
-    def body(own_ref, acc_ref, out_refs):
-        tp = lax.axis_index("tp")
-        query_ref, whole_ref = out_refs
-        for k in range(TP):
-            at = behind(tp, k, TP)
-            columns = pl.ds(pl.multiple_of(at * width, width), width)
-            whole_ref[:, columns] = own_ref[k]
-        for h in range(heads):
-            query = acc_ref[0, :, h * HD : (h + 1) * HD].astype(BF16)
-            for z in range(DEPTH):
-                query_ref[z * heads + h] = query
-
-    out_shape = [
-        jax.ShapeDtypeStruct((DEPTH * heads, rows, HD), BF16),
-        jax.ShapeDtypeStruct((rows, TP * width), BF16),
-    ]
-    return project_gathered(pieces, used, weight[None], body, out_shape)
-
-
-def project_keyval(pieces, used, weight):
-    rows = used[1] - used[0]
-    groups, _, _ = weight.shape
-
-    def body(own_ref, acc_ref, out_refs):
-        x = lax.axis_index("x")
-        for k, ref in enumerate(out_refs):
-            head = lax.rem(x + k, BREADTH)
-            columns = pl.ds(pl.multiple_of(head * HD, HD), HD)
-            for g in range(groups):
-                ref[g] = acc_ref[g, :, columns].astype(BF16)
-
-    out_shape = [jax.ShapeDtypeStruct((groups, rows, HD), BF16)] * BREADTH
-    return project_gathered(pieces, used, weight, body, out_shape)
+    )(*pieces, w_query, w_keyval)
 
 
 def cross_partial(pos, queries, pieces):
@@ -275,6 +264,7 @@
         out_specs=[vmem] * (1 + len(widths)),
         out_shape=[jax.ShapeDtypeStruct((joined, features), BF16)]
         + [jax.ShapeDtypeStruct((depth, width), BF16) for width in widths],
+        compiler_params=params(58),
         cost_estimate=cost(),
     )(prefix, latent_in, w_self_qkv, w_self_out, w_gate_up, w_down)
 
@@ -454,7 +444,7 @@
             pltpu.VMEM((width, share), BF16),
             pltpu.SemaphoreType.DMA((2,)),
         ],
-        compiler_params=params(58),
+        compiler_params=params(32),
         cost_estimate=cost(),
     )(*normed, weight)
 
@@ -483,13 +473,11 @@
     head_rows = jnp.stack([heads[0]] + [piece[:, : 4 * HD] for piece in beside])
     unit_rows = jnp.stack([heads[1]] + [piece[:, 4 * HD :] for piece in beside])
 
-    used = (positions, positions + rows)
-    queries, latents = project_queries( pieces, used, w_query)
-    queries, pieces, head_rows = lax.optimization_barrier((queries, pieces, head_rows))
+    pieces, head_rows = lax.optimization_barrier((pieces, head_rows))
+    queries, latents, *keyval = project_gathered(pieces, positions, w_query, w_keyval)
     all_queries = lax.all_to_all(queries, ZX, 0, 0).reshape(chips * rows, HD)
     head_rows = lax.all_gather(head_rows, ("z", "core"), axis=0)
 
-    keyval = project_keyval( pieces, (0, positions), w_keyval)
     keyval = [keyval[0]] + [shifted(keyval[k], "x", k, BREADTH) for k in range(1, BREADTH)]
     keyval = keyval + [shifted(piece, "core", 1, CORES) for piece in keyval]
     pos = lax.dynamic_index_in_dim(

time: 166 us -> 164 us (0.988)
  Pallas kernels: 22.4 us -> 18.5 us
  starting transfers between devices: 50.5 us -> 52.4 us
    pallas_call x2 -> x1, Pallas kernels: 6.75 us -> 4.69 us  [project_gathered(): pl.pallas_call(body, in_specs=[pl.BlockSpec(memory_space=pl.ANY)] * (TP +...]
    ppermute x29, starting transfers between devices: 35.4 us -> 37.3 us  [shifted(): lax.ppermute(x, axis, [(i, (i + shift) % count) for i in range(count)])]
    pallas_call x1, Pallas kernels: 4.09 us -> 2.27 us  [mlp(): pl.pallas_call(body, in_specs=[vmem] * BREADTH + [pl.BlockSpec(memory_spa...]
    unnamed x32 -> x26, local copies, waits for them, and re-layouts: 2.26 us -> 3.49 us
  transfers between devices with their start and end apart: 33 -> 33, of which waited for: 20 -> 18; matrix products, arithmetic and copies ran while one was open for 1% -> 1% of each run, Pallas kernels for 8% -> 9%
where the time goes in v6:
time: 164 us; the launch traced here: 163 us
  starting transfers between devices  52.4 us (32%)
  waiting for transfers between devices  42.9 us (26%)
  blocking collectives  29 us (18%)
  Pallas kernels  18.5 us (11%)
  between operations  13.7 us (8%)
  local copies, waits for them, and re-layouts  3.74 us (2%)
  other arithmetic  2.81 us (2%)
    ppermute x29, starting transfers between devices, shifted(): lax.ppermute(x, axis, [(i, (i + shift) % count) for i in range(count)])  37.3 us
    ppermute x29, waiting for transfers between devices, shifted(): lax.ppermute(x, axis, [(i, (i + shift) % count) for i in range(count)])  26 us
    all_to_all x1, blocking collectives, local(): mine = lax.all_to_all(keyval, 'z', 0, 0).reshape(-1, keyval.shape[2])  15.3 us
    all_to_all x1, blocking collectives, local(): lax.all_to_all(mlp(group, split_cores(unit_rows)), ('x', 'tp'), 0, 0)  13.7 us
    all_to_all x1, starting transfers between devices, local(): all_queries = lax.all_to_all(queries, ZX, 0, 0).reshape(chips * rows, HD)  11 us
    all_to_all x1, waiting for transfers between devices, local(): all_queries = lax.all_to_all(queries, ZX, 0, 0).reshape(chips * rows, HD)  9.05 us
    all_to_all x1, waiting for transfers between devices, local(): partial = lax.all_to_all(partial.reshape(chips, rows, -1), ZX, 0, 0)  7.76 us
    pallas_call x1, Pallas kernels, project_gathered(): pl.pallas_call(body, in_specs=[pl.BlockSpec(memory_space=pl.ANY)] * (TP +...  4.69 us
  transfers between devices with their start and end apart: 33, of which 18 were waited for; matrix products, arithmetic and copies ran while one was open for 1% of the time, Pallas kernels for 9%

profile of v6, /device:TPU:8, one launch (start us, length us, event | category | flops | bytes accessed | tf_op | source)
XLA Modules:
  0.0 163.0 jit_solution(16726689753134308915)
XLA Ops:
  6.5 2.0 %shard_map.118 = (bf16[272,512]{1,0:T(8,128)(2,1)}, bf16[32,512]{1,0:T(8,128)(2,1)}, bf16[32,768]{1,0:T(8,128)(2,1)}, bf16[32,1280]{1,0:T(8,128)(2,1)}, bf16[32,...) custom-call(bf16[256,512]{1,0:T(8,128)(2,1)} %prefix_ref.1, bf16[16,512]{1,0:T(8,128)(2,1)} %latent_ref.1, ...), custom_call_target="tpu_custom_call" | custom-call | flops 1 | bytes 1 | tf_op jit(solution)/shard_map/pallas_call | solution.py:261
  8.5 2.8 %collective-permute-start.5 = (bf16[32,1280]{1,0:T(8,128)(2,1)}, bf16[32,1280]{1,0:T(8,128)(2,1)S(1)}, u32[]{:S(2)}, u32[]{:S(2)}) collective-permute-start(bf16[32,1280]{1,0:T(8,128)(2,1)} %get-tuple-element.42), channel_id=1, source_target_pairs={{0,24},{8,0},{16,8},{24,16},{1,25},{9,1},{17,9},{25,17},{2,26},{10... | collective-permute-start | bytes 245768 | tf_op jit(solution)/shard_map/ppermute | solution.py:28
  11.3 1.6 collective-permute-start
  13.8 2.4 %collective-permute-start.2 = (bf16[272,512]{1,0:T(8,128)(2,1)}, bf16[272,512]{1,0:T(8,128)(2,1)S(1)}, u32[]{:S(2)}, u32[]{:S(2)}) collective-permute-start(bf16[272,512]{1,0:T(8,128)(2,1)} %get-tuple-element.43.refs_0_), channel_id=1, source_target_pairs={{0,3},{1,0},{2,1},{3,2},{4,7},{5,4},{6,5},{7,6},{8,11},{9,8},{10,9... | collective-permute-start | bytes 835592 | tf_op jit(solution)/shard_map/ppermute | solution.py:28
  17.9 4.5 %collective-permute-done.4 = bf16[32,1280]{1,0:T(8,128)(2,1)S(1)} collective-permute-done((bf16[32,1280]{1,0:T(8,128)(2,1)}, bf16[32,1280]{1,0:T(8,128)(2,1)S(1)}, u32[]{:S(2)}, u32[]{:S(2)}) %collective-permute-start.4) | collective-permute-done | bytes 81952 | tf_op jit(solution)/shard_map/ppermute | solution.py:28
  23.2 1.4 pad_maximum_fusion.1
  24.7 2.9 %collective-permute-done.2.refs_3_ = bf16[272,512]{1,0:T(8,128)(2,1)S(1)} collective-permute-done((bf16[272,512]{1,0:T(8,128)(2,1)}, bf16[272,512]{1,0:T(8,128)(2,1)S(1)}, u32[]{:S(2)}, u32[]{:S(2)}) %collective-permute-start.2) | collective-permute-done | bytes 278560 | tf_op jit(solution)/shard_map/ppermute | solution.py:28
  28.3 4.7 %shard_map.119 = (bf16[32,16,128]{2,1,0:T(8,128)(2,1)}, bf16[16,2048]{1,0:T(8,128)(2,1)}, bf16[2,256,128]{2,1,0:T(8,128)(2,1)}, bf16[2,256,128]{2,1,0:T(8,128)(2...) custom-call(bf16[272,512]{1,0:T(8,128)(2,1)} %get-tuple-element.43.refs_0_, bf16[272,512]{1,0:T(8,128)(2,1)} %copy-done.8, ...), custom_call_target="tpu_custom_call" | custom-call | flops 1 | bytes 1 | tf_op jit(solution)/shard_map/pallas_call | solution.py:118
  33.1 2.3 %collective-permute-start.7 = (bf16[2,256,128]{2,1,0:T(8,128)(2,1)}, bf16[2,256,128]{2,1,0:T(8,128)(2,1)S(1)}, u32[]{:S(2)}, u32[]{:S(2)}) collective-permute-start(bf16[2,256,128]{2,1,0:T(8,128)(2,1)} %get-tuple-element.51), channel_id=1, source_target_pairs={{0,16},{8,24},{16,0},{24,8},{1,17},{9,25},{17,1},{25,9},{2,18},{10... | collective-permute-start | bytes 393224 | tf_op jit(solution)/shard_map/ppermute | solution.py:28
  36.5 11.0 %all-to-all-start = ((bf16[32,16,128]{2,1,0:T(8,128)(2,1)}), bf16[32,16,128]{2,1,0:T(8,128)(2,1)S(1)}, u32[]{:S(2)}, u32[]{:S(2)}) async-start(bf16[32,16,128]{2,1,0:T(8,128)(2,1)} %get-tuple-element.48), calls=%async_computation | async-start | bytes 262144 | tf_op jit(solution)/shard_map/all_to_all | solution.py:478
  49.4 9.0 %all-to-all-done = bf16[32,16,128]{2,1,0:T(8,128)(2,1)S(1)} async-done(((bf16[32,16,128]{2,1,0:T(8,128)(2,1)}), bf16[32,16,128]{2,1,0:T(8,128)(2,1)S(1)}, u32[]{:S(2)}, u32[]{:S(2)}) %all-to-all-start) | async-done | bytes 131104 | tf_op jit(solution)/shard_map/all_to_all | solution.py:478
  59.4 4.5 %shard_map.120 = bf16[512,256]{1,0:T(8,128)(2,1)} custom-call(s32[1,512]{1,0:T(1,128)S(1)} %reshape.26.pos_ref, bf16[512,128]{1,0:T(8,128)(2,1)S(1)} %bitcast.28, bf16[2,256,128]{2,1,0:T(8,128)(2,1)S(1)} %copy-done.4, bf16[2,256,128]{2,1,0:T(8,128)(2,1)S(1)} %collective-permute-done.6.refs_1_, bf16[2,256,128]{2,1,0:T(8,128)(2,1)S(1)} %collective-permute-done.7.refs_2_, ...), custom_call_target="tpu_custom_call" | custom-call | flops 1 | bytes 1 | tf_op jit(solution)/shard_map/pallas_call | solution.py:171
  63.9 3.9 %all-to-all-start.1 = ((bf16[32,16,256]{2,1,0:T(8,128)(2,1)}), bf16[32,16,256]{2,1,0:T(8,128)(2,1)S(1)}, u32[]{:S(2)}, u32[]{:S(2)}) async-start(bf16[32,16,256]{2,1,0:T(8,128)(2,1)} %bitcast.7), calls=%async_computation.1 | async-start | bytes 524288 | tf_op jit(solution)/shard_map/all_to_all | solution.py:487
  68.7 3.0 %shard_map.121 = (bf16[2048,384]{1,0:T(8,128)(2,1)}, bf16[2048,128]{1,0:T(8,128)(2,1)}) custom-call(bf16[8,2,4,32,512]{4,3,2,1,0:T(8,128)(2,1)} %bitcast.31), custom_call_target="tpu_custom_call" | custom-call | flops 1 | bytes 1 | tf_op jit(solution)/shard_map/pallas_call | solution.py:303
  71.7 7.8 %all-to-all-done.1 = bf16[32,16,256]{2,1,0:T(8,128)(2,1)S(1)} async-done(((bf16[32,16,256]{2,1,0:T(8,128)(2,1)}), bf16[32,16,256]{2,1,0:T(8,128)(2,1)S(1)}, u32[]{:S(2)}, u32[]{:S(2)}) %all-to-all-start.1) | async-done | bytes 262176 | tf_op jit(solution)/shard_map/all_to_all | solution.py:487
  80.2 2.3 %collective-permute-start.13 = (bf16[16,2048]{1,0:T(8,128)(2,1)S(1)}, bf16[16,2048]{1,0:T(8,128)(2,1)S(1)}, u32[]{:S(2)}, u32[]{:S(2)}) collective-permute-start(bf16[16,2048]{1,0:T(8,128)(2,1)S(1)} %shard_map.122.a), channel_id=1, source_target_pairs={{0,1},{1,2},{2,3},{3,0},{4,5},{5,6},{6,7},{7,4},{8,9},{9,10},{10,1... | collective-permute-start | bytes 196616 | tf_op jit(solution)/shard_map/ppermute | solution.py:28
  83.8 1.5 collective-permute-start.15
  85.3 3.1 %collective-permute-done.14.c = bf16[16,2048]{1,0:T(8,128)(2,1)S(1)} collective-permute-done((bf16[16,2048]{1,0:T(8,128)(2,1)S(1)}, bf16[16,2048]{1,0:T(8,128)(2,1)S(1)}, u32[]{:S(2)}, u32[]{:S(2)}) %collective-permute-start.14) | collective-permute-done | bytes 65568 | tf_op jit(solution)/shard_map/ppermute | solution.py:28
  89.0 2.6 %collective-permute-start.17 = (bf16[16,2048]{1,0:T(8,128)(2,1)S(1)}, bf16[16,2048]{1,0:T(8,128)(2,1)S(1)}, u32[]{:S(2)}, u32[]{:S(2)}) collective-permute-start(bf16[16,2048]{1,0:T(8,128)(2,1)S(1)} %get-tuple-element.59.refs_0_), channel_id=1, source_target_pairs={{0,16},{8,24},{16,0},{24,8},{1,17},{9,25},{17,1},{25,9},{2,18},{10... | collective-permute-start | bytes 196616 | tf_op jit(solution)/shard_map/ppermute | solution.py:28
  93.0 2.2 %collective-permute-done.16.refs_1_ = bf16[16,2048]{1,0:T(8,128)(2,1)S(1)} collective-permute-done((bf16[16,2048]{1,0:T(8,128)(2,1)S(1)}, bf16[16,2048]{1,0:T(8,128)(2,1)S(1)}, u32[]{:S(2)}, u32[]{:S(2)}) %collective-permute-start.16) | collective-permute-done | bytes 65568 | tf_op jit(solution)/shard_map/ppermute | solution.py:28
  96.4 15.3 %all_to_all.20 = bf16[8,64,256]{2,1,0:T(8,128)(2,1)S(1)} all-to-all(bf16[8,64,256]{2,1,0:T(8,128)(2,1)S(1)} %get-tuple-element.62), channel_id=1, replica_groups=mesh['z'=8,'x'=4,'core'=2,'tp'=4] {'z'}, dimensions={0} | all-to-all | bytes 524288 | tf_op jit(solution)/shard_map/all_to_all | solution.py:499
  111.7 1.6 collective-permute-done.19.other_ref
  114.1 1.4 collective-permute-start.22
  115.4 2.7 %collective-permute-start.21 = (bf16[16,2048]{1,0:T(8,128)(2,1)S(1)}, bf16[16,2048]{1,0:T(8,128)(2,1)S(1)}, u32[]{:S(2)}, u32[]{:S(2)}) collective-permute-start(bf16[16,2048]{1,0:T(8,128)(2,1)S(1)} %get-tuple-element.66), channel_id=1, source_target_pairs={{0,16},{8,24},{16,0},{24,8},{1,17},{9,25},{17,1},{25,9},{2,18},{10... | collective-permute-start | bytes 196616 | tf_op jit(solution)/shard_map/ppermute | solution.py:28
  119.6 2.0 %collective-permute-done.21 = bf16[16,2048]{1,0:T(8,128)(2,1)S(1)} collective-permute-done((bf16[16,2048]{1,0:T(8,128)(2,1)S(1)}, bf16[16,2048]{1,0:T(8,128)(2,1)S(1)}, u32[]{:S(2)}, u32[]{:S(2)}) %collective-permute-start.21) | collective-permute-done | bytes 65568 | tf_op jit(solution)/shard_map/ppermute | solution.py:28
  123.6 2.1 %collective-permute-start.24 = (bf16[16,2048]{1,0:T(8,128)(2,1)S(1)}, bf16[16,2048]{1,0:T(8,128)(2,1)S(1)}, u32[]{:S(2)}, u32[]{:S(2)}) collective-permute-start(bf16[16,2048]{1,0:T(8,128)(2,1)S(1)} %add_convert_fusion.a), channel_id=1, source_target_pairs={{0,2},{1,3},{2,0},{3,1},{4,6},{5,7},{6,4},{7,5},{8,10},{9,11},{10,... | collective-permute-start | bytes 196616 | tf_op jit(solution)/shard_map/ppermute | solution.py:28
  125.7 2.4 %collective-permute-start.25 = (bf16[16,2048]{1,0:T(8,128)(2,1)S(1)}, bf16[16,2048]{1,0:T(8,128)(2,1)S(1)}, u32[]{:S(2)}, u32[]{:S(2)}) collective-permute-start(bf16[16,2048]{1,0:T(8,128)(2,1)S(1)} %add_convert_fusion.a), channel_id=1, source_target_pairs={{0,3},{1,0},{2,1},{3,2},{4,7},{5,4},{6,5},{7,6},{8,11},{9,8},{10,9... | collective-permute-start | bytes 196616 | tf_op jit(solution)/shard_map/ppermute | solution.py:28
  130.4 3.0 %collective-permute-start.27 = (bf16[16,2048]{1,0:T(8,128)(2,1)S(1)}, bf16[16,2048]{1,0:T(8,128)(2,1)S(1)}, u32[]{:S(2)}, u32[]{:S(2)}) collective-permute-start(bf16[16,2048]{1,0:T(8,128)(2,1)S(1)} %get-tuple-element.69.refs_0_), channel_id=1, source_target_pairs={{0,16},{8,24},{16,0},{24,8},{1,17},{9,25},{17,1},{25,9},{2,18},{10... | collective-permute-start | bytes 196616 | tf_op jit(solution)/shard_map/ppermute | solution.py:28
  134.5 2.0 %collective-permute-done.26.refs_1_ = bf16[16,2048]{1,0:T(8,128)(2,1)S(1)} collective-permute-done((bf16[16,2048]{1,0:T(8,128)(2,1)S(1)}, bf16[16,2048]{1,0:T(8,128)(2,1)S(1)}, u32[]{:S(2)}, u32[]{:S(2)}) %collective-permute-start.26) | collective-permute-done | bytes 65568 | tf_op jit(solution)/shard_map/ppermute | solution.py:28
  137.6 1.9 %copy-done = bf16[64,32,768]{2,1,0:T(8,128)(2,1)S(1)} copy-done((bf16[64,32,768]{2,1,0:T(8,128)(2,1)S(1)}, bf16[64,32,768]{2,1,0:T(8,128)(2,1)}, u32[]{:S(2)}) %copy-start) | copy-done | bytes 3145752
  139.5 2.3 %shard_map.127 = bf16[16,16,512]{2,1,0:T(8,128)(2,1)S(1)} custom-call(bf16[16,2048]{1,0:T(8,128)(2,1)S(1)} %get-tuple-element.69.refs_0_, bf16[16,2048]{1,0:T(8,128)(2,1)S(1)} %collective-permute-done.26.refs_1_, bf16[16,2048]{1,0:T(8,128)(2,1)S(1)} %collective-permute-done.27.refs_2_, bf16[16,2048]{1,0:T(8,128)(2,1)S(1)} %collective-permute-done.28.refs_3_, ...), custom_call_target="tpu_custom_call" | custom-call | flops 1 | bytes 1 | tf_op jit(solution)/shard_map/pallas_call | solution.py:436
  141.8 13.7 %all_to_all.21 = bf16[16,16,512]{2,1,0:T(8,128)(2,1)S(1)} all-to-all(bf16[16,16,512]{2,1,0:T(8,128)(2,1)S(1)} %shard_map.127), channel_id=1, replica_groups=mesh['z'=8,'x'=4,'core'=2,'tp'=4] {'x','tp'}, dimensions={0} | all-to-all | bytes 524288 | tf_op jit(solution)/shard_map/all_to_all | solution.py:507
  (88 shorter events, 23.7 us)
Async XLA Ops:
  6.5 62.2 %all-gather.5.cloned.1.call-start = ((), (), s32[]{:S(2)}) async-start(), calls=%async_computation.4 | async-start | bytes 2228224 | tf_op jit(solution)/shard_map/all_gather | solution.py:479
  8.5 8.5 %collective-permute-start.5 = (bf16[32,1280]{1,0:T(8,128)(2,1)}, bf16[32,1280]{1,0:T(8,128)(2,1)S(1)}, u32[]{:S(2)}, u32[]{:S(2)}) collective-permute-start(bf16[32,1280]{1,0:T(8,128)(2,1)} %get-tuple-element.42), channel_id=1, source_target_pairs={{0,24},{8,0},{16,8},{24,16},{1,25},{9,1},{17,9},{25,17},{2,26},{10... | collective-permute-start | bytes 245768 | tf_op jit(solution)/shard_map/ppermute | solution.py:28
  11.3 13.4 %collective-permute-start = (bf16[272,512]{1,0:T(8,128)(2,1)}, bf16[272,512]{1,0:T(8,128)(2,1)S(1)}, u32[]{:S(2)}, u32[]{:S(2)}) collective-permute-start(bf16[272,512]{1,0:T(8,128)(2,1)} %get-tuple-element.43.refs_0_), channel_id=1, source_target_pairs={{0,1},{1,2},{2,3},{3,0},{4,5},{5,6},{6,7},{7,4},{8,9},{9,10},{10,1... | collective-permute-start | bytes 835592 | tf_op jit(solution)/shard_map/ppermute | solution.py:28
  12.8 11.8 %collective-permute-start.1 = (bf16[272,512]{1,0:T(8,128)(2,1)}, bf16[272,512]{1,0:T(8,128)(2,1)S(1)}, u32[]{:S(2)}, u32[]{:S(2)}) collective-permute-start(bf16[272,512]{1,0:T(8,128)(2,1)} %get-tuple-element.43.refs_0_), channel_id=1, source_target_pairs={{0,2},{1,3},{2,0},{3,1},{4,6},{5,7},{6,4},{7,5},{8,10},{9,11},{10,... | collective-permute-start | bytes 835592 | tf_op jit(solution)/shard_map/ppermute | solution.py:28
  13.8 13.8 %collective-permute-start.2 = (bf16[272,512]{1,0:T(8,128)(2,1)}, bf16[272,512]{1,0:T(8,128)(2,1)S(1)}, u32[]{:S(2)}, u32[]{:S(2)}) collective-permute-start(bf16[272,512]{1,0:T(8,128)(2,1)} %get-tuple-element.43.refs_0_), channel_id=1, source_target_pairs={{0,3},{1,0},{2,1},{3,2},{4,7},{5,4},{6,5},{7,6},{8,11},{9,8},{10,9... | collective-permute-start | bytes 835592 | tf_op jit(solution)/shard_map/ppermute | solution.py:28
  16.2 6.2 %collective-permute-start.4 = (bf16[32,1280]{1,0:T(8,128)(2,1)}, bf16[32,1280]{1,0:T(8,128)(2,1)S(1)}, u32[]{:S(2)}, u32[]{:S(2)}) collective-permute-start(bf16[32,1280]{1,0:T(8,128)(2,1)} %get-tuple-element.41), channel_id=1, source_target_pairs={{0,16},{8,24},{16,0},{24,8},{1,17},{9,25},{17,1},{25,9},{2,18},{10... | collective-permute-start | bytes 245768 | tf_op jit(solution)/shard_map/ppermute | solution.py:28
  17.0 6.2 %collective-permute-start.3 = (bf16[32,1280]{1,0:T(8,128)(2,1)}, bf16[32,1280]{1,0:T(8,128)(2,1)S(1)}, u32[]{:S(2)}, u32[]{:S(2)}) collective-permute-start(bf16[32,1280]{1,0:T(8,128)(2,1)} %get-tuple-element.40), channel_id=1, source_target_pairs={{0,8},{8,16},{16,24},{24,0},{1,9},{9,17},{17,25},{25,1},{2,10},{10... | collective-permute-start | bytes 245768 | tf_op jit(solution)/shard_map/ppermute | solution.py:28
  33.0 14.8 %collective-permute-start.6 = (bf16[2,256,128]{2,1,0:T(8,128)(2,1)}, bf16[2,256,128]{2,1,0:T(8,128)(2,1)S(1)}, u32[]{:S(2)}, u32[]{:S(2)}) collective-permute-start(bf16[2,256,128]{2,1,0:T(8,128)(2,1)} %get-tuple-element.50), channel_id=1, source_target_pairs={{0,8},{8,16},{16,24},{24,0},{1,9},{9,17},{17,25},{25,1},{2,10},{10... | collective-permute-start | bytes 393224 | tf_op jit(solution)/shard_map/ppermute | solution.py:28
  33.1 15.3 %collective-permute-start.7 = (bf16[2,256,128]{2,1,0:T(8,128)(2,1)}, bf16[2,256,128]{2,1,0:T(8,128)(2,1)S(1)}, u32[]{:S(2)}, u32[]{:S(2)}) collective-permute-start(bf16[2,256,128]{2,1,0:T(8,128)(2,1)} %get-tuple-element.51), channel_id=1, source_target_pairs={{0,16},{8,24},{16,0},{24,8},{1,17},{9,25},{17,1},{25,9},{2,18},{10... | collective-permute-start | bytes 393224 | tf_op jit(solution)/shard_map/ppermute | solution.py:28
  35.4 13.1 %collective-permute-start.8 = (bf16[2,256,128]{2,1,0:T(8,128)(2,1)}, bf16[2,256,128]{2,1,0:T(8,128)(2,1)S(1)}, u32[]{:S(2)}, u32[]{:S(2)}) collective-permute-start(bf16[2,256,128]{2,1,0:T(8,128)(2,1)} %get-tuple-element.52), channel_id=1, source_target_pairs={{0,24},{8,0},{16,8},{24,16},{1,25},{9,1},{17,9},{25,17},{2,26},{10... | collective-permute-start | bytes 393224 | tf_op jit(solution)/shard_map/ppermute | solution.py:28
  36.5 21.9 %all-to-all-start = ((bf16[32,16,128]{2,1,0:T(8,128)(2,1)}), bf16[32,16,128]{2,1,0:T(8,128)(2,1)S(1)}, u32[]{:S(2)}, u32[]{:S(2)}) async-start(bf16[32,16,128]{2,1,0:T(8,128)(2,1)} %get-tuple-element.48), calls=%async_computation | async-start | bytes 262144 | tf_op jit(solution)/shard_map/all_to_all | solution.py:478
  47.8 10.6 %collective-permute-start.10 = (bf16[2,256,128]{2,1,0:T(8,128)(2,1)S(1)}, bf16[2,256,128]{2,1,0:T(8,128)(2,1)S(1)}, u32[]{:S(2)}, u32[]{:S(2)}) collective-permute-start(bf16[2,256,128]{2,1,0:T(8,128)(2,1)S(1)} %collective-permute-done.6.refs_1_), channel_id=1, source_target_pairs={{0,4},{4,0},{1,5},{5,1},{2,6},{6,2},{3,7},{7,3},{8,12},{12,8},{9,1... | collective-permute-start | bytes 393224 | tf_op jit(solution)/shard_map/ppermute | solution.py:28
  48.3 10.1 %collective-permute-start.11 = (bf16[2,256,128]{2,1,0:T(8,128)(2,1)S(1)}, bf16[2,256,128]{2,1,0:T(8,128)(2,1)S(1)}, u32[]{:S(2)}, u32[]{:S(2)}) collective-permute-start(bf16[2,256,128]{2,1,0:T(8,128)(2,1)S(1)} %collective-permute-done.7.refs_2_), channel_id=1, source_target_pairs={{0,4},{4,0},{1,5},{5,1},{2,6},{6,2},{3,7},{7,3},{8,12},{12,8},{9,1... | collective-permute-start | bytes 393224 | tf_op jit(solution)/shard_map/ppermute | solution.py:28
  48.5 10.0 %collective-permute-start.12 = (bf16[2,256,128]{2,1,0:T(8,128)(2,1)S(1)}, bf16[2,256,128]{2,1,0:T(8,128)(2,1)S(1)}, u32[]{:S(2)}, u32[]{:S(2)}) collective-permute-start(bf16[2,256,128]{2,1,0:T(8,128)(2,1)S(1)} %collective-permute-done.8.refs_3_), channel_id=1, source_target_pairs={{0,4},{4,0},{1,5},{5,1},{2,6},{6,2},{3,7},{7,3},{8,12},{12,8},{9,1... | collective-permute-start | bytes 393224 | tf_op jit(solution)/shard_map/ppermute | solution.py:28
  63.9 15.6 %all-to-all-start.1 = ((bf16[32,16,256]{2,1,0:T(8,128)(2,1)}), bf16[32,16,256]{2,1,0:T(8,128)(2,1)S(1)}, u32[]{:S(2)}, u32[]{:S(2)}) async-start(bf16[32,16,256]{2,1,0:T(8,128)(2,1)} %bitcast.7), calls=%async_computation.1 | async-start | bytes 524288 | tf_op jit(solution)/shard_map/all_to_all | solution.py:487
  67.7 69.9 %all-gather.7.cloned.1.call-start = ((), (), s32[]{:S(2)}) async-start(), calls=%async_computation.5 | async-start | bytes 3342336 | tf_op jit(solution)/shard_map/all_gather | solution.py:492
  80.2 5.1 %collective-permute-start.13 = (bf16[16,2048]{1,0:T(8,128)(2,1)S(1)}, bf16[16,2048]{1,0:T(8,128)(2,1)S(1)}, u32[]{:S(2)}, u32[]{:S(2)}) collective-permute-start(bf16[16,2048]{1,0:T(8,128)(2,1)S(1)} %shard_map.122.a), channel_id=1, source_target_pairs={{0,1},{1,2},{2,3},{3,0},{4,5},{5,6},{6,7},{7,4},{8,9},{9,10},{10,1... | collective-permute-start | bytes 196616 | tf_op jit(solution)/shard_map/ppermute | solution.py:28
  82.5 5.9 %collective-permute-start.14 = (bf16[16,2048]{1,0:T(8,128)(2,1)S(1)}, bf16[16,2048]{1,0:T(8,128)(2,1)S(1)}, u32[]{:S(2)}, u32[]{:S(2)}) collective-permute-start(bf16[16,2048]{1,0:T(8,128)(2,1)S(1)} %shard_map.122.a), channel_id=1, source_target_pairs={{0,2},{1,3},{2,0},{3,1},{4,6},{5,7},{6,4},{7,5},{8,10},{9,11},{10,... | collective-permute-start | bytes 196616 | tf_op jit(solution)/shard_map/ppermute | solution.py:28
  83.8 5.0 %collective-permute-start.15 = (bf16[16,2048]{1,0:T(8,128)(2,1)S(1)}, bf16[16,2048]{1,0:T(8,128)(2,1)S(1)}, u32[]{:S(2)}, u32[]{:S(2)}) collective-permute-start(bf16[16,2048]{1,0:T(8,128)(2,1)S(1)} %shard_map.122.a), channel_id=1, source_target_pairs={{0,3},{1,0},{2,1},{3,2},{4,7},{5,4},{6,5},{7,6},{8,11},{9,8},{10,9... | collective-permute-start | bytes 196616 | tf_op jit(solution)/shard_map/ppermute | solution.py:28
  88.9 6.3 %collective-permute-start.16 = (bf16[16,2048]{1,0:T(8,128)(2,1)S(1)}, bf16[16,2048]{1,0:T(8,128)(2,1)S(1)}, u32[]{:S(2)}, u32[]{:S(2)}) collective-permute-start(bf16[16,2048]{1,0:T(8,128)(2,1)S(1)} %get-tuple-element.59.refs_0_), channel_id=1, source_target_pairs={{0,8},{8,16},{16,24},{24,0},{1,9},{9,17},{17,25},{25,1},{2,10},{10... | collective-permute-start | bytes 196616 | tf_op jit(solution)/shard_map/ppermute | solution.py:28
  89.0 6.2 %collective-permute-start.17 = (bf16[16,2048]{1,0:T(8,128)(2,1)S(1)}, bf16[16,2048]{1,0:T(8,128)(2,1)S(1)}, u32[]{:S(2)}, u32[]{:S(2)}) collective-permute-start(bf16[16,2048]{1,0:T(8,128)(2,1)S(1)} %get-tuple-element.59.refs_0_), channel_id=1, source_target_pairs={{0,16},{8,24},{16,0},{24,8},{1,17},{9,25},{17,1},{25,9},{2,18},{10... | collective-permute-start | bytes 196616 | tf_op jit(solution)/shard_map/ppermute | solution.py:28
  91.6 4.4 %collective-permute-start.18 = (bf16[16,2048]{1,0:T(8,128)(2,1)S(1)}, bf16[16,2048]{1,0:T(8,128)(2,1)S(1)}, u32[]{:S(2)}, u32[]{:S(2)}) collective-permute-start(bf16[16,2048]{1,0:T(8,128)(2,1)S(1)} %get-tuple-element.59.refs_0_), channel_id=1, source_target_pairs={{0,24},{8,0},{16,8},{24,16},{1,25},{9,1},{17,9},{25,17},{2,26},{10... | collective-permute-start | bytes 196616 | tf_op jit(solution)/shard_map/ppermute | solution.py:28
  111.7 1.6 collective-permute-start.19
  114.1 5.6 %collective-permute-start.22 = (bf16[16,2048]{1,0:T(8,128)(2,1)S(1)}, bf16[16,2048]{1,0:T(8,128)(2,1)S(1)}, u32[]{:S(2)}, u32[]{:S(2)}) collective-permute-start(bf16[16,2048]{1,0:T(8,128)(2,1)S(1)} %get-tuple-element.67), channel_id=1, source_target_pairs={{0,8},{8,16},{16,24},{24,0},{1,9},{9,17},{17,25},{25,1},{2,10},{10... | collective-permute-start | bytes 196616 | tf_op jit(solution)/shard_map/ppermute | solution.py:28
  115.4 6.2 %collective-permute-start.21 = (bf16[16,2048]{1,0:T(8,128)(2,1)S(1)}, bf16[16,2048]{1,0:T(8,128)(2,1)S(1)}, u32[]{:S(2)}, u32[]{:S(2)}) collective-permute-start(bf16[16,2048]{1,0:T(8,128)(2,1)S(1)} %get-tuple-element.66), channel_id=1, source_target_pairs={{0,16},{8,24},{16,0},{24,8},{1,17},{9,25},{17,1},{25,9},{2,18},{10... | collective-permute-start | bytes 196616 | tf_op jit(solution)/shard_map/ppermute | solution.py:28
  118.2 4.3 %collective-permute-start.20 = (bf16[16,2048]{1,0:T(8,128)(2,1)S(1)}, bf16[16,2048]{1,0:T(8,128)(2,1)S(1)}, u32[]{:S(2)}, u32[]{:S(2)}) collective-permute-start(bf16[16,2048]{1,0:T(8,128)(2,1)S(1)} %get-tuple-element.65), channel_id=1, source_target_pairs={{0,24},{8,0},{16,8},{24,16},{1,25},{9,1},{17,9},{25,17},{2,26},{10... | collective-permute-start | bytes 196616 | tf_op jit(solution)/shard_map/ppermute | solution.py:28
  122.5 5.7 %collective-permute-start.23 = (bf16[16,2048]{1,0:T(8,128)(2,1)S(1)}, bf16[16,2048]{1,0:T(8,128)(2,1)S(1)}, u32[]{:S(2)}, u32[]{:S(2)}) collective-permute-start(bf16[16,2048]{1,0:T(8,128)(2,1)S(1)} %add_convert_fusion.a), channel_id=1, source_target_pairs={{0,1},{1,2},{2,3},{3,0},{4,5},{5,6},{6,7},{7,4},{8,9},{9,10},{10,1... | collective-permute-start | bytes 196616 | tf_op jit(solution)/shard_map/ppermute | solution.py:28
  123.6 5.8 %collective-permute-start.24 = (bf16[16,2048]{1,0:T(8,128)(2,1)S(1)}, bf16[16,2048]{1,0:T(8,128)(2,1)S(1)}, u32[]{:S(2)}, u32[]{:S(2)}) collective-permute-start(bf16[16,2048]{1,0:T(8,128)(2,1)S(1)} %add_convert_fusion.a), channel_id=1, source_target_pairs={{0,2},{1,3},{2,0},{3,1},{4,6},{5,7},{6,4},{7,5},{8,10},{9,11},{10,... | collective-permute-start | bytes 196616 | tf_op jit(solution)/shard_map/ppermute | solution.py:28
  125.7 4.4 %collective-permute-start.25 = (bf16[16,2048]{1,0:T(8,128)(2,1)S(1)}, bf16[16,2048]{1,0:T(8,128)(2,1)S(1)}, u32[]{:S(2)}, u32[]{:S(2)}) collective-permute-start(bf16[16,2048]{1,0:T(8,128)(2,1)S(1)} %add_convert_fusion.a), channel_id=1, source_target_pairs={{0,3},{1,0},{2,1},{3,2},{4,7},{5,4},{6,5},{7,6},{8,11},{9,8},{10,9... | collective-permute-start | bytes 196616 | tf_op jit(solution)/shard_map/ppermute | solution.py:28
  130.2 6.3 %collective-permute-start.26 = (bf16[16,2048]{1,0:T(8,128)(2,1)S(1)}, bf16[16,2048]{1,0:T(8,128)(2,1)S(1)}, u32[]{:S(2)}, u32[]{:S(2)}) collective-permute-start(bf16[16,2048]{1,0:T(8,128)(2,1)S(1)} %get-tuple-element.69.refs_0_), channel_id=1, source_target_pairs={{0,8},{8,16},{16,24},{24,0},{1,9},{9,17},{17,25},{25,1},{2,10},{10... | collective-permute-start | bytes 196616 | tf_op jit(solution)/shard_map/ppermute | solution.py:28
  130.4 6.1 %collective-permute-start.27 = (bf16[16,2048]{1,0:T(8,128)(2,1)S(1)}, bf16[16,2048]{1,0:T(8,128)(2,1)S(1)}, u32[]{:S(2)}, u32[]{:S(2)}) collective-permute-start(bf16[16,2048]{1,0:T(8,128)(2,1)S(1)} %get-tuple-element.69.refs_0_), channel_id=1, source_target_pairs={{0,16},{8,24},{16,0},{24,8},{1,17},{9,25},{17,1},{25,9},{2,18},{10... | collective-permute-start | bytes 196616 | tf_op jit(solution)/shard_map/ppermute | solution.py:28
  133.4 4.3 %collective-permute-start.28 = (bf16[16,2048]{1,0:T(8,128)(2,1)S(1)}, bf16[16,2048]{1,0:T(8,128)(2,1)S(1)}, u32[]{:S(2)}, u32[]{:S(2)}) collective-permute-start(bf16[16,2048]{1,0:T(8,128)(2,1)S(1)} %get-tuple-element.69.refs_0_), channel_id=1, source_target_pairs={{0,24},{8,0},{16,8},{24,16},{1,25},{9,1},{17,9},{25,17},{2,26},{10... | collective-permute-start | bytes 196616 | tf_op jit(solution)/shard_map/ppermute | solution.py:28
  (14 other events, 225.7 us)
Sparse Core Ops, SparseCore 0:
  27.7 40.2 all-gather.4
  79.6 39.7 all-gather.6

commit v7 on v6

--- a/solution.py
+++ b/solution.py
@@ -138,7 +138,7 @@
 def cross_partial(pos, queries, pieces):
     count = queries.shape[0]
     positions = pieces[0].shape[1]
-    rows = 128
+    rows = 256
 
     def body(pos_ref, q_ref, *refs):
         piece_refs, out_ref, stat_ref = refs[: len(pieces)], refs[-2], refs[-1]

time: 164 us -> 163 us (level)
  no operation moved by 1% of the time
where the time goes in v7:
time: 163 us
  starting transfers between devices  52.8 us (32%)
  waiting for transfers between devices  42.5 us (26%)
  blocking collectives  28.9 us (18%)
  Pallas kernels  18.3 us (11%)
  between operations  13.7 us (8%)
  local copies, waits for them, and re-layouts  3.74 us (2%)
  other arithmetic  2.81 us (2%)
    ppermute x29, starting transfers between devices, shifted(): lax.ppermute(x, axis, [(i, (i + shift) % count) for i in range(count)])  37.9 us
    ppermute x29, waiting for transfers between devices, shifted(): lax.ppermute(x, axis, [(i, (i + shift) % count) for i in range(count)])  25.4 us
    all_to_all x1, blocking collectives, local(): mine = lax.all_to_all(keyval, 'z', 0, 0).reshape(-1, keyval.shape[2])  15.3 us
    all_to_all x1, blocking collectives, local(): lax.all_to_all(mlp(group, split_cores(unit_rows)), ('x', 'tp'), 0, 0)  13.7 us
    all_to_all x1, starting transfers between devices, local(): all_queries = lax.all_to_all(queries, ZX, 0, 0).reshape(chips * rows, HD)  11 us
    all_to_all x1, waiting for transfers between devices, local(): all_queries = lax.all_to_all(queries, ZX, 0, 0).reshape(chips * rows, HD)  9.05 us
    all_to_all x1, waiting for transfers between devices, local(): partial = lax.all_to_all(partial.reshape(chips, rows, -1), ZX, 0, 0)  8 us
    pallas_call x1, Pallas kernels, project_gathered(): pl.pallas_call(body, in_specs=[pl.BlockSpec(memory_space=pl.ANY)] * (TP +...  4.69 us
  transfers between devices with their start and end apart: 33, of which 18 were waited for; matrix products, arithmetic and copies ran while one was open for 1% of the time, Pallas kernels for 9%

profile of v7, /device:TPU:8, one launch (start us, length us, event | category | flops | bytes accessed | tf_op | source)
XLA Modules:
  0.0 162.7 jit_solution(6372785135555752652)
XLA Ops:
  6.5 2.0 %shard_map.118 = (bf16[272,512]{1,0:T(8,128)(2,1)}, bf16[32,512]{1,0:T(8,128)(2,1)}, bf16[32,768]{1,0:T(8,128)(2,1)}, bf16[32,1280]{1,0:T(8,128)(2,1)}, bf16[32,...) custom-call(bf16[256,512]{1,0:T(8,128)(2,1)} %prefix_ref.1, bf16[16,512]{1,0:T(8,128)(2,1)} %latent_ref.1, ...), custom_call_target="tpu_custom_call" | custom-call | flops 1 | bytes 1 | tf_op jit(solution)/shard_map/pallas_call | solution.py:261
  8.5 2.8 %collective-permute-start.5 = (bf16[32,1280]{1,0:T(8,128)(2,1)}, bf16[32,1280]{1,0:T(8,128)(2,1)S(1)}, u32[]{:S(2)}, u32[]{:S(2)}) collective-permute-start(bf16[32,1280]{1,0:T(8,128)(2,1)} %get-tuple-element.42), channel_id=1, source_target_pairs={{0,24},{8,0},{16,8},{24,16},{1,25},{9,1},{17,9},{25,17},{2,26},{10... | collective-permute-start | bytes 245768 | tf_op jit(solution)/shard_map/ppermute | solution.py:28
  11.3 1.6 collective-permute-start
  13.8 2.4 %collective-permute-start.2 = (bf16[272,512]{1,0:T(8,128)(2,1)}, bf16[272,512]{1,0:T(8,128)(2,1)S(1)}, u32[]{:S(2)}, u32[]{:S(2)}) collective-permute-start(bf16[272,512]{1,0:T(8,128)(2,1)} %get-tuple-element.43.refs_0_), channel_id=1, source_target_pairs={{0,3},{1,0},{2,1},{3,2},{4,7},{5,4},{6,5},{7,6},{8,11},{9,8},{10,9... | collective-permute-start | bytes 835592 | tf_op jit(solution)/shard_map/ppermute | solution.py:28
  17.9 4.5 %collective-permute-done.4 = bf16[32,1280]{1,0:T(8,128)(2,1)S(1)} collective-permute-done((bf16[32,1280]{1,0:T(8,128)(2,1)}, bf16[32,1280]{1,0:T(8,128)(2,1)S(1)}, u32[]{:S(2)}, u32[]{:S(2)}) %collective-permute-start.4) | collective-permute-done | bytes 81952 | tf_op jit(solution)/shard_map/ppermute | solution.py:28
  23.2 1.4 pad_maximum_fusion.1
  24.7 2.9 %collective-permute-done.2.refs_3_ = bf16[272,512]{1,0:T(8,128)(2,1)S(1)} collective-permute-done((bf16[272,512]{1,0:T(8,128)(2,1)}, bf16[272,512]{1,0:T(8,128)(2,1)S(1)}, u32[]{:S(2)}, u32[]{:S(2)}) %collective-permute-start.2) | collective-permute-done | bytes 278560 | tf_op jit(solution)/shard_map/ppermute | solution.py:28
  28.3 4.7 %shard_map.119 = (bf16[32,16,128]{2,1,0:T(8,128)(2,1)}, bf16[16,2048]{1,0:T(8,128)(2,1)}, bf16[2,256,128]{2,1,0:T(8,128)(2,1)}, bf16[2,256,128]{2,1,0:T(8,128)(2...) custom-call(bf16[272,512]{1,0:T(8,128)(2,1)} %get-tuple-element.43.refs_0_, bf16[272,512]{1,0:T(8,128)(2,1)} %copy-done.8, ...), custom_call_target="tpu_custom_call" | custom-call | flops 1 | bytes 1 | tf_op jit(solution)/shard_map/pallas_call | solution.py:118
  33.1 2.3 %collective-permute-start.7 = (bf16[2,256,128]{2,1,0:T(8,128)(2,1)}, bf16[2,256,128]{2,1,0:T(8,128)(2,1)S(1)}, u32[]{:S(2)}, u32[]{:S(2)}) collective-permute-start(bf16[2,256,128]{2,1,0:T(8,128)(2,1)} %get-tuple-element.51), channel_id=1, source_target_pairs={{0,16},{8,24},{16,0},{24,8},{1,17},{9,25},{17,1},{25,9},{2,18},{10... | collective-permute-start | bytes 393224 | tf_op jit(solution)/shard_map/ppermute | solution.py:28
  36.5 11.0 %all-to-all-start = ((bf16[32,16,128]{2,1,0:T(8,128)(2,1)}), bf16[32,16,128]{2,1,0:T(8,128)(2,1)S(1)}, u32[]{:S(2)}, u32[]{:S(2)}) async-start(bf16[32,16,128]{2,1,0:T(8,128)(2,1)} %get-tuple-element.48), calls=%async_computation | async-start | bytes 262144 | tf_op jit(solution)/shard_map/all_to_all | solution.py:478
  49.4 9.0 %all-to-all-done = bf16[32,16,128]{2,1,0:T(8,128)(2,1)S(1)} async-done(((bf16[32,16,128]{2,1,0:T(8,128)(2,1)}), bf16[32,16,128]{2,1,0:T(8,128)(2,1)S(1)}, u32[]{:S(2)}, u32[]{:S(2)}) %all-to-all-start) | async-done | bytes 131104 | tf_op jit(solution)/shard_map/all_to_all | solution.py:478
  59.4 4.2 %shard_map.120 = bf16[512,256]{1,0:T(8,128)(2,1)} custom-call(s32[1,512]{1,0:T(1,128)S(1)} %reshape.26.pos_ref, bf16[512,128]{1,0:T(8,128)(2,1)S(1)} %bitcast.28, bf16[2,256,128]{2,1,0:T(8,128)(2,1)S(1)} %copy-done.4, bf16[2,256,128]{2,1,0:T(8,128)(2,1)S(1)} %collective-permute-done.6.refs_1_, bf16[2,256,128]{2,1,0:T(8,128)(2,1)S(1)} %collective-permute-done.7.refs_2_, ...), custom_call_target="tpu_custom_call" | custom-call | flops 1 | bytes 1 | tf_op jit(solution)/shard_map/pallas_call | solution.py:171
  63.6 3.9 %all-to-all-start.1 = ((bf16[32,16,256]{2,1,0:T(8,128)(2,1)}), bf16[32,16,256]{2,1,0:T(8,128)(2,1)S(1)}, u32[]{:S(2)}, u32[]{:S(2)}) async-start(bf16[32,16,256]{2,1,0:T(8,128)(2,1)} %bitcast.7), calls=%async_computation.1 | async-start | bytes 524288 | tf_op jit(solution)/shard_map/all_to_all | solution.py:487
  68.3 3.0 %shard_map.121 = (bf16[2048,384]{1,0:T(8,128)(2,1)}, bf16[2048,128]{1,0:T(8,128)(2,1)}) custom-call(bf16[8,2,4,32,512]{4,3,2,1,0:T(8,128)(2,1)} %bitcast.31), custom_call_target="tpu_custom_call" | custom-call | flops 1 | bytes 1 | tf_op jit(solution)/shard_map/pallas_call | solution.py:303
  71.3 8.0 %all-to-all-done.1 = bf16[32,16,256]{2,1,0:T(8,128)(2,1)S(1)} async-done(((bf16[32,16,256]{2,1,0:T(8,128)(2,1)}), bf16[32,16,256]{2,1,0:T(8,128)(2,1)S(1)}, u32[]{:S(2)}, u32[]{:S(2)}) %all-to-all-start.1) | async-done | bytes 262176 | tf_op jit(solution)/shard_map/all_to_all | solution.py:487
  80.0 2.2 %collective-permute-start.13 = (bf16[16,2048]{1,0:T(8,128)(2,1)S(1)}, bf16[16,2048]{1,0:T(8,128)(2,1)S(1)}, u32[]{:S(2)}, u32[]{:S(2)}) collective-permute-start(bf16[16,2048]{1,0:T(8,128)(2,1)S(1)} %shard_map.122.a), channel_id=1, source_target_pairs={{0,1},{1,2},{2,3},{3,0},{4,5},{5,6},{6,7},{7,4},{8,9},{9,10},{10,1... | collective-permute-start | bytes 196616 | tf_op jit(solution)/shard_map/ppermute | solution.py:28
  83.5 1.4 collective-permute-start.15
  85.0 3.1 %collective-permute-done.14.c = bf16[16,2048]{1,0:T(8,128)(2,1)S(1)} collective-permute-done((bf16[16,2048]{1,0:T(8,128)(2,1)S(1)}, bf16[16,2048]{1,0:T(8,128)(2,1)S(1)}, u32[]{:S(2)}, u32[]{:S(2)}) %collective-permute-start.14) | collective-permute-done | bytes 65568 | tf_op jit(solution)/shard_map/ppermute | solution.py:28
  88.8 2.6 %collective-permute-start.17 = (bf16[16,2048]{1,0:T(8,128)(2,1)S(1)}, bf16[16,2048]{1,0:T(8,128)(2,1)S(1)}, u32[]{:S(2)}, u32[]{:S(2)}) collective-permute-start(bf16[16,2048]{1,0:T(8,128)(2,1)S(1)} %get-tuple-element.59.refs_0_), channel_id=1, source_target_pairs={{0,16},{8,24},{16,0},{24,8},{1,17},{9,25},{17,1},{25,9},{2,18},{10... | collective-permute-start | bytes 196616 | tf_op jit(solution)/shard_map/ppermute | solution.py:28
  92.7 2.2 %collective-permute-done.16.refs_1_ = bf16[16,2048]{1,0:T(8,128)(2,1)S(1)} collective-permute-done((bf16[16,2048]{1,0:T(8,128)(2,1)S(1)}, bf16[16,2048]{1,0:T(8,128)(2,1)S(1)}, u32[]{:S(2)}, u32[]{:S(2)}) %collective-permute-start.16) | collective-permute-done | bytes 65568 | tf_op jit(solution)/shard_map/ppermute | solution.py:28
  96.2 15.3 %all_to_all.20 = bf16[8,64,256]{2,1,0:T(8,128)(2,1)S(1)} all-to-all(bf16[8,64,256]{2,1,0:T(8,128)(2,1)S(1)} %get-tuple-element.62), channel_id=1, replica_groups=mesh['z'=8,'x'=4,'core'=2,'tp'=4] {'z'}, dimensions={0} | all-to-all | bytes 524288 | tf_op jit(solution)/shard_map/all_to_all | solution.py:499
  111.4 1.5 collective-permute-done.19.other_ref
  115.1 2.1 %collective-permute-start.21 = (bf16[16,2048]{1,0:T(8,128)(2,1)S(1)}, bf16[16,2048]{1,0:T(8,128)(2,1)S(1)}, u32[]{:S(2)}, u32[]{:S(2)}) collective-permute-start(bf16[16,2048]{1,0:T(8,128)(2,1)S(1)} %get-tuple-element.66), channel_id=1, source_target_pairs={{0,16},{8,24},{16,0},{24,8},{1,17},{9,25},{17,1},{25,9},{2,18},{10... | collective-permute-start | bytes 196616 | tf_op jit(solution)/shard_map/ppermute | solution.py:28
  119.5 1.4 collective-permute-done.21
  121.5 1.9 %collective-permute-start.23 = (bf16[16,2048]{1,0:T(8,128)(2,1)S(1)}, bf16[16,2048]{1,0:T(8,128)(2,1)S(1)}, u32[]{:S(2)}, u32[]{:S(2)}) collective-permute-start(bf16[16,2048]{1,0:T(8,128)(2,1)S(1)} %add_convert_fusion.a), channel_id=1, source_target_pairs={{0,1},{1,2},{2,3},{3,0},{4,5},{5,6},{6,7},{7,4},{8,9},{9,10},{10,1... | collective-permute-start | bytes 196616 | tf_op jit(solution)/shard_map/ppermute | solution.py:28
  123.4 2.2 %collective-permute-start.24 = (bf16[16,2048]{1,0:T(8,128)(2,1)S(1)}, bf16[16,2048]{1,0:T(8,128)(2,1)S(1)}, u32[]{:S(2)}, u32[]{:S(2)}) collective-permute-start(bf16[16,2048]{1,0:T(8,128)(2,1)S(1)} %add_convert_fusion.a), channel_id=1, source_target_pairs={{0,2},{1,3},{2,0},{3,1},{4,6},{5,7},{6,4},{7,5},{8,10},{9,11},{10,... | collective-permute-start | bytes 196616 | tf_op jit(solution)/shard_map/ppermute | solution.py:28
  125.6 2.3 %collective-permute-start.25 = (bf16[16,2048]{1,0:T(8,128)(2,1)S(1)}, bf16[16,2048]{1,0:T(8,128)(2,1)S(1)}, u32[]{:S(2)}, u32[]{:S(2)}) collective-permute-start(bf16[16,2048]{1,0:T(8,128)(2,1)S(1)} %add_convert_fusion.a), channel_id=1, source_target_pairs={{0,3},{1,0},{2,1},{3,2},{4,7},{5,4},{6,5},{7,6},{8,11},{9,8},{10,9... | collective-permute-start | bytes 196616 | tf_op jit(solution)/shard_map/ppermute | solution.py:28
  130.2 3.0 %collective-permute-start.27 = (bf16[16,2048]{1,0:T(8,128)(2,1)S(1)}, bf16[16,2048]{1,0:T(8,128)(2,1)S(1)}, u32[]{:S(2)}, u32[]{:S(2)}) collective-permute-start(bf16[16,2048]{1,0:T(8,128)(2,1)S(1)} %get-tuple-element.69.refs_0_), channel_id=1, source_target_pairs={{0,16},{8,24},{16,0},{24,8},{1,17},{9,25},{17,1},{25,9},{2,18},{10... | collective-permute-start | bytes 196616 | tf_op jit(solution)/shard_map/ppermute | solution.py:28
  134.2 2.0 %collective-permute-done.26.refs_1_ = bf16[16,2048]{1,0:T(8,128)(2,1)S(1)} collective-permute-done((bf16[16,2048]{1,0:T(8,128)(2,1)S(1)}, bf16[16,2048]{1,0:T(8,128)(2,1)S(1)}, u32[]{:S(2)}, u32[]{:S(2)}) %collective-permute-start.26) | collective-permute-done | bytes 65568 | tf_op jit(solution)/shard_map/ppermute | solution.py:28
  137.4 1.9 %copy-done = bf16[64,32,768]{2,1,0:T(8,128)(2,1)S(1)} copy-done((bf16[64,32,768]{2,1,0:T(8,128)(2,1)S(1)}, bf16[64,32,768]{2,1,0:T(8,128)(2,1)}, u32[]{:S(2)}) %copy-start) | copy-done | bytes 3145752
  139.3 2.3 %shard_map.127 = bf16[16,16,512]{2,1,0:T(8,128)(2,1)S(1)} custom-call(bf16[16,2048]{1,0:T(8,128)(2,1)S(1)} %get-tuple-element.69.refs_0_, bf16[16,2048]{1,0:T(8,128)(2,1)S(1)} %collective-permute-done.26.refs_1_, bf16[16,2048]{1,0:T(8,128)(2,1)S(1)} %collective-permute-done.27.refs_2_, bf16[16,2048]{1,0:T(8,128)(2,1)S(1)} %collective-permute-done.28.refs_3_, ...), custom_call_target="tpu_custom_call" | custom-call | flops 1 | bytes 1 | tf_op jit(solution)/shard_map/pallas_call | solution.py:436
  141.6 13.7 %all_to_all.21 = bf16[16,16,512]{2,1,0:T(8,128)(2,1)S(1)} all-to-all(bf16[16,16,512]{2,1,0:T(8,128)(2,1)S(1)} %shard_map.127), channel_id=1, replica_groups=mesh['z'=8,'x'=4,'core'=2,'tp'=4] {'x','tp'}, dimensions={0} | all-to-all | bytes 524288 | tf_op jit(solution)/shard_map/all_to_all | solution.py:507
  (88 shorter events, 24.4 us)
Async XLA Ops:
  6.5 61.7 %all-gather.5.cloned.1.call-start = ((), (), s32[]{:S(2)}) async-start(), calls=%async_computation.4 | async-start | bytes 2228224 | tf_op jit(solution)/shard_map/all_gather | solution.py:479
  8.5 8.5 %collective-permute-start.5 = (bf16[32,1280]{1,0:T(8,128)(2,1)}, bf16[32,1280]{1,0:T(8,128)(2,1)S(1)}, u32[]{:S(2)}, u32[]{:S(2)}) collective-permute-start(bf16[32,1280]{1,0:T(8,128)(2,1)} %get-tuple-element.42), channel_id=1, source_target_pairs={{0,24},{8,0},{16,8},{24,16},{1,25},{9,1},{17,9},{25,17},{2,26},{10... | collective-permute-start | bytes 245768 | tf_op jit(solution)/shard_map/ppermute | solution.py:28
  11.3 13.4 %collective-permute-start = (bf16[272,512]{1,0:T(8,128)(2,1)}, bf16[272,512]{1,0:T(8,128)(2,1)S(1)}, u32[]{:S(2)}, u32[]{:S(2)}) collective-permute-start(bf16[272,512]{1,0:T(8,128)(2,1)} %get-tuple-element.43.refs_0_), channel_id=1, source_target_pairs={{0,1},{1,2},{2,3},{3,0},{4,5},{5,6},{6,7},{7,4},{8,9},{9,10},{10,1... | collective-permute-start | bytes 835592 | tf_op jit(solution)/shard_map/ppermute | solution.py:28
  12.8 11.8 %collective-permute-start.1 = (bf16[272,512]{1,0:T(8,128)(2,1)}, bf16[272,512]{1,0:T(8,128)(2,1)S(1)}, u32[]{:S(2)}, u32[]{:S(2)}) collective-permute-start(bf16[272,512]{1,0:T(8,128)(2,1)} %get-tuple-element.43.refs_0_), channel_id=1, source_target_pairs={{0,2},{1,3},{2,0},{3,1},{4,6},{5,7},{6,4},{7,5},{8,10},{9,11},{10,... | collective-permute-start | bytes 835592 | tf_op jit(solution)/shard_map/ppermute | solution.py:28
  13.8 13.8 %collective-permute-start.2 = (bf16[272,512]{1,0:T(8,128)(2,1)}, bf16[272,512]{1,0:T(8,128)(2,1)S(1)}, u32[]{:S(2)}, u32[]{:S(2)}) collective-permute-start(bf16[272,512]{1,0:T(8,128)(2,1)} %get-tuple-element.43.refs_0_), channel_id=1, source_target_pairs={{0,3},{1,0},{2,1},{3,2},{4,7},{5,4},{6,5},{7,6},{8,11},{9,8},{10,9... | collective-permute-start | bytes 835592 | tf_op jit(solution)/shard_map/ppermute | solution.py:28
  16.2 6.2 %collective-permute-start.4 = (bf16[32,1280]{1,0:T(8,128)(2,1)}, bf16[32,1280]{1,0:T(8,128)(2,1)S(1)}, u32[]{:S(2)}, u32[]{:S(2)}) collective-permute-start(bf16[32,1280]{1,0:T(8,128)(2,1)} %get-tuple-element.41), channel_id=1, source_target_pairs={{0,16},{8,24},{16,0},{24,8},{1,17},{9,25},{17,1},{25,9},{2,18},{10... | collective-permute-start | bytes 245768 | tf_op jit(solution)/shard_map/ppermute | solution.py:28
  17.0 6.2 %collective-permute-start.3 = (bf16[32,1280]{1,0:T(8,128)(2,1)}, bf16[32,1280]{1,0:T(8,128)(2,1)S(1)}, u32[]{:S(2)}, u32[]{:S(2)}) collective-permute-start(bf16[32,1280]{1,0:T(8,128)(2,1)} %get-tuple-element.40), channel_id=1, source_target_pairs={{0,8},{8,16},{16,24},{24,0},{1,9},{9,17},{17,25},{25,1},{2,10},{10... | collective-permute-start | bytes 245768 | tf_op jit(solution)/shard_map/ppermute | solution.py:28
  33.0 14.8 %collective-permute-start.6 = (bf16[2,256,128]{2,1,0:T(8,128)(2,1)}, bf16[2,256,128]{2,1,0:T(8,128)(2,1)S(1)}, u32[]{:S(2)}, u32[]{:S(2)}) collective-permute-start(bf16[2,256,128]{2,1,0:T(8,128)(2,1)} %get-tuple-element.50), channel_id=1, source_target_pairs={{0,8},{8,16},{16,24},{24,0},{1,9},{9,17},{17,25},{25,1},{2,10},{10... | collective-permute-start | bytes 393224 | tf_op jit(solution)/shard_map/ppermute | solution.py:28
  33.1 15.3 %collective-permute-start.7 = (bf16[2,256,128]{2,1,0:T(8,128)(2,1)}, bf16[2,256,128]{2,1,0:T(8,128)(2,1)S(1)}, u32[]{:S(2)}, u32[]{:S(2)}) collective-permute-start(bf16[2,256,128]{2,1,0:T(8,128)(2,1)} %get-tuple-element.51), channel_id=1, source_target_pairs={{0,16},{8,24},{16,0},{24,8},{1,17},{9,25},{17,1},{25,9},{2,18},{10... | collective-permute-start | bytes 393224 | tf_op jit(solution)/shard_map/ppermute | solution.py:28
  35.4 13.1 %collective-permute-start.8 = (bf16[2,256,128]{2,1,0:T(8,128)(2,1)}, bf16[2,256,128]{2,1,0:T(8,128)(2,1)S(1)}, u32[]{:S(2)}, u32[]{:S(2)}) collective-permute-start(bf16[2,256,128]{2,1,0:T(8,128)(2,1)} %get-tuple-element.52), channel_id=1, source_target_pairs={{0,24},{8,0},{16,8},{24,16},{1,25},{9,1},{17,9},{25,17},{2,26},{10... | collective-permute-start | bytes 393224 | tf_op jit(solution)/shard_map/ppermute | solution.py:28
  36.5 21.9 %all-to-all-start = ((bf16[32,16,128]{2,1,0:T(8,128)(2,1)}), bf16[32,16,128]{2,1,0:T(8,128)(2,1)S(1)}, u32[]{:S(2)}, u32[]{:S(2)}) async-start(bf16[32,16,128]{2,1,0:T(8,128)(2,1)} %get-tuple-element.48), calls=%async_computation | async-start | bytes 262144 | tf_op jit(solution)/shard_map/all_to_all | solution.py:478
  47.8 1.6 collective-permute-start.9
  47.8 10.6 %collective-permute-start.10 = (bf16[2,256,128]{2,1,0:T(8,128)(2,1)S(1)}, bf16[2,256,128]{2,1,0:T(8,128)(2,1)S(1)}, u32[]{:S(2)}, u32[]{:S(2)}) collective-permute-start(bf16[2,256,128]{2,1,0:T(8,128)(2,1)S(1)} %collective-permute-done.6.refs_1_), channel_id=1, source_target_pairs={{0,4},{4,0},{1,5},{5,1},{2,6},{6,2},{3,7},{7,3},{8,12},{12,8},{9,1... | collective-permute-start | bytes 393224 | tf_op jit(solution)/shard_map/ppermute | solution.py:28
  48.3 10.1 %collective-permute-start.11 = (bf16[2,256,128]{2,1,0:T(8,128)(2,1)S(1)}, bf16[2,256,128]{2,1,0:T(8,128)(2,1)S(1)}, u32[]{:S(2)}, u32[]{:S(2)}) collective-permute-start(bf16[2,256,128]{2,1,0:T(8,128)(2,1)S(1)} %collective-permute-done.7.refs_2_), channel_id=1, source_target_pairs={{0,4},{4,0},{1,5},{5,1},{2,6},{6,2},{3,7},{7,3},{8,12},{12,8},{9,1... | collective-permute-start | bytes 393224 | tf_op jit(solution)/shard_map/ppermute | solution.py:28
  48.5 10.0 %collective-permute-start.12 = (bf16[2,256,128]{2,1,0:T(8,128)(2,1)S(1)}, bf16[2,256,128]{2,1,0:T(8,128)(2,1)S(1)}, u32[]{:S(2)}, u32[]{:S(2)}) collective-permute-start(bf16[2,256,128]{2,1,0:T(8,128)(2,1)S(1)} %collective-permute-done.8.refs_3_), channel_id=1, source_target_pairs={{0,4},{4,0},{1,5},{5,1},{2,6},{6,2},{3,7},{7,3},{8,12},{12,8},{9,1... | collective-permute-start | bytes 393224 | tf_op jit(solution)/shard_map/ppermute | solution.py:28
  63.6 15.7 %all-to-all-start.1 = ((bf16[32,16,256]{2,1,0:T(8,128)(2,1)}), bf16[32,16,256]{2,1,0:T(8,128)(2,1)S(1)}, u32[]{:S(2)}, u32[]{:S(2)}) async-start(bf16[32,16,256]{2,1,0:T(8,128)(2,1)} %bitcast.7), calls=%async_computation.1 | async-start | bytes 524288 | tf_op jit(solution)/shard_map/all_to_all | solution.py:487
  67.5 69.9 %all-gather.7.cloned.1.call-start = ((), (), s32[]{:S(2)}) async-start(), calls=%async_computation.5 | async-start | bytes 3342336 | tf_op jit(solution)/shard_map/all_gather | solution.py:492
  80.0 5.0 %collective-permute-start.13 = (bf16[16,2048]{1,0:T(8,128)(2,1)S(1)}, bf16[16,2048]{1,0:T(8,128)(2,1)S(1)}, u32[]{:S(2)}, u32[]{:S(2)}) collective-permute-start(bf16[16,2048]{1,0:T(8,128)(2,1)S(1)} %shard_map.122.a), channel_id=1, source_target_pairs={{0,1},{1,2},{2,3},{3,0},{4,5},{5,6},{6,7},{7,4},{8,9},{9,10},{10,1... | collective-permute-start | bytes 196616 | tf_op jit(solution)/shard_map/ppermute | solution.py:28
  82.2 5.9 %collective-permute-start.14 = (bf16[16,2048]{1,0:T(8,128)(2,1)S(1)}, bf16[16,2048]{1,0:T(8,128)(2,1)S(1)}, u32[]{:S(2)}, u32[]{:S(2)}) collective-permute-start(bf16[16,2048]{1,0:T(8,128)(2,1)S(1)} %shard_map.122.a), channel_id=1, source_target_pairs={{0,2},{1,3},{2,0},{3,1},{4,6},{5,7},{6,4},{7,5},{8,10},{9,11},{10,... | collective-permute-start | bytes 196616 | tf_op jit(solution)/shard_map/ppermute | solution.py:28
  83.5 5.0 %collective-permute-start.15 = (bf16[16,2048]{1,0:T(8,128)(2,1)S(1)}, bf16[16,2048]{1,0:T(8,128)(2,1)S(1)}, u32[]{:S(2)}, u32[]{:S(2)}) collective-permute-start(bf16[16,2048]{1,0:T(8,128)(2,1)S(1)} %shard_map.122.a), channel_id=1, source_target_pairs={{0,3},{1,0},{2,1},{3,2},{4,7},{5,4},{6,5},{7,6},{8,11},{9,8},{10,9... | collective-permute-start | bytes 196616 | tf_op jit(solution)/shard_map/ppermute | solution.py:28
  88.7 6.3 %collective-permute-start.16 = (bf16[16,2048]{1,0:T(8,128)(2,1)S(1)}, bf16[16,2048]{1,0:T(8,128)(2,1)S(1)}, u32[]{:S(2)}, u32[]{:S(2)}) collective-permute-start(bf16[16,2048]{1,0:T(8,128)(2,1)S(1)} %get-tuple-element.59.refs_0_), channel_id=1, source_target_pairs={{0,8},{8,16},{16,24},{24,0},{1,9},{9,17},{17,25},{25,1},{2,10},{10... | collective-permute-start | bytes 196616 | tf_op jit(solution)/shard_map/ppermute | solution.py:28
  88.8 6.2 %collective-permute-start.17 = (bf16[16,2048]{1,0:T(8,128)(2,1)S(1)}, bf16[16,2048]{1,0:T(8,128)(2,1)S(1)}, u32[]{:S(2)}, u32[]{:S(2)}) collective-permute-start(bf16[16,2048]{1,0:T(8,128)(2,1)S(1)} %get-tuple-element.59.refs_0_), channel_id=1, source_target_pairs={{0,16},{8,24},{16,0},{24,8},{1,17},{9,25},{17,1},{25,9},{2,18},{10... | collective-permute-start | bytes 196616 | tf_op jit(solution)/shard_map/ppermute | solution.py:28
  91.4 4.4 %collective-permute-start.18 = (bf16[16,2048]{1,0:T(8,128)(2,1)S(1)}, bf16[16,2048]{1,0:T(8,128)(2,1)S(1)}, u32[]{:S(2)}, u32[]{:S(2)}) collective-permute-start(bf16[16,2048]{1,0:T(8,128)(2,1)S(1)} %get-tuple-element.59.refs_0_), channel_id=1, source_target_pairs={{0,24},{8,0},{16,8},{24,16},{1,25},{9,1},{17,9},{25,17},{2,26},{10... | collective-permute-start | bytes 196616 | tf_op jit(solution)/shard_map/ppermute | solution.py:28
  113.7 5.7 %collective-permute-start.22 = (bf16[16,2048]{1,0:T(8,128)(2,1)S(1)}, bf16[16,2048]{1,0:T(8,128)(2,1)S(1)}, u32[]{:S(2)}, u32[]{:S(2)}) collective-permute-start(bf16[16,2048]{1,0:T(8,128)(2,1)S(1)} %get-tuple-element.67), channel_id=1, source_target_pairs={{0,8},{8,16},{16,24},{24,0},{1,9},{9,17},{17,25},{25,1},{2,10},{10... | collective-permute-start | bytes 196616 | tf_op jit(solution)/shard_map/ppermute | solution.py:28
  115.1 5.8 %collective-permute-start.21 = (bf16[16,2048]{1,0:T(8,128)(2,1)S(1)}, bf16[16,2048]{1,0:T(8,128)(2,1)S(1)}, u32[]{:S(2)}, u32[]{:S(2)}) collective-permute-start(bf16[16,2048]{1,0:T(8,128)(2,1)S(1)} %get-tuple-element.66), channel_id=1, source_target_pairs={{0,16},{8,24},{16,0},{24,8},{1,17},{9,25},{17,1},{25,9},{2,18},{10... | collective-permute-start | bytes 196616 | tf_op jit(solution)/shard_map/ppermute | solution.py:28
  117.2 4.3 %collective-permute-start.20 = (bf16[16,2048]{1,0:T(8,128)(2,1)S(1)}, bf16[16,2048]{1,0:T(8,128)(2,1)S(1)}, u32[]{:S(2)}, u32[]{:S(2)}) collective-permute-start(bf16[16,2048]{1,0:T(8,128)(2,1)S(1)} %get-tuple-element.65), channel_id=1, source_target_pairs={{0,24},{8,0},{16,8},{24,16},{1,25},{9,1},{17,9},{25,17},{2,26},{10... | collective-permute-start | bytes 196616 | tf_op jit(solution)/shard_map/ppermute | solution.py:28
  121.5 6.3 %collective-permute-start.23 = (bf16[16,2048]{1,0:T(8,128)(2,1)S(1)}, bf16[16,2048]{1,0:T(8,128)(2,1)S(1)}, u32[]{:S(2)}, u32[]{:S(2)}) collective-permute-start(bf16[16,2048]{1,0:T(8,128)(2,1)S(1)} %add_convert_fusion.a), channel_id=1, source_target_pairs={{0,1},{1,2},{2,3},{3,0},{4,5},{5,6},{6,7},{7,4},{8,9},{9,10},{10,1... | collective-permute-start | bytes 196616 | tf_op jit(solution)/shard_map/ppermute | solution.py:28
  123.4 5.8 %collective-permute-start.24 = (bf16[16,2048]{1,0:T(8,128)(2,1)S(1)}, bf16[16,2048]{1,0:T(8,128)(2,1)S(1)}, u32[]{:S(2)}, u32[]{:S(2)}) collective-permute-start(bf16[16,2048]{1,0:T(8,128)(2,1)S(1)} %add_convert_fusion.a), channel_id=1, source_target_pairs={{0,2},{1,3},{2,0},{3,1},{4,6},{5,7},{6,4},{7,5},{8,10},{9,11},{10,... | collective-permute-start | bytes 196616 | tf_op jit(solution)/shard_map/ppermute | solution.py:28
  125.6 4.3 %collective-permute-start.25 = (bf16[16,2048]{1,0:T(8,128)(2,1)S(1)}, bf16[16,2048]{1,0:T(8,128)(2,1)S(1)}, u32[]{:S(2)}, u32[]{:S(2)}) collective-permute-start(bf16[16,2048]{1,0:T(8,128)(2,1)S(1)} %add_convert_fusion.a), channel_id=1, source_target_pairs={{0,3},{1,0},{2,1},{3,2},{4,7},{5,4},{6,5},{7,6},{8,11},{9,8},{10,9... | collective-permute-start | bytes 196616 | tf_op jit(solution)/shard_map/ppermute | solution.py:28
  130.0 6.3 %collective-permute-start.26 = (bf16[16,2048]{1,0:T(8,128)(2,1)S(1)}, bf16[16,2048]{1,0:T(8,128)(2,1)S(1)}, u32[]{:S(2)}, u32[]{:S(2)}) collective-permute-start(bf16[16,2048]{1,0:T(8,128)(2,1)S(1)} %get-tuple-element.69.refs_0_), channel_id=1, source_target_pairs={{0,8},{8,16},{16,24},{24,0},{1,9},{9,17},{17,25},{25,1},{2,10},{10... | collective-permute-start | bytes 196616 | tf_op jit(solution)/shard_map/ppermute | solution.py:28
  130.2 6.1 %collective-permute-start.27 = (bf16[16,2048]{1,0:T(8,128)(2,1)S(1)}, bf16[16,2048]{1,0:T(8,128)(2,1)S(1)}, u32[]{:S(2)}, u32[]{:S(2)}) collective-permute-start(bf16[16,2048]{1,0:T(8,128)(2,1)S(1)} %get-tuple-element.69.refs_0_), channel_id=1, source_target_pairs={{0,16},{8,24},{16,0},{24,8},{1,17},{9,25},{17,1},{25,9},{2,18},{10... | collective-permute-start | bytes 196616 | tf_op jit(solution)/shard_map/ppermute | solution.py:28
  133.1 4.3 %collective-permute-start.28 = (bf16[16,2048]{1,0:T(8,128)(2,1)S(1)}, bf16[16,2048]{1,0:T(8,128)(2,1)S(1)}, u32[]{:S(2)}, u32[]{:S(2)}) collective-permute-start(bf16[16,2048]{1,0:T(8,128)(2,1)S(1)} %get-tuple-element.69.refs_0_), channel_id=1, source_target_pairs={{0,24},{8,0},{16,8},{24,16},{1,25},{9,1},{17,9},{25,17},{2,26},{10... | collective-permute-start | bytes 196616 | tf_op jit(solution)/shard_map/ppermute | solution.py:28
  (14 other events, 225.2 us)
Sparse Core Ops, SparseCore 0:
  27.7 40.2 all-gather.4
  79.4 39.6 all-gather.6
